TPU v7x, 128 devices: a whole 4x4x4 slice. The times are simulated.
128 devices in a mesh: dp: 32 (over z, y, core), segment: 2 (over x_hi), frame: 2 (over x_lo).
Axes of the slice: x: 4 (x_hi: 2, x_lo: 2; x = x_hi * 2 + x_lo), y: 4, z: 4, core: 2. Of those that a mesh axis runs over, the one named last changes fastest.
Arguments:
- frames_in: bfloat16 [32, 256, 4096], P('dp', 'frame'), may hold values from -6 to 6
- qkv_weight: bfloat16 [2, 4096, 3, 2048], P('segment', 'dp', None, 'frame'), may hold values from -3 to 3
- out_weight: bfloat16 [2, 2048, 4096], P('segment', 'frame', 'dp'), may hold values from -0.125 to 0.125
- proj_weight: bfloat16 [4096, 1024], replicated, may hold values from -0.09375 to 0.09375
- depth_qkv: bfloat16 [1024, 3, 512], replicated, may hold values from -5 to 5
- depth_out: bfloat16 [512, 1024], replicated, may hold values from -0.25 to 0.25
- code_table: bfloat16 [2048, 1024], replicated, may hold values from -6 to 6
- logit_weight: bfloat16 [1024, 2048], replicated, may hold values from -24 to 24
- codes: int32 [32, 256, 6], P('dp', 'frame'), may hold values from 0 to 2047
- delays: int32 [6], replicated, may hold values from 0 to 2
Outputs:
- losses: float32 [32, 256, 6], P('dp', 'frame')
All inputs are finite; a program needn't handle non-finite values.
Results may differ from a plain program's by a relative error of at most 0.005.
Values may be sent and summed in bfloat16 or wider, within the bound.
No kernel may reach another device: no remote copies, remote signals or barrier semaphores. Data moves between devices by JAX's collectives and lax.ppermute only.
A program may use at most 192 MiB of HBM per device.

v0:
```python
import jax
import jax.numpy as jnp
from jax import lax
from jax.sharding import PartitionSpec as P

HD = 128
HDD = 64
DMAX = 2


def shifted(value, axis, steps):
    count = lax.axis_size(axis)
    first, last = (max(0, -steps), min(count, count - steps))
    return lax.ppermute(value, axis, [(source, source + steps) for source in range(first, last)])


def spread(value, axis, source):
    kept = jnp.where(lax.axis_index(axis) == source, value, 0).astype(value.dtype)
    return lax.psum(kept, axis)


def rms_round(values):
    scale = lax.rsqrt(jnp.mean(values * values, axis=-1, keepdims=True) + 1e-05)
    return (values * scale).astype(jnp.bfloat16)


def rotate(values, positions):
    half_width = values.shape[-1] // 2
    frequency = 10000.0 ** (-jnp.arange(half_width, dtype=jnp.float32) / half_width)
    angles = positions[:, None].astype(jnp.float32) * frequency[None, :]
    cosine = jnp.cos(angles)[:, None, :]
    sine = jnp.sin(angles)[:, None, :]
    first = values[..., :half_width]
    second = values[..., half_width:]
    return jnp.concatenate(
        [first * cosine - second * sine, first * sine + second * cosine], axis=-1
    )


def attend(projected, head_size, positions):
    row_count = projected.shape[0]
    split = projected.reshape(row_count, 3, -1, head_size)
    queries = rotate(split[:, 0], positions).astype(jnp.bfloat16)
    keys = rotate(split[:, 1], positions).astype(jnp.bfloat16)
    values = split[:, 2].astype(jnp.bfloat16)
    scores = jnp.einsum(
        "qhd,khd->hqk", queries, keys, preferred_element_type=jnp.float32
    ) / jnp.sqrt(jnp.float32(head_size))
    causal_mask = positions[:, None] >= positions[None, :]
    scores = jnp.where(causal_mask[None], scores, -1e30)
    weights = jax.nn.softmax(scores, axis=-1).astype(jnp.bfloat16)
    context = jnp.einsum("hqk,khd->qhd", weights, values, preferred_element_type=jnp.float32)
    return context.reshape(row_count, -1).astype(jnp.bfloat16)


def depth_loss(depth_in, targets, is_valid, depth_qkv, depth_out, code_table, logit_weight):
    count, streams = targets.shape
    width = depth_in.shape[1]
    safe = jnp.clip(targets, 0, code_table.shape[0] - 1)
    embedded = jnp.take(code_table, safe[:, :-1], axis=0).astype(jnp.float32)
    embedded = embedded * is_valid[:, :-1, None].astype(jnp.float32)
    embedded = jnp.concatenate([jnp.zeros((count, 1, width), jnp.float32), embedded], axis=1)
    inputs = depth_in.astype(jnp.float32)[:, None, :] + embedded
    normed = rms_round(inputs).reshape(count * streams, width)
    head_width = depth_out.shape[0]
    projected = jnp.dot(
        normed, depth_qkv.reshape(width, 3 * head_width), preferred_element_type=jnp.float32
    )
    split = projected.reshape(count, streams, 3, -1, HDD).astype(jnp.bfloat16)
    scores = jnp.einsum(
        "fqhd,fkhd->fhqk", split[:, :, 0], split[:, :, 1], preferred_element_type=jnp.float32
    ) / jnp.sqrt(jnp.float32(HDD))
    order = jnp.arange(streams)
    scores = jnp.where((order[:, None] >= order[None, :])[None, None], scores, -1e30)
    weights = jax.nn.softmax(scores, axis=-1).astype(jnp.bfloat16)
    context = jnp.einsum(
        "fhqk,fkhd->fqhd", weights, split[:, :, 2], preferred_element_type=jnp.float32
    )
    context = context.reshape(count * streams, head_width).astype(jnp.bfloat16)
    mixed_rows = inputs.reshape(count * streams, width) + jnp.dot(
        context, depth_out, preferred_element_type=jnp.float32
    )
    logits = jnp.dot(rms_round(mixed_rows), logit_weight, preferred_element_type=jnp.float32)
    log_total = jax.nn.logsumexp(logits, axis=-1)
    picked = jnp.take_along_axis(logits, safe.reshape(-1, 1), axis=1)[:, 0]
    return jnp.where(is_valid, (log_total - picked).reshape(count, streams), 0.0)


def local(
    frames_in,
    qkv_weight,
    out_weight,
    proj_weight,
    depth_qkv,
    depth_out,
    code_table,
    logit_weight,
    codes,
    delays,
):
    phase_count = lax.axis_size("segment")
    phase_id = lax.axis_index("segment")
    frame_id = lax.axis_index("frame")
    micro_count = frames_in.shape[0]
    row_count = frames_in.shape[1]
    stream_count = codes.shape[2]
    total_rows = row_count * lax.axis_size("frame")
    positions = jnp.arange(total_rows)
    w_qkv, w_out = (
        lax.all_gather(qkv_weight[0], "dp", axis=0, tiled=True),
        lax.all_gather(out_weight[0], "dp", axis=1, tiled=True),
    )
    w_matrix = w_qkv.reshape(w_qkv.shape[0], -1)
    carried = jnp.zeros((row_count, frames_in.shape[2]), jnp.bfloat16)
    finished = []
    for turn_index in range(micro_count + phase_count - 1):
        if turn_index < micro_count:
            current = jnp.where(phase_id == 0, frames_in[turn_index], carried)
        else:
            current = carried
        normed = rms_round(current.astype(jnp.float32))
        projected = jnp.dot(
            lax.all_gather(normed, "frame", axis=0, tiled=True),
            w_matrix,
            preferred_element_type=jnp.float32,
        )
        context = attend(projected, HD, positions)
        mixed_out = lax.psum_scatter(
            jnp.dot(context, w_out, preferred_element_type=jnp.float32),
            "frame",
            scatter_dimension=0,
            tiled=True,
        )
        result = (current.astype(jnp.float32) + mixed_out).astype(jnp.bfloat16)
        if turn_index >= phase_count - 1:
            finished.append(result)
        if turn_index < micro_count + phase_count - 2:
            carried = shifted(result, "segment", 1)
    final_hidden = jnp.stack(finished)
    flat_hidden = rms_round(final_hidden.reshape(micro_count * row_count, -1).astype(jnp.float32))
    depth_all = jnp.dot(flat_hidden, proj_weight, preferred_element_type=jnp.float32).astype(
        jnp.bfloat16
    )
    depth_all = depth_all.reshape(micro_count, row_count, -1)
    code_tail = shifted(codes[:, row_count - DMAX :], "frame", 1)
    extended = jnp.concatenate([code_tail, codes], axis=1)
    offsets = jnp.arange(row_count, dtype=jnp.int32)[:, None] + DMAX - delays[None, :]
    offsets = offsets[None]
    targets = jnp.take_along_axis(extended, offsets, axis=1)
    global_rows = frame_id * row_count + jnp.arange(row_count, dtype=jnp.int32)
    is_valid = (global_rows[:, None] >= delays[None, :])[None]
    computed = depth_loss(
        depth_all.reshape(micro_count * row_count, -1),
        targets.reshape(micro_count * row_count, stream_count),
        is_valid.reshape(micro_count * row_count, stream_count),
        depth_qkv,
        depth_out,
        code_table,
        logit_weight,
    )
    losses = spread(
        computed.reshape(micro_count, row_count, stream_count), "segment", phase_count - 1
    )
    return losses


def solution(mesh):
    return jax.shard_map(
        local,
        mesh=mesh,
        in_specs=(
            P("dp", "frame", None),
            P("segment", "dp", None, "frame"),
            P("segment", "frame", "dp"),
            P(),
            P(),
            P(),
            P(),
            P(),
            P("dp", "frame", None),
            P(),
        ),
        out_specs=P("dp", "frame", None),
        check_vma=False,
    )
```

profile of v0, /device:TPU:0, one launch (start us, length us, event | category | flops | bytes accessed | tf_op | source)
XLA Modules:
  0.0 531.2 jit_solution(12622523536236584381)
XLA Ops:
  13.2 34.3 %all-gather.7.cloned.1.call-done = bf16[256,4096]{1,0:T(8,128)(2,1)} async-done(((bf16[128,4096]{1,0:T(8,128)(2,1)}), bf16[256,4096]{1,0:T(8,128)(2,1)}) %all-gather.7.cloned.1.call-update) | async-done | bytes 2097168 | tf_op jit(solution)/shard_map/all_gather | solution.py:123
  47.5 106.5 %all-gather.11.cloned.1.call-done = bf16[1,4096,3,1024]{1,3,2,0:T(8,128)(2,1)} async-done(((bf16[1,128,3,1024]{1,3,2,0:T(8,128)(2,1)}), bf16[1,4096,3,1024]{1,3,2,0:T(8,128)(2,1)}) %all-gather.11.cloned.1.call-update) | async-done | bytes 25165840 | tf_op jit(solution)/shard_map/all_gather | solution.py:110
  154.0 12.5 %fusion.17 = f32[256,3,8,128]{0,3,2,1:T(8,128)S(1)} fusion(bf16[3,8,128,4096]{3,2,1,0:T(8,128)(2,1)} %bitcast.90, bf16[256,4096]{1,0:T(8,128)(2,1)} %all-gather.7.cloned.1.call-done), kind=kOutput, calls=%fused_computation.35 | convolution fusion | flops 6442450944 | bytes 30408704 | tf_op jit(solution)/shard_map/dot_general | solution.py:122
  173.0 43.7 %all-gather.13.cloned.1.call-done = bf16[1,1024,4096]{2,1,0:T(8,128)(2,1)} async-done(((bf16[1,1024,128]{2,1,0:T(8,128)(2,1)}), bf16[1,1024,4096]{2,1,0:T(8,128)(2,1)}) %all-gather.13.cloned.1.call-update) | async-done | bytes 8388624 | tf_op jit(solution)/shard_map/all_gather | solution.py:111
  216.6 7.8 %fusion.4 = f32[256,4096]{1,0:T(8,128)} fusion(bf16[256,1024]{0,1:T(8,128)(2,1)S(1)} %bitcast.87, bf16[1,1024,4096]{2,1,0:T(8,128)(2,1)} %all-gather.13.cloned.1.call-done), kind=kOutput, calls=%fused_computation.7 | convolution fusion | flops 2147483648 | bytes 13107200 | tf_op jit(solution)/shard_map/dot_general | solution.py:129
  224.5 56.5 %reduce-scatter.3.cloned.1.call-done = f32[128,4096]{1,0:T(8,128)} async-done(((f32[256,4096]{1,0:T(8,128)}), f32[128,4096]{1,0:T(8,128)}) %reduce-scatter.3.cloned.1.call-update) | async-done | bytes 2097168 | tf_op jit(solution)/shard_map/reduce_scatter | solution.py:128
  282.9 4.7 collective-permute-start
  287.5 22.3 %collective-permute-done = bf16[128,4096]{1,0:T(8,128)(2,1)S(1)} collective-permute-done((bf16[128,4096]{1,0:T(8,128)(2,1)S(1)}, bf16[128,4096]{1,0:T(8,128)(2,1)S(1)}, u32[]{:S(2)}, u32[]{:S(2)}) %collective-permute-start) | collective-permute-done | bytes 1048608 | tf_op jit(solution)/shard_map/ppermute | solution.py:14
  312.0 37.5 %all-gather.9.cloned.1.call-done = bf16[256,4096]{1,0:T(8,128)(2,1)} async-done(((bf16[128,4096]{1,0:T(8,128)(2,1)}), bf16[256,4096]{1,0:T(8,128)(2,1)}) %all-gather.9.cloned.1.call-update) | async-done | bytes 2097168 | tf_op jit(solution)/shard_map/all_gather | solution.py:123
  349.5 12.5 %fusion.15 = f32[256,3,8,128]{0,3,2,1:T(8,128)S(1)} fusion(bf16[3,8,128,4096]{3,2,1,0:T(8,128)(2,1)} %bitcast.91, bf16[256,4096]{1,0:T(8,128)(2,1)} %all-gather.9.cloned.1.call-done), kind=kOutput, calls=%fused_computation.33 | convolution fusion | flops 6442450944 | bytes 30408704 | tf_op jit(solution)/shard_map/dot_general | solution.py:122
  368.5 7.7 %fusion.2 = f32[256,4096]{1,0:T(8,128)} fusion(bf16[256,1024]{0,1:T(8,128)(2,1)S(1)} %bitcast.88, bf16[1,1024,4096]{2,1,0:T(8,128)(2,1)} %all-gather.13.cloned.1.call-done), kind=kOutput, calls=%fused_computation.5 | convolution fusion | flops 2147483648 | bytes 13107200 | tf_op jit(solution)/shard_map/dot_general | solution.py:129
  379.6 4.7 copy.70
  386.0 4.9 gather_fusion.1
  392.1 6.6 %gather_fusion = bf16[640,1024]{1,0:T(8,128)(2,1)S(1)} fusion(bf16[2048,1024]{1,0:T(8,128)(2,1)} %param.16, s32[1024]{0:T(1024)S(1)} %pad_clamp_fusion), kind=kCustom, calls=%fused_computation | custom fusion | bytes 2624000 | tf_op jit(solution)/shard_map/jit(_take)/gather | solution.py:60
  400.3 4.2 convert_multiply_fusion
  404.6 29.6 %reduce-scatter.5.cloned.1.call-done = f32[128,4096]{1,0:T(8,128)} async-done(((f32[256,4096]{1,0:T(8,128)}), f32[128,4096]{1,0:T(8,128)}) %reduce-scatter.5.cloned.1.call-update) | async-done | bytes 2097168 | tf_op jit(solution)/shard_map/reduce_scatter | solution.py:128
  436.4 5.0 fusion.24
  441.4 2.9 multiply_reduce_fusion
  444.5 4.8 reshape.790
  452.4 5.0 convolution_convert_fusion
  458.8 3.9 copy.72
  462.7 5.0 copy.73
  467.7 4.7 fusion.114
  472.4 3.8 copy.74
  476.6 3.2 copy.76
  479.8 4.8 copy.75
  484.6 2.8 convert_bitcast_fusion
  488.7 3.1 multiply_reduce_fusion.1
  491.8 5.9 %fusion.113 = (f32[768]{0:T(1024)S(1)}, f32[768,2048]{1,0:T(8,128)}) fusion(bf16[1024,2048]{1,0:T(8,128)(2,1)S(1)} %copy-done.17, f32[768,1024]{1,0:T(8,128)S(1)} %get-tuple-element.35, f32[768]{0:T(1024)S(1)} %add_rsqrt_fusion), kind=kOutput, calls=%fused_computation.160 | convolution fusion | flops 3224370432 | bytes 13637632 | tf_op jit(solution)/shard_map/dot_general | solution.py:83
  497.8 9.8 %gather_fusion.2 = f32[768]{0:T(1024)S(1)} fusion(f32[768,2048]{1,0:T(8,128)} %get-tuple-element.37, s32[768]{0:T(1024)S(1)} %fusion.83), kind=kCustom, calls=%fused_computation.2 | custom fusion | bytes 12288 | tf_op jit(solution)/shard_map/jit(take_along_axis)/gather | solution.py:85
  507.8 3.8 exponential_reduce_fusion
  511.9 11.5 %psum.7 = f32[1,128,6]{2,1,0:T(8,128)S(1)} all-reduce(f32[1,128,6]{2,1,0:T(8,128)S(1)} %fusion.75), channel_id=1, replica_groups=mesh['dp'=32,'segment'=2,'frame'=2] {'segment'}, use_global_device_ids=true, to_apply=%region_15.16 | all-reduce | flops 768 | bytes 6144 | tf_op jit(solution)/shard_map/psum | solution.py:19
  (112 shorter events, 41.0 us)
Async XLA Ops:
  6.5 482.1 %copy-start = (bf16[512,1024]{1,0:T(8,128)(2,1)S(1)}, bf16[512,1024]{1,0:T(8,128)(2,1)}, u32[]{:S(2)}) copy-start(bf16[512,1024]{1,0:T(8,128)(2,1)} %param.15) | copy-start | bytes 3145732
  6.5 40.9 %all-gather.7.cloned.1.call-start = ((), (), s32[]{:S(2)}) async-start(), calls=%async_computation.2 | async-start | bytes 3145728 | tf_op jit(solution)/shard_map/all_gather | solution.py:123
  6.5 4.3 copy-start.7
  10.8 143.2 %all-gather.11.cloned.1.call-start = ((), (), s32[]{:S(2)}) async-start(), calls=%async_computation.6 | async-start | bytes 25952256 | tf_op jit(solution)/shard_map/all_gather | solution.py:110
  12.0 204.6 %all-gather.13.cloned.1.call-start = ((), (), s32[]{:S(2)}) async-start(), calls=%async_computation.7 | async-start | bytes 8650752 | tf_op jit(solution)/shard_map/all_gather | solution.py:111
  12.8 268.2 %reduce-scatter.3.cloned.1.call-start = ((), (), s32[]{:S(2)}) async-start(), calls=%async_computation.3 | async-start | bytes 6291456 | tf_op jit(solution)/shard_map/reduce_scatter | solution.py:128
  166.5 1.6 copy-start.6
  224.4 56.6 %copy-start.3 = (bf16[1,128,4096]{2,1,0:T(8,128)(2,1)S(1)}, bf16[1,128,4096]{2,1,0:T(8,128)(2,1)}, u32[]{:S(2)}) copy-start(bf16[1,128,4096]{2,1,0:T(8,128)(2,1)} %param.10) | copy-start | bytes 3145732
  224.5 125.0 %all-gather.9.cloned.1.call-start = ((), (), s32[]{:S(2)}) async-start(), calls=%async_computation.4 | async-start | bytes 3145728 | tf_op jit(solution)/shard_map/all_gather | solution.py:123
  282.9 27.0 %collective-permute-start = (bf16[128,4096]{1,0:T(8,128)(2,1)S(1)}, bf16[128,4096]{1,0:T(8,128)(2,1)S(1)}, u32[]{:S(2)}, u32[]{:S(2)}) collective-permute-start(bf16[128,4096]{1,0:T(8,128)(2,1)S(1)} %fusion.13), channel_id=1, source_target_pairs={{0,2},{1,3},{4,6},{5,7},{8,10},{9,11},{12,14},{13,15},{16,18},{17,... | collective-permute-start | bytes 3145736 | tf_op jit(solution)/shard_map/ppermute | solution.py:14
  311.5 122.7 %reduce-scatter.5.cloned.1.call-start = ((), (), s32[]{:S(2)}) async-start(), calls=%async_computation.5 | async-start | bytes 6291456 | tf_op jit(solution)/shard_map/reduce_scatter | solution.py:128
  362.0 1.7 copy-start.5
  376.2 0.7 copy-start.14
  376.2 3.2 copy-start.8
  377.0 8.9 %collective-permute-start.1 = (s32[1,2,6]{1,2,0:T(8,128)S(1)}, s32[1,2,6]{1,2,0:T(8,128)S(1)}, u32[]{:S(2)}, u32[]{:S(2)}) collective-permute-start(s32[1,2,6]{1,2,0:T(8,128)S(1)} %slice.76), channel_id=1, source_target_pairs={{0,1},{2,3},{4,5},{6,7},{8,9},{10,11},{12,13},{14,15},{16,17},{18,... | collective-permute-start | bytes 152 | tf_op jit(solution)/shard_map/ppermute | solution.py:14
  379.4 6.3 %copy-start.12 = (s32[128]{0:T(128)}, s32[128]{0:T(128)S(1)}, u32[]{:S(2)}) copy-start(s32[128]{0:T(128)S(1)} %iota_add_fusion) | copy-start | bytes 1540
  385.1 0.8 copy-start.15
  398.7 1.6 copy-start.10
  434.2 2.2 copy-start.1
  436.4 5.0 copy-start.2
  449.3 3.2 copy-start.4
  472.4 3.8 copy-start.11
  488.7 3.2 copy-start.17
  507.8 3.9 copy-start.9
  507.8 3.9 copy-start.13
  507.8 3.9 copy-start.16
Sparse Core Ops, SparseCore 0:
  10.9 36.5 all-gather.6
  49.7 104.2 all-gather.10
  156.2 60.4 all-gather.12
  224.6 56.3 reduce-scatter.2
  311.6 37.8 all-gather.8
  376.4 57.7 reduce-scatter.4
where the time goes:
time: 539 us; the launch traced here: 531 us
  waiting for transfers between devices  331 us (61%)
  matrix products  76 us (14%)
  local copies, waits for them, and re-layouts  64 us (12%)
  other arithmetic  26.4 us (5%)
  between operations  14.3 us (3%)
  blocking collectives  11.5 us (2%)
  starting transfers between devices  7.78 us (1%)
    all_gather x1, waiting for transfers between devices, local(): lax.all_gather(qkv_weight[0], 'dp', axis=0, tiled=True)  106 us
    reduce_scatter x2, waiting for transfers between devices, local(): lax.psum_scatter(jnp.dot(context, w_out, preferred_element_type=jnp.float...  86.1 us
    all_gather x2, waiting for transfers between devices, local(): lax.all_gather(normed, 'frame', axis=0, tiled=True)  71.7 us
    all_gather x1, waiting for transfers between devices, local(): lax.all_gather(out_weight[0], 'dp', axis=1, tiled=True)  43.7 us
    dot_general x2, matrix products, local(): jnp.dot(lax.all_gather(normed, 'frame', axis=0, tiled=True), w_matrix, pr...  25.1 us
    ppermute x2, waiting for transfers between devices, shifted(): lax.ppermute(value, axis, [(source, source + steps) for source in range(f...  22.3 us
    dot_general x2, matrix products, local(): jnp.dot(context, w_out, preferred_element_type=jnp.float32)  15.5 us
    psum x1, blocking collectives, spread(): return lax.psum(kept, axis)  11.5 us
  transfers between devices with their start and end apart: 8, of which 7 were waited for; matrix products, arithmetic and copies ran while one was open for 8% of the time, Pallas kernels for 0%

commit v1 on v0

v1 whole, which is shorter than its diff:
```python
import functools

import jax
import jax.numpy as jnp
from jax import lax
from jax.experimental import pallas as pl
from jax.experimental.pallas import tpu as pltpu
from jax.sharding import PartitionSpec as P

HD = 128
DMAX = 2
ZN, YN = 4, 4
SIDE = 4
BF = jnp.bfloat16
F32 = jnp.float32
EPS = 1e-05


def hop(value, axis, sign=1):
    pairs = []
    for z in range(ZN):
        for y in range(YN):
            for c in range(2):
                step = sign * (1 - 2 * c)
                there = {
                    "z": ((z + step) % ZN, y, c),
                    "y": (z, (y + step) % YN, c),
                    "core": (z, y, 1 - c),
                }[axis]
                pairs.append(
                    ((z * YN + y) * 2 + c, (there[0] * YN + there[1]) * 2 + there[2])
                )
    return lax.ppermute(value, "dp", pairs)


def xswap(value, pairs):
    return lax.ppermute(value, ("segment", "frame"), pairs)


def xhop(value, sign):
    pairs = []
    for d in range(2 * ZN * YN):
        step = sign * (1 - 2 * (d % 2))
        pairs += [(d * SIDE + i, d * SIDE + (i + step) % SIDE) for i in range(SIDE)]
    return lax.ppermute(value, ("dp", "segment", "frame"), pairs)


def tied(values, after):
    return lax.optimization_barrier((values, after))[0]


ORDER = (0, 1, -1, 2)


def ring(first, second):
    each = (first, second)
    near = [[hop(block, axis), hop(block, axis, -1)] for axis, block in each]
    near, blocks = lax.optimization_barrier((near, [first[1], second[1]]))
    far = [hop(ahead, axis) for (axis, _), (ahead, _) in zip(each, near)]
    return [[block, *two, one] for block, two, one in zip(blocks, near, far)]


def gather(a, b):
    a, b = ring(("z", a), ("y", b))
    a, b = jnp.concatenate(a), jnp.concatenate(b)
    a, b = ring(("y", a), ("z", b))
    return [p for mine in (a, b) for p in mine + [hop(block, "core") for block in mine]]


def vmem():
    return pl.BlockSpec(memory_space=pltpu.VMEM)


def smem():
    return pl.BlockSpec(memory_space=pltpu.SMEM)


def anywhere():
    return pl.BlockSpec(memory_space=pl.ANY)


def rms(values):
    scale = lax.rsqrt(jnp.mean(values * values, axis=-1, keepdims=True) + EPS)
    return (values * scale).astype(BF)


def norm_kernel(x_ref, o_ref):
    o_ref[...] = rms(x_ref[...].astype(F32))


def norm_rows(x):
    return pl.pallas_call(
        norm_kernel,
        out_shape=jax.ShapeDtypeStruct(x.shape, BF),
        in_specs=[vmem()],
        out_specs=vmem(),
        name="norm_rows",
    )(x)


def summed(*refs):
    total = refs[0][...].astype(F32)
    for ref in refs[1:]:
        total = total + ref[...].astype(F32)
    return total.astype(BF)


def merge_kernel(x_ref, a_ref, b_ref, c_ref, x_out, n_out):
    new = summed(x_ref, a_ref, b_ref, c_ref)
    x_out[...] = new
    n_out[...] = rms(new.astype(F32))


def merge_rows(x, parts):
    return pl.pallas_call(
        merge_kernel,
        out_shape=[jax.ShapeDtypeStruct(x.shape, BF)] * 2,
        in_specs=[vmem()] * 4,
        out_specs=[vmem()] * 2,
        name="merge_rows",
    )(x, *parts)


def softmax_rounded(scores):
    top = jnp.max(scores, axis=-1, keepdims=True)
    weights = jnp.exp(scores - top)
    return (weights / jnp.sum(weights, axis=-1, keepdims=True)).astype(BF)


NT = (((1,), (1,)), ((), ()))


def layer_kernel(x_count, w_count, *refs):
    place, cos_ref, sin_ref = refs[:3]
    at = 3 + x_count
    x_refs, w_refs = refs[3:at], refs[at : at + w_count]
    outs = refs[at + w_count : at + w_count + SIDE]
    x_s, w_s, ctx_s, out_s, x_sem, w_sem, o_sem = refs[at + w_count + SIDE :]
    z, y, c = place[0], place[1], place[2]

    def chunk_of(piece, j):
        near, far = (j, piece % 4) if piece < 8 else (piece % 4, j)
        core = c if piece % 8 < 4 else 1 - c
        step = 2 * core - 1
        far_z, far_y = z + step * ORDER[near], y + step * ORDER[far]
        return ((far_z & 3) * YN + (far_y & 3)) * 2 + core

    for i, ref in enumerate(x_refs):
        start = pl.multiple_of(place[3 + i], 64)
        pltpu.make_async_copy(ref, x_s.at[pl.ds(start, ref.shape[0])], x_sem).start()
    for half in range(2):
        if w_count == 1:
            pltpu.make_async_copy(
                w_refs[0].at[:, half], w_s.at[half], w_sem.at[half]
            ).start()
            continue
        for i in range(8 * half, 8 * half + 8):
            for j in range(4):
                pltpu.make_async_copy(
                    w_refs[i].at[pl.ds(128 * j, 128)],
                    w_s.at[half, chunk_of(i, j)],
                    w_sem.at[half],
                ).start()

    pltpu.make_async_copy(x_s, x_s, x_sem).wait()
    rows = x_s.shape[0]
    lower = lax.broadcasted_iota(jnp.int32, (rows, rows), 0) >= lax.broadcasted_iota(
        jnp.int32, (rows, rows), 1
    )
    cosine, sine = cos_ref[...], sin_ref[...]
    scale = 1.0 / jnp.sqrt(F32(HD))

    def turned(v):
        return (v * cosine + pltpu.roll(v, HD // 2, 1) * sine).astype(BF)

    width = x_s.shape[1]
    for half in range(2):
        pltpu.make_async_copy(w_s.at[half], w_s.at[half], w_sem.at[half]).wait()
        q, k, v = (
            jnp.dot(
                x_s[...],
                w_s[half, :, :, 256 * i : 256 * i + 256].reshape(width, 256),
                preferred_element_type=F32,
            )
            for i in range(3)
        )
        for head in range(2):
            cut = slice(head * HD, head * HD + HD)
            scores = lax.dot_general(
                turned(q[:, cut]), turned(k[:, cut]), NT, preferred_element_type=F32
            )
            weights = softmax_rounded(jnp.where(lower, scores * scale, -1e30))
            context = jnp.dot(weights, v[:, cut].astype(BF), preferred_element_type=F32)
            ctx_s[half, :, cut] = context.astype(BF)

    tile = 512

    def project(n, _):
        total = None
        for half in range(2):
            part = lax.dot_general(
                ctx_s[half],
                w_s[half, pl.ds(n * (tile // 128), tile // 128), :, 768:].reshape(tile, 256),
                NT, preferred_element_type=F32,
            )
            total = part if total is None else total + part
        out_s[:, pl.ds(pl.multiple_of(n * tile, tile), tile)] = total.astype(BF)
        return _

    lax.fori_loop(0, out_s.shape[1] // tile, project, 0)
    copies = []
    for i, ref in enumerate(outs):
        start = pl.multiple_of(place[8 + i], 64)
        copies.append(
            pltpu.make_async_copy(out_s.at[pl.ds(start, 64)], ref, o_sem.at[i])
        )
        copies[-1].start()
    for copy in copies:
        copy.wait()


def layer(place, cosine, sine, x_blocks, weights):
    width = x_blocks[0].shape[1]
    rows = sum(b.shape[0] for b in x_blocks)
    return pl.pallas_call(
        functools.partial(layer_kernel, len(x_blocks), len(weights)),
        out_shape=[jax.ShapeDtypeStruct((64, width), BF)] * SIDE,
        in_specs=[smem(), vmem(), vmem()]
        + [anywhere()] * (len(x_blocks) + len(weights)),
        out_specs=[anywhere()] * SIDE,
        scratch_shapes=[
            pltpu.VMEM((rows, width), BF),
            pltpu.VMEM((2, width // 128, 128, 1024), BF),
            pltpu.VMEM((2, rows, 256), BF),
            pltpu.VMEM((rows, width), BF),
            pltpu.SemaphoreType.DMA,
            pltpu.SemaphoreType.DMA((2,)),
            pltpu.SemaphoreType.DMA((SIDE,)),
        ],
        compiler_params=pltpu.CompilerParams(vmem_limit_bytes=56 * 2**20),
        cost_estimate=pl.CostEstimate(
            flops=2 * rows * width * 2048, bytes_accessed=2**24, transcendentals=0
        ),
        name="layer",
    )(place, cosine, sine, *x_blocks, *weights)


TF = 16


def depth_kernel(x_ref, a_ref, b_ref, c_ref, proj, dqkv, dout, logit, emb, target,
                 o_ref, u_s, qkv_s, ctx_s):
    new = summed(x_ref, a_ref, b_ref, c_ref)
    normed = rms(new.astype(F32))
    depth_in = jnp.dot(normed, proj[...], preferred_element_type=F32).astype(BF)
    depth_in = depth_in.astype(F32)
    frames = x_ref.shape[0]
    streams = u_s.shape[0] // frames
    span = TF * streams
    for tile in range(frames // TF):
        base = depth_in[tile * TF : tile * TF + TF]
        for k in range(streams):
            cut = slice(tile * span + k * TF, tile * span + k * TF + TF)
            u_s[cut] = base + emb[cut].astype(F32)
    inputs = rms(u_s[...])
    for i in range(3):
        qkv_s[i] = jnp.dot(inputs, dqkv[i], preferred_element_type=F32).astype(BF)
    r = lax.broadcasted_iota(jnp.int32, (span, span), 0)
    q = lax.broadcasted_iota(jnp.int32, (span, span), 1)
    seen = ((r & (TF - 1)) == (q & (TF - 1))) & (r >= q)
    head_width = dout.shape[0]
    lane = lax.broadcasted_iota(jnp.int32, (span, 128), 1)
    for tile in range(frames // TF):
        rows = slice(tile * span, tile * span + span)
        for pair in range(head_width // 128):
            cut = slice(pair * 128, pair * 128 + 128)
            queries, keys, values = (qkv_s[i, rows, cut] for i in range(3))
            both = []
            for head in range(2):
                mine = (lane < 64) if head == 0 else (lane >= 64)
                scores = lax.dot_general(
                    jnp.where(mine, queries, jnp.zeros_like(queries)),
                    keys, NT, preferred_element_type=F32,
                )
                weights = softmax_rounded(jnp.where(seen, scores * 0.125, -1e30))
                both.append(jnp.dot(weights, values, preferred_element_type=F32))
            ctx_s[rows, cut] = jnp.where(lane < 64, both[0], both[1]).astype(BF)
    mixed = u_s[...] + jnp.dot(ctx_s[...], dout[...], preferred_element_type=F32)
    logits = jnp.dot(rms(mixed), logit[...], preferred_element_type=F32)
    top = jnp.max(logits, axis=-1, keepdims=True)
    total = jnp.sum(jnp.exp(logits - top), axis=-1, keepdims=True)
    entry = lax.broadcasted_iota(jnp.int32, logits.shape, 1)
    picked = jnp.sum(jnp.where(entry == target[...], logits, 0.0), axis=-1, keepdims=True)
    o_ref[...] = jnp.log(total) + top - picked


def depth(x, parts, proj, dqkv, dout, logit, emb, target):
    count, width = emb.shape
    head_width = dout.shape[0]
    return pl.pallas_call(
        depth_kernel,
        out_shape=jax.ShapeDtypeStruct((count, 1), F32),
        in_specs=[vmem()] * 10,
        out_specs=vmem(),
        scratch_shapes=[
            pltpu.VMEM((count, width), F32),
            pltpu.VMEM((3, count, head_width), BF),
            pltpu.VMEM((count, head_width), BF),
        ],
        compiler_params=pltpu.CompilerParams(vmem_limit_bytes=48 * 2**20),
        cost_estimate=pl.CostEstimate(
            flops=2 * count * width * 5120, bytes_accessed=2**24, transcendentals=0
        ),
        name="depth",
    )(x, *parts, proj, dqkv, dout, logit, emb, target)


def rope_tables(rows):
    half = HD // 2
    frequency = 10000.0 ** (-jnp.arange(half, dtype=F32) / half)
    angles = jnp.arange(rows).astype(F32)[:, None] * frequency[None, :]
    cosine, sine = jnp.cos(angles), jnp.sin(angles)
    return (
        jnp.concatenate([cosine, cosine], axis=1),
        jnp.concatenate([-sine, sine], axis=1),
    )


def packed_weights(qkv_weight, out_weight):
    w = jnp.transpose(qkv_weight[0], (1, 0, 2))
    o = out_weight[0]
    blocks = []
    for i in range(4):
        cut = slice(256 * i, 256 * i + 256)
        blocks.append(
            jnp.concatenate([w[0][:, cut], w[1][:, cut], w[2][:, cut], o[cut].T], axis=1)
        )
    return jnp.stack(blocks).reshape(2, 2, 128, 1024)


def local(
    frames_in, qkv_weight, out_weight, proj_weight, depth_qkv, depth_out, code_table,
    logit_weight, codes, delays,
):
    s = lax.axis_index("segment")
    f = lax.axis_index("frame")
    d = lax.axis_index("dp")
    z, y, c = d // (YN * 2), (d // 2) % YN, d % 2
    row_count = frames_in.shape[1]
    part = row_count // 2
    streams = codes.shape[2]
    me = s * 2 + f

    def rows_of(i):
        i = i % SIDE
        return (i % 2) * row_count + (i // 2) * part

    sign = 1 - 2 * c

    def place_of(starts):
        starts = (list(starts) + [0] * 5)[:5]
        targets = [rows_of(me + k * sign + 4) for k in (0, 1, 2, 3)]
        return jnp.stack([z, y, c, *starts, *targets]).astype(jnp.int32)

    packed = packed_weights(qkv_weight, out_weight)
    kept = lax.dynamic_index_in_dim(packed, s, 0, keepdims=False)
    given = lax.dynamic_index_in_dim(packed, 1 - s, 0, keepdims=False)
    got = xswap(given, [(0, 3), (3, 0), (1, 2), (2, 1)])
    first = jnp.where(s == 0, kept, got)
    second = jnp.where(s == 0, got, kept)
    frames = frames_in[0]
    normed = norm_rows(frames)
    far = xhop(tied(normed, got), 1)

    w0 = gather(first[0], first[1])
    w1 = [lax.all_gather(tied(second, (w0[1], w0[2], w0[9], w0[10])), "dp")]

    tail = lax.ppermute(codes[0, row_count - DMAX :], "frame", [(0, 1)])
    extended = jnp.concatenate([tail, codes[0]], axis=0)
    extended = lax.dynamic_slice_in_dim(extended, s * part, part + DMAX, 0)
    targets = extended[DMAX : DMAX + part]
    for lag in range(1, DMAX + 1):
        targets = jnp.where(
            delays[None, :] == lag, extended[DMAX - lag : DMAX - lag + part], targets
        )
    frame = rows_of(me) + jnp.arange(part, dtype=jnp.int32)
    is_valid = frame[:, None] >= delays[None, :]
    targets = jnp.clip(targets, 0, code_table.shape[0] - 1)

    def tiled(a):
        return jnp.transpose(a.reshape(part // TF, TF, streams), (0, 2, 1)).reshape(-1)

    def behind(a):
        return jnp.concatenate([jnp.zeros_like(a[:, :1]), a[:, :-1]], axis=1)

    emb = jnp.take(code_table, tiled(behind(targets)), axis=0, mode="clip")
    emb = jnp.where(tiled(behind(is_valid))[:, None], emb, jnp.zeros_like(emb))

    cosine, sine = tied(rope_tables(2 * row_count), emb)
    sent = layer(
        place_of([f * row_count, (1 - f) * row_count]), cosine, sine, [normed, far], w0
    )

    def scattered(sent):
        back = xhop(sent[3], -1)
        relayed = xhop(sent[2], 1)
        relayed = (sent[1].astype(F32) + relayed.astype(F32)).astype(BF)
        return [sent[0], xhop(relayed, 1), back]

    mine = lax.dynamic_slice_in_dim(frames, s * part, part, 0)
    x1, n1 = merge_rows(mine, scattered(sent))
    ahead = xhop(n1, 1)
    blocks = [n1, ahead, xhop(n1, -1), xhop(ahead, 1)]
    starts = [rows_of(me + k * sign + 4) for k in (0, -1, 1, -2)]
    sent = layer(place_of(starts), cosine, sine, blocks, w1)

    losses = depth(
        x1, scattered(sent), proj_weight, jnp.transpose(depth_qkv, (1, 0, 2)),
        depth_out, logit_weight, emb, tiled(targets)[:, None],
    )
    losses = jnp.transpose(losses.reshape(part // TF, streams, TF), (0, 2, 1))
    losses = jnp.where(is_valid, losses.reshape(part, streams), 0.0)
    other = xswap(losses, [(i, (i + 2) % SIDE) for i in range(SIDE)])
    both = jnp.where(s == 0, jnp.stack([losses, other]), jnp.stack([other, losses]))
    return both.reshape(1, row_count, streams)


def solution(mesh):
    return jax.shard_map(
        local,
        mesh=mesh,
        in_specs=(
            P("dp", "frame", None),
            P("segment", "dp", None, "frame"),
            P("segment", "frame", "dp"),
            P(),
            P(),
            P(),
            P(),
            P(),
            P("dp", "frame", None),
            P(),
        ),
        out_specs=P("dp", "frame", None),
        check_vma=False,
    )
```

time: 539 us -> 269 us (0.50); the launches traced: 531 us -> 268 us
  waiting for transfers between devices: 331 us -> 138 us
  matrix products: 76 us -> 0 us
  Pallas kernels: 0 us -> 60.1 us
  local copies, waits for them, and re-layouts: 64 us -> 17.7 us
  starting transfers between devices: 7.78 us -> 32.8 us
  other arithmetic: 26.4 us -> 6.23 us
  blocking collectives: 11.5 us -> 0 us
    all_gather x4 -> x1, waiting for transfers between devices: 222 us -> 0.01 us  [local(): w1 = [lax.all_gather(tied(second, (w0[1], w0[2], w0[9], w0[10])), 'dp')]]
    ppermute x2 -> x33, waiting for transfers between devices: 22.3 us -> 138 us  [the longest x10 63.1 us: xhop(): return lax.ppermute(value, ('dp', 'segment', 'frame'), pairs)]
    reduce_scatter x2 -> x0, waiting for transfers between devices: 86.1 us -> none  [local(): lax.psum_scatter(jnp.dot(context, w_out, preferred_element_type=jnp.float...]
    dot_general x12 -> x0, matrix products: 71.5 us -> none  [the longest x2 25.1 us: local(): jnp.dot(lax.all_gather(normed, 'frame', axis=0, tiled=True), w_matrix, pr...]
    pallas_call x0 -> x5, Pallas kernels: none -> 60.1 us  [the longest x2 33.1 us: layer(): pl.pallas_call(functools.partial(layer_kernel, len(x_blocks), len(weights...]
    ppermute x2 -> x33, starting transfers between devices: 7.05 us -> 32.8 us  [the longest x20 18.4 us: hop(): return lax.ppermute(value, 'dp', pairs)]
    gather x8 -> x1, local copies, waits for them, and re-layouts: 23.4 us -> 5.76 us  [local(): emb = jnp.take(code_table, tiled(behind(targets)), axis=0, mode='clip')]
    squeeze x6 -> x2, local copies, waits for them, and re-layouts: 15.4 us -> 0.09 us  [the longest x1 0.05 us: packed_weights(): w[0][:, cut]]
  transfers between devices with their start and end apart: 8 -> 34, of which waited for: 7 -> 17; matrix products, arithmetic and copies ran while one was open for 8% -> 6% of each run, Pallas kernels for 0% -> 9%
where the time goes in v1:
time: 269 us; the launch traced here: 268 us
  waiting for transfers between devices  138 us (51%)
  Pallas kernels  60.1 us (22%)
  starting transfers between devices  32.8 us (12%)
  local copies, waits for them, and re-layouts  17.7 us (7%)
  between operations  13.8 us (5%)
  other arithmetic  6.23 us (2%)
    ppermute x10, waiting for transfers between devices, xhop(): return lax.ppermute(value, ('dp', 'segment', 'frame'), pairs)  63.1 us
    ppermute x20, waiting for transfers between devices, hop(): return lax.ppermute(value, 'dp', pairs)  50 us
    pallas_call x2, Pallas kernels, layer(): pl.pallas_call(functools.partial(layer_kernel, len(x_blocks), len(weights...  33.1 us
    pallas_call x1, Pallas kernels, depth(): pl.pallas_call(depth_kernel, out_shape=jax.ShapeDtypeStruct((count, 1), F...  21.5 us
    ppermute x20, starting transfers between devices, hop(): return lax.ppermute(value, 'dp', pairs)  18.4 us
    ppermute x2, waiting for transfers between devices, xswap(): return lax.ppermute(value, ('segment', 'frame'), pairs)  16.7 us
    ppermute x10, starting transfers between devices, xhop(): return lax.ppermute(value, ('dp', 'segment', 'frame'), pairs)  10.2 us
    ppermute x1, waiting for transfers between devices, local(): tail = lax.ppermute(codes[0, row_count - DMAX:], 'frame', [(0, 1)])  7.99 us
  transfers between devices with their start and end apart: 34, of which 17 were waited for; matrix products, arithmetic and copies ran while one was open for 6% of the time, Pallas kernels for 9%

profile of v1, /device:TPU:0, one launch (start us, length us, event | category | flops | bytes accessed | tf_op | source)
XLA Modules:
  0.0 268.5 jit_solution(3550757588542949827)
XLA Ops:
  9.7 2.9 %collective-permute-start.1 = (bf16[2,128,1024]{2,1,0:T(8,128)(2,1)S(1)}, bf16[2,128,1024]{2,1,0:T(8,128)(2,1)S(1)}, u32[]{:S(2)}, u32[]{:S(2)}) collective-permute-start(bf16[2,128,1024]{2,1,0:T(8,128)(2,1)S(1)} %bitcast.92), channel_id=1, source_target_pairs={{0,3},{3,0},{1,2},{2,1},{4,7},{7,4},{5,6},{6,5},{8,11},{11,8},{9,1... | collective-permute-start | bytes 1572872 | tf_op jit(solution)/shard_map/ppermute | solution.py:37
  12.8 11.7 %collective-permute-done.1 = bf16[2,128,1024]{2,1,0:T(8,128)(2,1)S(1)} collective-permute-done((bf16[2,128,1024]{2,1,0:T(8,128)(2,1)S(1)}, bf16[2,128,1024]{2,1,0:T(8,128)(2,1)S(1)}, u32[]{:S(2)}, u32[]{:S(2)}) %collective-permute-start.1) | collective-permute-done | bytes 524320 | tf_op jit(solution)/shard_map/ppermute | solution.py:37
  25.4 2.2 collective-permute-start.3
  27.6 2.2 collective-permute-start.4
  33.1 2.9 %collective-permute-done.3 = bf16[128,1024]{1,0:T(8,128)(2,1)S(1)} collective-permute-done((bf16[128,1024]{1,0:T(8,128)(2,1)S(1)}, bf16[128,1024]{1,0:T(8,128)(2,1)S(1)}, u32[]{:S(2)}, u32[]{:S(2)}) %collective-permute-start.3) | collective-permute-done | bytes 262176 | tf_op jit(solution)/shard_map/ppermute | solution.py:33
  36.0 4.0 %collective-permute-done.5 = bf16[128,1024]{1,0:T(8,128)(2,1)S(1)} collective-permute-done((bf16[128,1024]{1,0:T(8,128)(2,1)S(1)}, bf16[128,1024]{1,0:T(8,128)(2,1)S(1)}, u32[]{:S(2)}, u32[]{:S(2)}) %collective-permute-start.5) | collective-permute-done | bytes 262176 | tf_op jit(solution)/shard_map/ppermute | solution.py:33
  42.3 5.3 %collective-permute-done.7 = bf16[128,1024]{1,0:T(8,128)(2,1)S(1)} collective-permute-done((bf16[128,1024]{1,0:T(8,128)(2,1)S(1)}, bf16[128,1024]{1,0:T(8,128)(2,1)S(1)}, u32[]{:S(2)}, u32[]{:S(2)}) %collective-permute-start.7) | collective-permute-done | bytes 262176 | tf_op jit(solution)/shard_map/ppermute | solution.py:33
  47.7 3.2 %collective-permute-start.9 = (bf16[512,1024]{1,0:T(8,128)(2,1)S(1)}, bf16[512,1024]{1,0:T(8,128)(2,1)S(1)}, u32[]{:S(2)}, u32[]{:S(2)}) collective-permute-start(bf16[512,1024]{1,0:T(8,128)(2,1)S(1)} %constant_dynamic-update-slice_fusion.refs_5_), channel_id=1, source_target_pairs={{0,24},{4,12},{8,0},{12,20},{16,8},{20,28},{24,16},{28,4},{32,56},... | collective-permute-start | bytes 3145736 | tf_op jit(solution)/shard_map/ppermute | solution.py:33
  51.7 3.2 %collective-permute-start.12 = (bf16[512,1024]{1,0:T(8,128)(2,1)}, bf16[512,1024]{1,0:T(8,128)(2,1)}, u32[]{:S(2)}, u32[]{:S(2)}) collective-permute-start(bf16[512,1024]{1,0:T(8,128)(2,1)} %constant_dynamic-update-slice_fusion.4.refs_13_), channel_id=1, source_target_pairs={{0,96},{4,36},{8,104},{12,44},{16,112},{20,52},{24,120},{28,60},{3... | collective-permute-start | bytes 3145736 | tf_op jit(solution)/shard_map/ppermute | solution.py:33
  54.9 17.2 %collective-permute-done.8.refs_6_ = bf16[512,1024]{1,0:T(8,128)(2,1)S(1)} collective-permute-done((bf16[512,1024]{1,0:T(8,128)(2,1)S(1)}, bf16[512,1024]{1,0:T(8,128)(2,1)S(1)}, u32[]{:S(2)}, u32[]{:S(2)}) %collective-permute-start.8) | collective-permute-done | bytes 1048608 | tf_op jit(solution)/shard_map/ppermute | solution.py:33
  72.1 5.0 %collective-permute-done.11.refs_14_ = bf16[512,1024]{1,0:T(8,128)(2,1)} collective-permute-done((bf16[512,1024]{1,0:T(8,128)(2,1)}, bf16[512,1024]{1,0:T(8,128)(2,1)}, u32[]{:S(2)}, u32[]{:S(2)}) %collective-permute-start.11) | collective-permute-done | bytes 1048608 | tf_op jit(solution)/shard_map/ppermute | solution.py:33
  77.1 2.7 norm_rows.1.refs_3_
  80.8 2.6 collective-permute-start.14
  84.7 8.0 %collective-permute-done = s32[2,6]{1,0:T(2,128)S(1)} collective-permute-done((s32[2,6]{1,0:T(2,128)S(1)}, s32[2,6]{1,0:T(2,128)S(1)}, u32[]{:S(2)}, u32[]{:S(2)}) %collective-permute-start) | collective-permute-done | bytes 80 | tf_op jit(solution)/shard_map/ppermute | solution.py:378
  92.7 3.4 %collective-permute-done.2.refs_4_ = bf16[128,4096]{1,0:T(8,128)(2,1)} collective-permute-done((bf16[128,4096]{1,0:T(8,128)(2,1)}, bf16[128,4096]{1,0:T(8,128)(2,1)}, u32[]{:S(2)}, u32[]{:S(2)}) %collective-permute-start.2) | collective-permute-done | bytes 1048608 | tf_op jit(solution)/shard_map/ppermute | solution.py:45
  97.6 7.2 %collective-permute-done.13.refs_8_ = bf16[512,1024]{1,0:T(8,128)(2,1)} collective-permute-done((bf16[512,1024]{1,0:T(8,128)(2,1)S(1)}, bf16[512,1024]{1,0:T(8,128)(2,1)}, u32[]{:S(2)}, u32[]{:S(2)}) %collective-permute-start.13) | collective-permute-done | bytes 1048608 | tf_op jit(solution)/shard_map/ppermute | solution.py:33
  105.8 8.4 %collective-permute-done.18.refs_16_ = bf16[512,1024]{1,0:T(8,128)(2,1)} collective-permute-done((bf16[512,1024]{1,0:T(8,128)(2,1)}, bf16[512,1024]{1,0:T(8,128)(2,1)}, u32[]{:S(2)}, u32[]{:S(2)}) %collective-permute-start.18) | collective-permute-done | bytes 1048608 | tf_op jit(solution)/shard_map/ppermute | solution.py:33
  115.5 5.8 %gather_fusion = bf16[384,1024]{1,0:T(8,128)(2,1)S(1)} fusion(bf16[2048,1024]{1,0:T(8,128)(2,1)} %param.16, s32[1024]{0:T(1024)S(1)} %pad_clamp_fusion), kind=kCustom, calls=%fused_computation | custom fusion | bytes 1574400 | tf_op jit(solution)/shard_map/jit(_take)/gather | solution.py:396
  121.4 18.2 %layer.2 = (bf16[64,4096]{1,0:T(8,128)(2,1)}, bf16[64,4096]{1,0:T(8,128)(2,1)}, bf16[64,4096]{1,0:T(8,128)(2,1)}, bf16[64,4096]{1,0:T(8,128)(2,1)}) custom-call(s32[12]{0:T(128)} %stack.84.refs_0_, f32[256,128]{1,0:T(8,128)} %get-tuple-element.31.refs_1_, f32[256,128]{1,0:T(8,128)} %get-tuple-element.32.refs_2_, bf16[128,4096]{1,0:T(8,128)(2,1)} %norm_rows.1.refs_3_, ...), custom_call_target="tpu_custom_call" | custom-call | flops 4294967296 | bytes 16777216 | tf_op jit(solution)/shard_map/layer/pallas_call | solution.py:225
  139.7 3.2 %collective-permute-start.25 = (bf16[64,4096]{1,0:T(8,128)(2,1)}, bf16[64,4096]{1,0:T(8,128)(2,1)S(1)}, u32[]{:S(2)}, u32[]{:S(2)}) collective-permute-start(bf16[64,4096]{1,0:T(8,128)(2,1)} %get-tuple-element.49), channel_id=1, source_target_pairs={{0,3},{1,0},{2,1},{3,2},{4,5},{5,6},{6,7},{7,4},{8,11},{9,8},{10,9... | collective-permute-start | bytes 1572872 | tf_op jit(solution)/shard_map/ppermute | solution.py:45
  142.9 12.5 %collective-permute-done.23 = bf16[64,4096]{1,0:T(8,128)(2,1)S(1)} collective-permute-done((bf16[64,4096]{1,0:T(8,128)(2,1)}, bf16[64,4096]{1,0:T(8,128)(2,1)S(1)}, u32[]{:S(2)}, u32[]{:S(2)}) %collective-permute-start.23) | collective-permute-done | bytes 524320 | tf_op jit(solution)/shard_map/ppermute | solution.py:45
  157.6 9.6 %collective-permute-done.24.b_ref = bf16[64,4096]{1,0:T(8,128)(2,1)} collective-permute-done((bf16[64,4096]{1,0:T(8,128)(2,1)S(1)}, bf16[64,4096]{1,0:T(8,128)(2,1)}, u32[]{:S(2)}, u32[]{:S(2)}) %collective-permute-start.24) | collective-permute-done | bytes 524320 | tf_op jit(solution)/shard_map/ppermute | solution.py:45
  167.2 2.8 %merge_rows.1 = (bf16[64,4096]{1,0:T(8,128)(2,1)}, bf16[64,4096]{1,0:T(8,128)(2,1)}) custom-call(bf16[64,4096]{1,0:T(8,128)(2,1)} %dynamic-slice_bitcast_fusion.x_ref, bf16[64,4096]{1,0:T(8,128)(2,1)} %get-tuple-element.46.a_ref, bf16[64,4096]{1,0:T(8,128)(2,1)} %collective-permute-done.24.b_ref, bf16[64,4096]{1,0:T(8,128)(2,1)} %copy-done.10), custom_call_target="tpu_custom_call" | custom-call | tf_op jit(solution)/shard_map/merge_rows/pallas_call | solution.py:115
  170.1 3.2 %collective-permute-start.27 = (bf16[64,4096]{1,0:T(8,128)(2,1)}, bf16[64,4096]{1,0:T(8,128)(2,1)S(1)}, u32[]{:S(2)}, u32[]{:S(2)}) collective-permute-start(bf16[64,4096]{1,0:T(8,128)(2,1)} %get-tuple-element.51.refs_3_), channel_id=1, source_target_pairs={{0,3},{1,0},{2,1},{3,2},{4,5},{5,6},{6,7},{7,4},{8,11},{9,8},{10,9... | collective-permute-start | bytes 1572872 | tf_op jit(solution)/shard_map/ppermute | solution.py:45
  173.3 9.6 %collective-permute-done.26.refs_4_ = bf16[64,4096]{1,0:T(8,128)(2,1)S(1)} collective-permute-done((bf16[64,4096]{1,0:T(8,128)(2,1)}, bf16[64,4096]{1,0:T(8,128)(2,1)S(1)}, u32[]{:S(2)}, u32[]{:S(2)}) %collective-permute-start.26) | collective-permute-done | bytes 524320 | tf_op jit(solution)/shard_map/ppermute | solution.py:45
  183.6 9.7 %collective-permute-done.28.refs_6_ = bf16[64,4096]{1,0:T(8,128)(2,1)S(1)} collective-permute-done((bf16[64,4096]{1,0:T(8,128)(2,1)S(1)}, bf16[64,4096]{1,0:T(8,128)(2,1)S(1)}, u32[]{:S(2)}, u32[]{:S(2)}) %collective-permute-start.28) | collective-permute-done | bytes 524320 | tf_op jit(solution)/shard_map/ppermute | solution.py:45
  194.1 14.9 %layer.3 = (bf16[64,4096]{1,0:T(8,128)(2,1)}, bf16[64,4096]{1,0:T(8,128)(2,1)}, bf16[64,4096]{1,0:T(8,128)(2,1)}, bf16[64,4096]{1,0:T(8,128)(2,1)}) custom-call(s32[12]{0:T(128)} %stack.92.refs_0_, f32[256,128]{1,0:T(8,128)} %get-tuple-element.31.refs_1_, f32[256,128]{1,0:T(8,128)} %get-tuple-element.32.refs_2_, bf16[64,4096]{1,0:T(8,128)(2,1)} %get-tuple-element.51.refs_3_, ...), custom_call_target="tpu_custom_call" | custom-call | flops 4294967296 | bytes 16777216 | tf_op jit(solution)/shard_map/layer/pallas_call | solution.py:225
  209.1 3.2 %collective-permute-start.31 = (bf16[64,4096]{1,0:T(8,128)(2,1)}, bf16[64,4096]{1,0:T(8,128)(2,1)S(1)}, u32[]{:S(2)}, u32[]{:S(2)}) collective-permute-start(bf16[64,4096]{1,0:T(8,128)(2,1)} %get-tuple-element.56), channel_id=1, source_target_pairs={{0,3},{1,0},{2,1},{3,2},{4,5},{5,6},{6,7},{7,4},{8,11},{9,8},{10,9... | collective-permute-start | bytes 1572872 | tf_op jit(solution)/shard_map/ppermute | solution.py:45
  212.4 7.8 %collective-permute-done.29 = bf16[64,4096]{1,0:T(8,128)(2,1)S(1)} collective-permute-done((bf16[64,4096]{1,0:T(8,128)(2,1)}, bf16[64,4096]{1,0:T(8,128)(2,1)S(1)}, u32[]{:S(2)}, u32[]{:S(2)}) %collective-permute-start.29) | collective-permute-done | bytes 524320 | tf_op jit(solution)/shard_map/ppermute | solution.py:45
  222.3 10.5 %collective-permute-done.30.b_ref = bf16[64,4096]{1,0:T(8,128)(2,1)} collective-permute-done((bf16[64,4096]{1,0:T(8,128)(2,1)}, bf16[64,4096]{1,0:T(8,128)(2,1)}, u32[]{:S(2)}, u32[]{:S(2)}) %collective-permute-start.30) | collective-permute-done | bytes 524320 | tf_op jit(solution)/shard_map/ppermute | solution.py:45
  233.8 21.5 %depth.1 = f32[384,1]{1,0:T(8,128)S(1)} custom-call(bf16[64,4096]{1,0:T(8,128)(2,1)S(1)} %copy-done.1, bf16[64,4096]{1,0:T(8,128)(2,1)S(1)} %copy-done.2, bf16[64,4096]{1,0:T(8,128)(2,1)} %collective-permute-done.30.b_ref, bf16[64,4096]{1,0:T(8,128)(2,1)S(1)} %collective-permute-done.31.c_ref, bf16[4096,1024]{1,0:T(8,128)(2,1)} %proj.1, ...), custom_call_target="tpu_custom_call" | custom-call | flops 4026531840 | bytes 16777216 | tf_op jit(solution)/shard_map/depth/pallas_call | solution.py:300
  255.9 5.0 %collective-permute-done.32 = f32[64,6]{0,1:T(8,128)S(1)} collective-permute-done((f32[64,6]{0,1:T(8,128)S(1)}, f32[64,6]{0,1:T(8,128)S(1)}, u32[]{:S(2)}, u32[]{:S(2)}) %collective-permute-start.32) | collective-permute-done | bytes 1568 | tf_op jit(solution)/shard_map/ppermute | solution.py:37
  (133 shorter events, 25.0 us)
Async XLA Ops:
  6.5 186.8 %all-gather.3.cloned.1.call-start = ((), (), s32[]{:S(2)}) async-start(), calls=%async_computation | async-start | bytes 17301504 | tf_op jit(solution)/shard_map/all_gather | solution.py:376
  9.7 14.8 %collective-permute-start.1 = (bf16[2,128,1024]{2,1,0:T(8,128)(2,1)S(1)}, bf16[2,128,1024]{2,1,0:T(8,128)(2,1)S(1)}, u32[]{:S(2)}, u32[]{:S(2)}) collective-permute-start(bf16[2,128,1024]{2,1,0:T(8,128)(2,1)S(1)} %bitcast.92), channel_id=1, source_target_pairs={{0,3},{3,0},{1,2},{2,1},{4,7},{7,4},{5,6},{6,5},{8,11},{11,8},{9,1... | collective-permute-start | bytes 1572872 | tf_op jit(solution)/shard_map/ppermute | solution.py:37
  25.4 10.5 %collective-permute-start.3 = (bf16[128,1024]{1,0:T(8,128)(2,1)S(1)}, bf16[128,1024]{1,0:T(8,128)(2,1)S(1)}, u32[]{:S(2)}, u32[]{:S(2)}) collective-permute-start(bf16[128,1024]{1,0:T(8,128)(2,1)S(1)} %get-tuple-element.34), channel_id=1, source_target_pairs={{0,32},{4,100},{8,40},{12,108},{16,48},{20,116},{24,56},{28,124},{... | collective-permute-start | bytes 786440 | tf_op jit(solution)/shard_map/ppermute | solution.py:33
  27.6 8.3 %collective-permute-start.4 = (bf16[128,1024]{1,0:T(8,128)(2,1)S(1)}, bf16[128,1024]{1,0:T(8,128)(2,1)S(1)}, u32[]{:S(2)}, u32[]{:S(2)}) collective-permute-start(bf16[128,1024]{1,0:T(8,128)(2,1)S(1)} %get-tuple-element.34), channel_id=1, source_target_pairs={{0,96},{4,36},{8,104},{12,44},{16,112},{20,52},{24,120},{28,60},{3... | collective-permute-start | bytes 786440 | tf_op jit(solution)/shard_map/ppermute | solution.py:33
  29.8 10.1 %collective-permute-start.5 = (bf16[128,1024]{1,0:T(8,128)(2,1)S(1)}, bf16[128,1024]{1,0:T(8,128)(2,1)S(1)}, u32[]{:S(2)}, u32[]{:S(2)}) collective-permute-start(bf16[128,1024]{1,0:T(8,128)(2,1)S(1)} %get-tuple-element.37), channel_id=1, source_target_pairs={{0,8},{4,28},{8,16},{12,4},{16,24},{20,12},{24,0},{28,20},{32,40},... | collective-permute-start | bytes 786440 | tf_op jit(solution)/shard_map/ppermute | solution.py:33
  31.4 8.5 %collective-permute-start.6 = (bf16[128,1024]{1,0:T(8,128)(2,1)S(1)}, bf16[128,1024]{1,0:T(8,128)(2,1)S(1)}, u32[]{:S(2)}, u32[]{:S(2)}) collective-permute-start(bf16[128,1024]{1,0:T(8,128)(2,1)S(1)} %get-tuple-element.37), channel_id=1, source_target_pairs={{0,24},{4,12},{8,0},{12,20},{16,8},{20,28},{24,16},{28,4},{32,56},... | collective-permute-start | bytes 786440 | tf_op jit(solution)/shard_map/ppermute | solution.py:33
  40.0 7.7 %collective-permute-start.7 = (bf16[128,1024]{1,0:T(8,128)(2,1)S(1)}, bf16[128,1024]{1,0:T(8,128)(2,1)S(1)}, u32[]{:S(2)}, u32[]{:S(2)}) collective-permute-start(bf16[128,1024]{1,0:T(8,128)(2,1)S(1)} %collective-permute-done.3), channel_id=1, source_target_pairs={{0,32},{4,100},{8,40},{12,108},{16,48},{20,116},{24,56},{28,124},{... | collective-permute-start | bytes 786440 | tf_op jit(solution)/shard_map/ppermute | solution.py:33
  40.8 10.2 %collective-permute-start.10 = (bf16[128,1024]{1,0:T(8,128)(2,1)S(1)}, bf16[128,1024]{1,0:T(8,128)(2,1)S(1)}, u32[]{:S(2)}, u32[]{:S(2)}) collective-permute-start(bf16[128,1024]{1,0:T(8,128)(2,1)S(1)} %collective-permute-done.5), channel_id=1, source_target_pairs={{0,8},{4,28},{8,16},{12,4},{16,24},{20,12},{24,0},{28,20},{32,40},... | collective-permute-start | bytes 786440 | tf_op jit(solution)/shard_map/ppermute | solution.py:33
  47.6 24.5 %collective-permute-start.8 = (bf16[512,1024]{1,0:T(8,128)(2,1)S(1)}, bf16[512,1024]{1,0:T(8,128)(2,1)S(1)}, u32[]{:S(2)}, u32[]{:S(2)}) collective-permute-start(bf16[512,1024]{1,0:T(8,128)(2,1)S(1)} %constant_dynamic-update-slice_fusion.refs_5_), channel_id=1, source_target_pairs={{0,8},{4,28},{8,16},{12,4},{16,24},{20,12},{24,0},{28,20},{32,40},... | collective-permute-start | bytes 3145736 | tf_op jit(solution)/shard_map/ppermute | solution.py:33
  47.7 24.4 %collective-permute-start.9 = (bf16[512,1024]{1,0:T(8,128)(2,1)S(1)}, bf16[512,1024]{1,0:T(8,128)(2,1)S(1)}, u32[]{:S(2)}, u32[]{:S(2)}) collective-permute-start(bf16[512,1024]{1,0:T(8,128)(2,1)S(1)} %constant_dynamic-update-slice_fusion.refs_5_), channel_id=1, source_target_pairs={{0,24},{4,12},{8,0},{12,20},{16,8},{20,28},{24,16},{28,4},{32,56},... | collective-permute-start | bytes 3145736 | tf_op jit(solution)/shard_map/ppermute | solution.py:33
  51.7 25.4 %collective-permute-start.11 = (bf16[512,1024]{1,0:T(8,128)(2,1)}, bf16[512,1024]{1,0:T(8,128)(2,1)}, u32[]{:S(2)}, u32[]{:S(2)}) collective-permute-start(bf16[512,1024]{1,0:T(8,128)(2,1)} %constant_dynamic-update-slice_fusion.4.refs_13_), channel_id=1, source_target_pairs={{0,32},{4,100},{8,40},{12,108},{16,48},{20,116},{24,56},{28,124},{... | collective-permute-start | bytes 3145736 | tf_op jit(solution)/shard_map/ppermute | solution.py:33
  51.7 25.4 %collective-permute-start.12 = (bf16[512,1024]{1,0:T(8,128)(2,1)}, bf16[512,1024]{1,0:T(8,128)(2,1)}, u32[]{:S(2)}, u32[]{:S(2)}) collective-permute-start(bf16[512,1024]{1,0:T(8,128)(2,1)} %constant_dynamic-update-slice_fusion.4.refs_13_), channel_id=1, source_target_pairs={{0,96},{4,36},{8,104},{12,44},{16,112},{20,52},{24,120},{28,60},{3... | collective-permute-start | bytes 3145736 | tf_op jit(solution)/shard_map/ppermute | solution.py:33
  79.8 16.3 %collective-permute-start.2 = (bf16[128,4096]{1,0:T(8,128)(2,1)}, bf16[128,4096]{1,0:T(8,128)(2,1)}, u32[]{:S(2)}, u32[]{:S(2)}) collective-permute-start(bf16[128,4096]{1,0:T(8,128)(2,1)} %norm_rows.1.refs_3_), channel_id=1, source_target_pairs={{0,1},{1,2},{2,3},{3,0},{4,7},{5,4},{6,5},{7,6},{8,9},{9,10},{10,1... | collective-permute-start | bytes 3145736 | tf_op jit(solution)/shard_map/ppermute | solution.py:45
  80.2 24.5 %collective-permute-start.13 = (bf16[512,1024]{1,0:T(8,128)(2,1)S(1)}, bf16[512,1024]{1,0:T(8,128)(2,1)}, u32[]{:S(2)}, u32[]{:S(2)}) collective-permute-start(bf16[512,1024]{1,0:T(8,128)(2,1)S(1)} %collective-permute-done.8.refs_6_), channel_id=1, source_target_pairs={{0,8},{4,28},{8,16},{12,4},{16,24},{20,12},{24,0},{28,20},{32,40},... | collective-permute-start | bytes 3145736 | tf_op jit(solution)/shard_map/ppermute | solution.py:33
  80.8 24.0 %collective-permute-start.14 = (bf16[512,1024]{1,0:T(8,128)(2,1)S(1)}, bf16[512,1024]{1,0:T(8,128)(2,1)}, u32[]{:S(2)}, u32[]{:S(2)}) collective-permute-start(bf16[512,1024]{1,0:T(8,128)(2,1)S(1)} %constant_dynamic-update-slice_fusion.refs_5_), channel_id=1, source_target_pairs={{0,4},{4,0},{8,12},{12,8},{16,20},{20,16},{24,28},{28,24},{32,36},... | collective-permute-start | bytes 3145736 | tf_op jit(solution)/shard_map/ppermute | solution.py:33
  83.4 21.9 %collective-permute-start.15 = (bf16[512,1024]{1,0:T(8,128)(2,1)S(1)}, bf16[512,1024]{1,0:T(8,128)(2,1)}, u32[]{:S(2)}, u32[]{:S(2)}) collective-permute-start(bf16[512,1024]{1,0:T(8,128)(2,1)S(1)} %collective-permute-done.8.refs_6_), channel_id=1, source_target_pairs={{0,4},{4,0},{8,12},{12,8},{16,20},{20,16},{24,28},{28,24},{32,36},... | collective-permute-start | bytes 3145736 | tf_op jit(solution)/shard_map/ppermute | solution.py:33
  83.4 9.3 %collective-permute-start = (s32[2,6]{1,0:T(2,128)S(1)}, s32[2,6]{1,0:T(2,128)S(1)}, u32[]{:S(2)}, u32[]{:S(2)}) collective-permute-start(s32[2,6]{1,0:T(2,128)S(1)} %bitcast.101), channel_id=1, source_target_pairs={{0,1},{2,3},{4,5},{6,7},{8,9},{10,11},{12,13},{14,15},{16,17},{18,... | collective-permute-start | bytes 152 | tf_op jit(solution)/shard_map/ppermute | solution.py:378
  92.7 12.7 %collective-permute-start.16 = (bf16[512,1024]{1,0:T(8,128)(2,1)S(1)}, bf16[512,1024]{1,0:T(8,128)(2,1)}, u32[]{:S(2)}, u32[]{:S(2)}) collective-permute-start(bf16[512,1024]{1,0:T(8,128)(2,1)S(1)} %collective-permute-done.9.refs_7_), channel_id=1, source_target_pairs={{0,4},{4,0},{8,12},{12,8},{16,20},{20,16},{24,28},{28,24},{32,36},... | collective-permute-start | bytes 3145736 | tf_op jit(solution)/shard_map/ppermute | solution.py:33
  96.1 18.1 %collective-permute-start.18 = (bf16[512,1024]{1,0:T(8,128)(2,1)}, bf16[512,1024]{1,0:T(8,128)(2,1)}, u32[]{:S(2)}, u32[]{:S(2)}) collective-permute-start(bf16[512,1024]{1,0:T(8,128)(2,1)} %collective-permute-done.11.refs_14_), channel_id=1, source_target_pairs={{0,32},{4,100},{8,40},{12,108},{16,48},{20,116},{24,56},{28,124},{... | collective-permute-start | bytes 3145736 | tf_op jit(solution)/shard_map/ppermute | solution.py:33
  104.8 16.6 %collective-permute-start.20 = (bf16[512,1024]{1,0:T(8,128)(2,1)}, bf16[512,1024]{1,0:T(8,128)(2,1)}, u32[]{:S(2)}, u32[]{:S(2)}) collective-permute-start(bf16[512,1024]{1,0:T(8,128)(2,1)} %collective-permute-done.11.refs_14_), channel_id=1, source_target_pairs={{0,4},{4,0},{8,12},{12,8},{16,20},{20,16},{24,28},{28,24},{32,36},... | collective-permute-start | bytes 3145736 | tf_op jit(solution)/shard_map/ppermute | solution.py:33
  104.8 16.6 %collective-permute-start.21 = (bf16[512,1024]{1,0:T(8,128)(2,1)}, bf16[512,1024]{1,0:T(8,128)(2,1)}, u32[]{:S(2)}, u32[]{:S(2)}) collective-permute-start(bf16[512,1024]{1,0:T(8,128)(2,1)} %collective-permute-done.12.refs_15_), channel_id=1, source_target_pairs={{0,4},{4,0},{8,12},{12,8},{16,20},{20,16},{24,28},{28,24},{32,36},... | collective-permute-start | bytes 3145736 | tf_op jit(solution)/shard_map/ppermute | solution.py:33
  105.3 16.1 %collective-permute-start.19 = (bf16[512,1024]{1,0:T(8,128)(2,1)}, bf16[512,1024]{1,0:T(8,128)(2,1)}, u32[]{:S(2)}, u32[]{:S(2)}) collective-permute-start(bf16[512,1024]{1,0:T(8,128)(2,1)} %constant_dynamic-update-slice_fusion.4.refs_13_), channel_id=1, source_target_pairs={{0,4},{4,0},{8,12},{12,8},{16,20},{20,16},{24,28},{28,24},{32,36},... | collective-permute-start | bytes 3145736 | tf_op jit(solution)/shard_map/ppermute | solution.py:33
  105.4 16.0 %collective-permute-start.17 = (bf16[512,1024]{1,0:T(8,128)(2,1)}, bf16[512,1024]{1,0:T(8,128)(2,1)}, u32[]{:S(2)}, u32[]{:S(2)}) collective-permute-start(bf16[512,1024]{1,0:T(8,128)(2,1)} %collective-permute-done.13.refs_8_), channel_id=1, source_target_pairs={{0,4},{4,0},{8,12},{12,8},{16,20},{20,16},{24,28},{28,24},{32,36},... | collective-permute-start | bytes 3145736 | tf_op jit(solution)/shard_map/ppermute | solution.py:33
  139.6 15.8 %collective-permute-start.23 = (bf16[64,4096]{1,0:T(8,128)(2,1)}, bf16[64,4096]{1,0:T(8,128)(2,1)S(1)}, u32[]{:S(2)}, u32[]{:S(2)}) collective-permute-start(bf16[64,4096]{1,0:T(8,128)(2,1)} %get-tuple-element.48), channel_id=1, source_target_pairs={{0,1},{1,2},{2,3},{3,0},{4,7},{5,4},{6,5},{7,6},{8,9},{9,10},{10,1... | collective-permute-start | bytes 1572872 | tf_op jit(solution)/shard_map/ppermute | solution.py:45
  139.7 17.9 %collective-permute-start.25 = (bf16[64,4096]{1,0:T(8,128)(2,1)}, bf16[64,4096]{1,0:T(8,128)(2,1)S(1)}, u32[]{:S(2)}, u32[]{:S(2)}) collective-permute-start(bf16[64,4096]{1,0:T(8,128)(2,1)} %get-tuple-element.49), channel_id=1, source_target_pairs={{0,3},{1,0},{2,1},{3,2},{4,5},{5,6},{6,7},{7,4},{8,11},{9,8},{10,9... | collective-permute-start | bytes 1572872 | tf_op jit(solution)/shard_map/ppermute | solution.py:45
  156.6 10.6 %collective-permute-start.24 = (bf16[64,4096]{1,0:T(8,128)(2,1)S(1)}, bf16[64,4096]{1,0:T(8,128)(2,1)}, u32[]{:S(2)}, u32[]{:S(2)}) collective-permute-start(bf16[64,4096]{1,0:T(8,128)(2,1)S(1)} %add_convert_fusion.1), channel_id=1, source_target_pairs={{0,1},{1,2},{2,3},{3,0},{4,7},{5,4},{6,5},{7,6},{8,9},{9,10},{10,1... | collective-permute-start | bytes 1572872 | tf_op jit(solution)/shard_map/ppermute | solution.py:45
  170.1 12.9 %collective-permute-start.26 = (bf16[64,4096]{1,0:T(8,128)(2,1)}, bf16[64,4096]{1,0:T(8,128)(2,1)S(1)}, u32[]{:S(2)}, u32[]{:S(2)}) collective-permute-start(bf16[64,4096]{1,0:T(8,128)(2,1)} %get-tuple-element.51.refs_3_), channel_id=1, source_target_pairs={{0,1},{1,2},{2,3},{3,0},{4,7},{5,4},{6,5},{7,6},{8,9},{9,10},{10,1... | collective-permute-start | bytes 1572872 | tf_op jit(solution)/shard_map/ppermute | solution.py:45
  170.1 13.6 %collective-permute-start.27 = (bf16[64,4096]{1,0:T(8,128)(2,1)}, bf16[64,4096]{1,0:T(8,128)(2,1)S(1)}, u32[]{:S(2)}, u32[]{:S(2)}) collective-permute-start(bf16[64,4096]{1,0:T(8,128)(2,1)} %get-tuple-element.51.refs_3_), channel_id=1, source_target_pairs={{0,3},{1,0},{2,1},{3,2},{4,5},{5,6},{6,7},{7,4},{8,11},{9,8},{10,9... | collective-permute-start | bytes 1572872 | tf_op jit(solution)/shard_map/ppermute | solution.py:45
  182.9 10.4 %collective-permute-start.28 = (bf16[64,4096]{1,0:T(8,128)(2,1)S(1)}, bf16[64,4096]{1,0:T(8,128)(2,1)S(1)}, u32[]{:S(2)}, u32[]{:S(2)}) collective-permute-start(bf16[64,4096]{1,0:T(8,128)(2,1)S(1)} %collective-permute-done.26.refs_4_), channel_id=1, source_target_pairs={{0,1},{1,2},{2,3},{3,0},{4,7},{5,4},{6,5},{7,6},{8,9},{9,10},{10,1... | collective-permute-start | bytes 1572872 | tf_op jit(solution)/shard_map/ppermute | solution.py:45
  209.1 11.1 %collective-permute-start.29 = (bf16[64,4096]{1,0:T(8,128)(2,1)}, bf16[64,4096]{1,0:T(8,128)(2,1)S(1)}, u32[]{:S(2)}, u32[]{:S(2)}) collective-permute-start(bf16[64,4096]{1,0:T(8,128)(2,1)} %get-tuple-element.55), channel_id=1, source_target_pairs={{0,1},{1,2},{2,3},{3,0},{4,7},{5,4},{6,5},{7,6},{8,9},{9,10},{10,1... | collective-permute-start | bytes 1572872 | tf_op jit(solution)/shard_map/ppermute | solution.py:45
  209.1 13.2 %collective-permute-start.31 = (bf16[64,4096]{1,0:T(8,128)(2,1)}, bf16[64,4096]{1,0:T(8,128)(2,1)S(1)}, u32[]{:S(2)}, u32[]{:S(2)}) collective-permute-start(bf16[64,4096]{1,0:T(8,128)(2,1)} %get-tuple-element.56), channel_id=1, source_target_pairs={{0,3},{1,0},{2,1},{3,2},{4,5},{5,6},{6,7},{7,4},{8,11},{9,8},{10,9... | collective-permute-start | bytes 1572872 | tf_op jit(solution)/shard_map/ppermute | solution.py:45
  222.1 10.7 %collective-permute-start.30 = (bf16[64,4096]{1,0:T(8,128)(2,1)}, bf16[64,4096]{1,0:T(8,128)(2,1)}, u32[]{:S(2)}, u32[]{:S(2)}) collective-permute-start(bf16[64,4096]{1,0:T(8,128)(2,1)} %add_convert_fusion), channel_id=1, source_target_pairs={{0,1},{1,2},{2,3},{3,0},{4,7},{5,4},{6,5},{7,6},{8,9},{9,10},{10,1... | collective-permute-start | bytes 1572872 | tf_op jit(solution)/shard_map/ppermute | solution.py:45
  (15 other events, 443.1 us)
Sparse Core Ops, SparseCore 0:
  77.3 71.6 all-gather.2

commit v2 on v1

v2 whole, which is shorter than its diff:
```python
import functools

import jax
import jax.numpy as jnp
from jax import lax
from jax.experimental import pallas as pl
from jax.experimental.pallas import tpu as pltpu
from jax.sharding import PartitionSpec as P

HD = 128
HDD = 64
DMAX = 2
ZN, YN = 4, 4
SIDE = 4
BF = jnp.bfloat16
F32 = jnp.float32
EPS = 1e-05


def xswap(value, pairs):
    return lax.ppermute(value, ("segment", "frame"), pairs)


def xhop(value, sign):
    pairs = []
    for d in range(2 * ZN * YN):
        step = sign * (1 - 2 * (d % 2))
        pairs += [(d * SIDE + i, d * SIDE + (i + step) % SIDE) for i in range(SIDE)]
    return lax.ppermute(value, ("dp", "segment", "frame"), pairs)


def tied(values, after):
    return lax.optimization_barrier((values, after))[0]


def xhop2(value):
    return xswap(value, [(i, (i + 2) % SIDE) for i in range(SIDE)])


def vmem():
    return pl.BlockSpec(memory_space=pltpu.VMEM)


def smem():
    return pl.BlockSpec(memory_space=pltpu.SMEM)


def anywhere():
    return pl.BlockSpec(memory_space=pl.ANY)


def rms(values):
    scale = lax.rsqrt(jnp.mean(values * values, axis=-1, keepdims=True) + EPS)
    return (values * scale).astype(BF)


def norm_kernel(x_ref, o_ref):
    o_ref[...] = rms(x_ref[...].astype(F32))


def norm_rows(x):
    return pl.pallas_call(
        norm_kernel,
        out_shape=pltpu.HBM(x.shape, BF),
        in_specs=[vmem()],
        out_specs=vmem(),
        compiler_params=pltpu.CompilerParams(vmem_limit_bytes=8 * 2**20),
        name="norm_rows",
    )(x)


def summed(*refs):
    total = refs[0][...].astype(F32)
    for ref in refs[1:]:
        total = total + ref[...].astype(F32)
    return total.astype(BF)


def merge_kernel(x_ref, a_ref, b_ref, c_ref, d_ref, x_out, n_out):
    new = summed(x_ref, a_ref, b_ref, c_ref, d_ref)
    x_out[...] = new
    n_out[...] = rms(new.astype(F32))


def merge_rows(x, parts):
    return pl.pallas_call(
        merge_kernel,
        out_shape=[pltpu.HBM(x.shape, BF)] * 2,
        in_specs=[vmem()] * 5,
        out_specs=[vmem()] * 2,
        compiler_params=pltpu.CompilerParams(vmem_limit_bytes=8 * 2**20),
        name="merge_rows",
    )(x, *in_hbm(parts))


def in_hbm(arrays):
    return [pltpu.with_memory_space_constraint(a, pltpu.HBM) for a in arrays]


def load_kernel(*refs):
    n = len(refs) // 2
    copies = [pltpu.make_async_copy(refs[i], refs[n + i], refs[-1].at[i]) for i in range(n)]
    for copy in copies:
        copy.start()
    for copy in copies:
        copy.wait()


def load(arrays):
    return pl.pallas_call(
        load_kernel,
        out_shape=[pltpu.VMEM(a.shape, a.dtype) for a in arrays],
        in_specs=[anywhere()] * len(arrays),
        out_specs=[vmem()] * len(arrays),
        scratch_shapes=[pltpu.SemaphoreType.DMA((len(arrays),))],
        compiler_params=pltpu.CompilerParams(vmem_limit_bytes=4 * 2**20),
        cost_estimate=pl.CostEstimate(
            flops=0, bytes_accessed=2**24, transcendentals=0
        ),
        name="load",
    )(*in_hbm(arrays))


def softmax_rounded(scores):
    top = jnp.max(scores, axis=-1, keepdims=True)
    weights = jnp.exp(scores - top)
    return (weights / jnp.sum(weights, axis=-1, keepdims=True)).astype(BF)


NT = (((1,), (1,)), ((), ()))


PAIR = 768
HEADS = 4


def layer_kernel(place, cos_ref, sin_ref, *refs):
    *x_refs, w_ref = refs[: -SIDE - 6]
    outs = refs[-SIDE - 6 : -6]
    x_s, ctx_s, out_s, w_s, w_sem, o_sem = refs[-6:]
    groups = (pl.ds(0, PAIR), pl.ds(PAIR, PAIR), pl.ds(2 * PAIR, HEADS * HD))
    fetch = [
        pltpu.make_async_copy(w_ref.at[:, :, cut], w_s.at[:, :, cut], w_sem.at[i])
        for i, cut in enumerate(groups)
    ]
    for copy in fetch:
        copy.start()
    for i, ref in enumerate(x_refs):
        start = pl.multiple_of(place[i], 64)
        x_s[pl.ds(start, ref.shape[0])] = ref[...]
    rows, width = x_s.shape

    projected = []
    for half in range(2):
        fetch[half].wait()
        starts = [half * PAIR + 256 * i for i in range(3)]
        projected.append([
            jnp.dot(
                x_s[...], w_s[:, :, start : start + 256].reshape(width, 256),
                preferred_element_type=F32,
            )
            for start in starts
        ])
    fetch[2].wait()
    lower = lax.broadcasted_iota(jnp.int32, (rows, rows), 0) >= lax.broadcasted_iota(
        jnp.int32, (rows, rows), 1
    )
    cosine, sine = cos_ref[...], sin_ref[...]
    scale = 1.0 / jnp.sqrt(F32(HD))

    def turned(v):
        return (v * cosine + pltpu.roll(v, HD // 2, 1) * sine).astype(BF)

    for half, (q, k, v) in enumerate(projected):
        for head in range(2):
            cut = slice(head * HD, head * HD + HD)
            scores = lax.dot_general(
                turned(q[:, cut]), turned(k[:, cut]), NT, preferred_element_type=F32
            )
            weights = softmax_rounded(jnp.where(lower, scores * scale, -1e30))
            context = jnp.dot(weights, v[:, cut].astype(BF), preferred_element_type=F32)
            there = half * 256 + head * HD
            ctx_s[:, there : there + HD] = context.astype(BF)
    tile = 512
    for n in range(width // tile):
        chunks = slice(n * tile // 128, (n + 1) * tile // 128)
        total = lax.dot_general(
            ctx_s[...], w_s[chunks, :, 2 * PAIR :].reshape(tile, HEADS * HD), NT,
            preferred_element_type=F32,
        )
        out_s[:, n * tile : (n + 1) * tile] = total.astype(BF)
    copies = []
    for i, ref in enumerate(outs):
        start = pl.multiple_of(place[SIDE + i], 64)
        copies.append(pltpu.make_async_copy(out_s.at[pl.ds(start, 64)], ref, o_sem.at[i]))
        copies[-1].start()
    for copy in copies:
        copy.wait()


def layer(place, tables, blocks, weight):
    rows, width = sum(b.shape[0] for b in blocks), blocks[0].shape[1]
    return pl.pallas_call(
        layer_kernel,
        out_shape=[pltpu.HBM((64, width), BF)] * SIDE,
        in_specs=[smem()] + [vmem()] * (2 + len(blocks)) + [anywhere()],
        out_specs=[anywhere()] * SIDE,
        scratch_shapes=[
            pltpu.VMEM((rows, width), BF),
            pltpu.VMEM((rows, HEADS * HD), BF),
            pltpu.VMEM((rows, width), BF),
            pltpu.VMEM(weight.shape, BF),
            pltpu.SemaphoreType.DMA((3,)),
            pltpu.SemaphoreType.DMA((SIDE,)),
        ],
        compiler_params=pltpu.CompilerParams(vmem_limit_bytes=36 * 2**20),
        cost_estimate=pl.CostEstimate(
            flops=2 * rows * width * 2048, bytes_accessed=2**24, transcendentals=0
        ),
        name="layer",
    )(place, *tables, *in_hbm([*blocks, weight]))


TF = 16


def depth_kernel(x_ref, a_ref, b_ref, c_ref, d_ref, proj, dqkv, dout, logit, emb, target,
                 o_ref, u_s, qkv_s, ctx_s):
    new = summed(x_ref, a_ref, b_ref, c_ref, d_ref)
    normed = rms(new.astype(F32))
    depth_in = jnp.dot(normed, proj[...], preferred_element_type=F32).astype(BF)
    depth_in = depth_in.astype(F32)
    frames = x_ref.shape[0]
    streams = u_s.shape[0] // frames
    span = TF * streams
    for tile in range(frames // TF):
        base = depth_in[tile * TF : tile * TF + TF]
        for k in range(streams):
            cut = slice(tile * span + k * TF, tile * span + k * TF + TF)
            u_s[cut] = base + emb[cut].astype(F32)
    inputs = rms(u_s[...])
    for i in range(3):
        qkv_s[i] = jnp.dot(inputs, dqkv[i], preferred_element_type=F32).astype(BF)
    r = lax.broadcasted_iota(jnp.int32, (span, span), 0)
    q = lax.broadcasted_iota(jnp.int32, (span, span), 1)
    seen = ((r & (TF - 1)) == (q & (TF - 1))) & (r >= q)
    head_width = dout.shape[0]
    heads = head_width // HDD
    head = lax.broadcasted_iota(jnp.int32, (span, head_width), 1) // HDD
    seen = jnp.broadcast_to(seen[None], (heads, span, span)).reshape(heads * span, span)
    for tile in range(frames // TF):
        rows = slice(tile * span, tile * span + span)
        queries, keys, values = (qkv_s[i, rows] for i in range(3))
        queries = jnp.concatenate(
            [jnp.where(head == h, queries, jnp.zeros_like(queries)) for h in range(heads)]
        )
        scores = lax.dot_general(queries, keys, NT, preferred_element_type=F32)
        weights = softmax_rounded(jnp.where(seen, scores * HDD**-0.5, -1e30))
        context = jnp.dot(weights, values, preferred_element_type=F32)
        picked = context[:span]
        for h in range(1, heads):
            picked = jnp.where(head == h, context[h * span : (h + 1) * span], picked)
        ctx_s[rows] = picked.astype(BF)
    mixed = u_s[...] + jnp.dot(ctx_s[...], dout[...], preferred_element_type=F32)
    logits = jnp.dot(rms(mixed), logit[...], preferred_element_type=F32)
    top = jnp.max(logits, axis=-1, keepdims=True)
    total = jnp.sum(jnp.exp(logits - top), axis=-1, keepdims=True)
    entry = lax.broadcasted_iota(jnp.int32, logits.shape, 1)
    picked = jnp.sum(jnp.where(entry == target[...], logits, 0.0), axis=-1, keepdims=True)
    o_ref[...] = jnp.log(total) + top - picked


def depth(x, parts, proj, dqkv, dout, logit, emb, target):
    count, width = emb.shape
    head_width = dout.shape[0]
    return pl.pallas_call(
        depth_kernel,
        out_shape=jax.ShapeDtypeStruct((count, 1), F32),
        in_specs=[vmem()] * 11,
        out_specs=vmem(),
        scratch_shapes=[
            pltpu.VMEM((count, width), F32),
            pltpu.VMEM((3, count, head_width), BF),
            pltpu.VMEM((count, head_width), BF),
        ],
        compiler_params=pltpu.CompilerParams(vmem_limit_bytes=16 * 2**20),
        cost_estimate=pl.CostEstimate(
            flops=2 * count * width * 5120, bytes_accessed=2**22, transcendentals=0
        ),
        name="depth",
    )(x, *in_hbm(parts), proj, dqkv, dout, logit, emb, target)


def rope_tables(rows):
    half = HD // 2
    frequency = 10000.0 ** (-jnp.arange(half, dtype=F32) / half)
    angles = jnp.arange(rows).astype(F32)[:, None] * frequency[None, :]
    cosine, sine = jnp.cos(angles), jnp.sin(angles)
    return (
        jnp.concatenate([cosine, cosine], axis=1),
        jnp.concatenate([-sine, sine], axis=1),
    )


def packed_weights(qkv_weight, out_weight):
    w = jnp.transpose(qkv_weight[0], (1, 0, 2))
    o = out_weight[0]
    halves = []
    for i in range(2):
        cuts = [slice(512 * i + 256 * j, 512 * i + 256 * j + 256) for j in range(2)]
        parts = [w[k][:, cut] for cut in cuts for k in range(3)]
        halves.append(jnp.concatenate([*parts, o[512 * i : 512 * i + 512].T], axis=1))
    return jnp.stack(halves)


def local(
    frames_in, qkv_weight, out_weight, proj_weight, depth_qkv, depth_out, code_table,
    logit_weight, given_codes, given_delays,
):
    s = lax.axis_index("segment")
    f = lax.axis_index("frame")
    d = lax.axis_index("dp")
    row_count = frames_in.shape[1]
    part = row_count // 2
    streams = given_codes.shape[2]
    me = s * 2 + f

    def rows_of(i):
        i = i % SIDE
        return (i % 2) * row_count + (i // 2) * part

    sign = 1 - 2 * (d % 2)

    def place_of(starts):
        starts = (list(starts) + [0] * SIDE)[:SIDE]
        targets = [rows_of(me + k * sign + 4) for k in (0, 1, -1, 2)]
        return jnp.stack([*starts, *targets]).astype(jnp.int32)

    packed = packed_weights(qkv_weight, out_weight)
    kept = lax.dynamic_index_in_dim(packed, s, 0, keepdims=False)
    given = lax.dynamic_index_in_dim(packed, 1 - s, 0, keepdims=False)
    got = xswap(given, [(0, 3), (3, 0), (1, 2), (2, 1)])
    first = jnp.where(s == 0, kept, got)
    second = jnp.where(s == 0, got, kept)
    w0 = lax.all_gather(first, "dp")
    frames = frames_in[0]
    normed = norm_rows(frames)
    far = xhop(tied(normed, got), 1)

    given_tail = lax.ppermute(given_codes[0, row_count - DMAX :], "frame", [(0, 1)])

    def prepare(after):
        codes, delays = tied((given_codes, given_delays), after)
        tail = tied(given_tail, after)
        extended = jnp.concatenate([tail, codes[0]], axis=0)
        extended = lax.dynamic_slice_in_dim(extended, s * part, part + DMAX, 0)
        targets = extended[DMAX : DMAX + part]
        for lag in range(1, DMAX + 1):
            targets = jnp.where(
                delays[None, :] == lag, extended[DMAX - lag : DMAX - lag + part], targets
            )
        frame = rows_of(me) + jnp.arange(part, dtype=jnp.int32)
        is_valid = frame[:, None] >= delays[None, :]
        targets = jnp.clip(targets, 0, code_table.shape[0] - 1)

        def tiled(a):
            return jnp.transpose(a.reshape(part // TF, TF, streams), (0, 2, 1)).reshape(-1)

        def behind(a):
            return jnp.concatenate([jnp.zeros_like(a[:, :1]), a[:, :-1]], axis=1)

        emb = jnp.take(code_table, tiled(behind(targets)), axis=0, mode="clip")
        emb = jnp.where(tiled(behind(is_valid))[:, None], emb, jnp.zeros_like(emb))
        return emb, tiled(targets)[:, None], is_valid, rope_tables(2 * row_count)

    emb, target, is_valid, tables = prepare(far)
    w0, far, emb, target, tables, second = lax.optimization_barrier(
        (w0, far, emb, target, tables, second)
    )
    w1 = lax.all_gather(second, "dp")
    place0 = place_of([f * row_count, (1 - f) * row_count])
    sent = layer(place0, tables, [normed, far], w0)

    def spread(block):
        return [block, xhop(block, 1), xhop(block, -1), xhop2(block)]

    def scattered(sent):
        return [sent[0], xhop(sent[1], 1), xhop(sent[2], -1), xhop2(sent[3])]

    mine = lax.dynamic_slice_in_dim(frames, s * part, part, 0)
    x1, n1 = merge_rows(mine, scattered(sent))
    starts = [rows_of(me + k * sign + 4) for k in (0, -1, 1, 2)]
    sent = layer(place_of(starts), tables, spread(n1), w1)

    ready = [proj_weight, jnp.transpose(depth_qkv, (1, 0, 2)), depth_out, logit_weight]
    ready = load(tied(ready, sent))
    losses = depth(x1, scattered(sent), *ready, emb, target)
    losses = jnp.transpose(losses.reshape(part // TF, streams, TF), (0, 2, 1))
    losses = jnp.where(is_valid, losses.reshape(part, streams), 0.0)
    other = xhop2(losses)
    both = jnp.where(s == 0, jnp.stack([losses, other]), jnp.stack([other, losses]))
    return both.reshape(1, row_count, streams)


def solution(mesh):
    return jax.shard_map(
        local,
        mesh=mesh,
        in_specs=(
            P("dp", "frame", None),
            P("segment", "dp", None, "frame"),
            P("segment", "frame", "dp"),
            P(),
            P(),
            P(),
            P(),
            P(),
            P("dp", "frame", None),
            P(),
        ),
        out_specs=P("dp", "frame", None),
        check_vma=False,
    )
```

time: 269 us -> 239 us (0.89)
  Pallas kernels: 60.1 us -> 46.7 us
  starting transfers between devices: 32.8 us -> 21.4 us
  local copies, waits for them, and re-layouts: 17.7 us -> 10.3 us
  waiting for transfers between devices: 138 us -> 143 us
  other arithmetic: 6.23 us -> 2.75 us
    ppermute x21 -> x1, waiting for transfers between devices: 58 us -> 0.01 us  [local(): lax.ppermute(given_codes[0, row_count - DMAX:], 'frame', [(0, 1)])]
    all_gather x1 -> x2, waiting for transfers between devices: 0.01 us -> 53.7 us  [the longest x1 50.8 us: local(): w0 = lax.all_gather(first, 'dp')]
    ppermute x21 -> x1, starting transfers between devices: 19.7 us -> 3.39 us  [local(): lax.ppermute(given_codes[0, row_count - DMAX:], 'frame', [(0, 1)])]
    pallas_call x1, Pallas kernels: 21.5 us -> 10.1 us  [depth(): pl.pallas_call(depth_kernel, out_shape=jax.ShapeDtypeStruct((count, 1), F...]
    ppermute x10 -> x7, waiting for transfers between devices: 63.1 us -> 71.6 us  [xhop(): return lax.ppermute(value, ('dp', 'segment', 'frame'), pairs)]
    unnamed x36 -> x33, local copies, waits for them, and re-layouts: 6.05 us -> 0.43 us
    ppermute x2 -> x5, starting transfers between devices: 2.92 us -> 7.36 us  [xswap(): return lax.ppermute(value, ('segment', 'frame'), pairs)]
    convert_element_type x2 -> x0, other arithmetic: 3.12 us -> none  [scattered(): relayed = (sent[1].astype(F32) + relayed.astype(F32)).astype(BF)]
  transfers between devices with their start and end apart: 34 -> 15, of which waited for: 17 -> 11; matrix products, arithmetic and copies ran while one was open for 6% -> 3% of each run, Pallas kernels for 9% -> 10%
where the time goes in v2:
time: 239 us; the launch traced here: 238 us
  waiting for transfers between devices  143 us (60%)
  Pallas kernels  46.7 us (20%)
  starting transfers between devices  21.4 us (9%)
  between operations  13.9 us (6%)
  local copies, waits for them, and re-layouts  10.3 us (4%)
  other arithmetic  2.75 us (1%)
    ppermute x7, waiting for transfers between devices, xhop(): return lax.ppermute(value, ('dp', 'segment', 'frame'), pairs)  71.6 us
    all_gather x1, waiting for transfers between devices, local(): w0 = lax.all_gather(first, 'dp')  50.8 us
    pallas_call x2, Pallas kernels, layer(): pl.pallas_call(layer_kernel, out_shape=[pltpu.HBM((64, width), BF)] * SID...  26.2 us
    ppermute x5, waiting for transfers between devices, xswap(): return lax.ppermute(value, ('segment', 'frame'), pairs)  17.7 us
    ppermute x7, starting transfers between devices, xhop(): return lax.ppermute(value, ('dp', 'segment', 'frame'), pairs)  10.6 us
    pallas_call x1, Pallas kernels, depth(): pl.pallas_call(depth_kernel, out_shape=jax.ShapeDtypeStruct((count, 1), F...  10.1 us
    ppermute x5, starting transfers between devices, xswap(): return lax.ppermute(value, ('segment', 'frame'), pairs)  7.36 us
    pallas_call x1, Pallas kernels, load(): pl.pallas_call(load_kernel, out_shape=[pltpu.VMEM(a.shape, a.dtype) for a...  5.86 us
  transfers between devices with their start and end apart: 15, of which 11 were waited for; matrix products, arithmetic and copies ran while one was open for 3% of the time, Pallas kernels for 10%

profile of v2, /device:TPU:0, one launch (start us, length us, event | category | flops | bytes accessed | tf_op | source)
XLA Modules:
  0.0 238.2 jit_solution(4023910680680694072)
XLA Ops:
  6.5 1.2 slice_bitcast_fusion
  7.7 1.1 fusion.6
  9.4 2.9 %collective-permute-start = (bf16[128,2048]{1,0:T(8,128)(2,1)S(1)}, bf16[128,2048]{1,0:T(8,128)(2,1)S(1)}, u32[]{:S(2)}, u32[]{:S(2)}) collective-permute-start(bf16[128,2048]{1,0:T(8,128)(2,1)S(1)} %fusion.3), channel_id=1, source_target_pairs={{0,3},{3,0},{1,2},{2,1},{4,7},{7,4},{5,6},{6,5},{8,11},{11,8},{9,1... | collective-permute-start | bytes 1572872 | tf_op jit(solution)/shard_map/ppermute | solution.py:21
  12.3 11.9 %collective-permute-done = bf16[128,2048]{1,0:T(8,128)(2,1)S(1)} collective-permute-done((bf16[128,2048]{1,0:T(8,128)(2,1)S(1)}, bf16[128,2048]{1,0:T(8,128)(2,1)S(1)}, u32[]{:S(2)}, u32[]{:S(2)}) %collective-permute-start) | collective-permute-done | bytes 524320 | tf_op jit(solution)/shard_map/ppermute | solution.py:21
  24.3 1.2 broadcast_select_fusion.1
  25.5 1.4 norm_rows.1.refs_0_
  27.6 3.4 %collective-permute-start.2 = (s32[2,6]{1,0:T(2,128)S(1)}, s32[2,6]{1,0:T(2,128)S(1)}, u32[]{:S(2)}, u32[]{:S(2)}) collective-permute-start(s32[2,6]{1,0:T(2,128)S(1)} %bitcast.85), channel_id=1, source_target_pairs={{0,1},{2,3},{4,5},{6,7},{8,9},{10,11},{12,13},{14,15},{16,17},{18,... | collective-permute-start | bytes 152 | tf_op jit(solution)/shard_map/ppermute | solution.py:350
  31.8 11.4 %collective-permute-done.1.refs_1_ = bf16[128,4096]{1,0:T(8,128)(2,1)S(1)} collective-permute-done((bf16[128,4096]{1,0:T(8,128)(2,1)}, bf16[128,4096]{1,0:T(8,128)(2,1)S(1)}, u32[]{:S(2)}, u32[]{:S(2)}) %collective-permute-start.1) | collective-permute-done | bytes 1048608 | tf_op jit(solution)/shard_map/ppermute | solution.py:29
  44.2 5.6 %gather_fusion = bf16[384,1024]{1,0:T(8,128)(2,1)S(1)} fusion(bf16[2048,1024]{1,0:T(8,128)(2,1)} %param.16, s32[1024]{0:T(1024)S(1)} %pad_clamp_fusion), kind=kCustom, calls=%fused_computation | custom fusion | bytes 1574400 | tf_op jit(solution)/shard_map/jit(_take)/gather | solution.py:372
  49.9 50.8 %all-gather.5.cloned.1.call-done = bf16[4096,2048]{1,0:T(8,128)(2,1)} async-done(((bf16[128,2048]{1,0:T(8,128)(2,1)}), bf16[4096,2048]{1,0:T(8,128)(2,1)}) %all-gather.5.cloned.1.call-update) | async-done | bytes 16777232 | tf_op jit(solution)/shard_map/all_gather | solution.py:345
  101.0 13.1 %layer.2 = (bf16[64,4096]{1,0:T(8,128)(2,1)}, bf16[64,4096]{1,0:T(8,128)(2,1)}, bf16[64,4096]{1,0:T(8,128)(2,1)}, bf16[64,4096]{1,0:T(8,128)(2,1)}) custom-call(s32[8]{0:T(128)S(1)} %stack.62.place, f32[256,128]{1,0:T(8,128)S(1)} %get-tuple-element.38.cos_ref, f32[256,128]{1,0:T(8,128)S(1)} %get-tuple-element.39.sin_ref, ...), custom_call_target="tpu_custom_call" | custom-call | flops 4294967296 | bytes 16777216 | tf_op jit(solution)/shard_map/layer/pallas_call | solution.py:203
  114.1 1.5 collective-permute-start.3
  115.7 1.8 collective-permute-start.4
  117.4 1.8 collective-permute-start.5
  119.3 9.4 %collective-permute-done.3.b_ref = bf16[64,4096]{1,0:T(8,128)(2,1)S(1)} collective-permute-done((bf16[64,4096]{1,0:T(8,128)(2,1)}, bf16[64,4096]{1,0:T(8,128)(2,1)S(1)}, u32[]{:S(2)}, u32[]{:S(2)}) %collective-permute-start.3) | collective-permute-done | bytes 524320 | tf_op jit(solution)/shard_map/ppermute | solution.py:29
  128.7 11.4 %collective-permute-done.4.c_ref = bf16[64,4096]{1,0:T(8,128)(2,1)S(1)} collective-permute-done((bf16[64,4096]{1,0:T(8,128)(2,1)}, bf16[64,4096]{1,0:T(8,128)(2,1)S(1)}, u32[]{:S(2)}, u32[]{:S(2)}) %collective-permute-start.4) | collective-permute-done | bytes 524320 | tf_op jit(solution)/shard_map/ppermute | solution.py:29
  140.1 2.5 %collective-permute-done.5.d_ref = bf16[64,4096]{1,0:T(8,128)(2,1)} collective-permute-done((bf16[64,4096]{1,0:T(8,128)(2,1)}, bf16[64,4096]{1,0:T(8,128)(2,1)}, u32[]{:S(2)}, u32[]{:S(2)}) %collective-permute-start.5) | collective-permute-done | bytes 524320 | tf_op jit(solution)/shard_map/ppermute | solution.py:21
  142.6 3.1 %merge_rows.1 = (bf16[64,4096]{1,0:T(8,128)(2,1)}, bf16[64,4096]{1,0:T(8,128)(2,1)}) custom-call(bf16[64,4096]{1,0:T(8,128)(2,1)S(1)} %dynamic-slice_bitcast_fusion.x_ref, bf16[64,4096]{1,0:T(8,128)(2,1)} %get-tuple-element.42.a_ref, bf16[64,4096]{1,0:T(8,128)(2,1)} %copy-done.5, bf16[64,4096]{1,0:T(8,128)(2,1)} %copy-done.8, ...), custom_call_target="tpu_custom_call" | custom-call | tf_op jit(solution)/shard_map/merge_rows/pallas_call | solution.py:86
  145.7 3.2 %collective-permute-start.7 = (bf16[64,4096]{1,0:T(8,128)(2,1)}, bf16[64,4096]{1,0:T(8,128)(2,1)S(1)}, u32[]{:S(2)}, u32[]{:S(2)}) collective-permute-start(bf16[64,4096]{1,0:T(8,128)(2,1)} %get-tuple-element.47.refs_0_), channel_id=1, source_target_pairs={{0,3},{1,0},{2,1},{3,2},{4,5},{5,6},{6,7},{7,4},{8,11},{9,8},{10,9... | collective-permute-start | bytes 1572872 | tf_op jit(solution)/shard_map/ppermute | solution.py:29
  149.0 23.0 %collective-permute-done.6.refs_1_ = bf16[64,4096]{1,0:T(8,128)(2,1)S(1)} collective-permute-done((bf16[64,4096]{1,0:T(8,128)(2,1)}, bf16[64,4096]{1,0:T(8,128)(2,1)S(1)}, u32[]{:S(2)}, u32[]{:S(2)}) %collective-permute-start.6) | collective-permute-done | bytes 524320 | tf_op jit(solution)/shard_map/ppermute | solution.py:29
  172.0 3.0 %all-gather.7.cloned.1.call-done = bf16[4096,2048]{1,0:T(8,128)(2,1)} async-done(((bf16[128,2048]{1,0:T(8,128)(2,1)}), bf16[4096,2048]{1,0:T(8,128)(2,1)}) %all-gather.7.cloned.1.call-update) | async-done | bytes 16777232 | tf_op jit(solution)/shard_map/all_gather | solution.py:380
  175.0 13.1 %layer.3 = (bf16[64,4096]{1,0:T(8,128)(2,1)}, bf16[64,4096]{1,0:T(8,128)(2,1)}, bf16[64,4096]{1,0:T(8,128)(2,1)}, bf16[64,4096]{1,0:T(8,128)(2,1)}) custom-call(s32[8]{0:T(128)S(1)} %stack.63.place, f32[256,128]{1,0:T(8,128)S(1)} %get-tuple-element.38.cos_ref, f32[256,128]{1,0:T(8,128)S(1)} %get-tuple-element.39.sin_ref, ...), custom_call_target="tpu_custom_call" | custom-call | flops 4294967296 | bytes 16777216 | tf_op jit(solution)/shard_map/layer/pallas_call | solution.py:203
  188.1 2.8 %collective-permute-start.10 = (bf16[64,4096]{1,0:T(8,128)(2,1)}, bf16[64,4096]{1,0:T(8,128)(2,1)S(1)}, u32[]{:S(2)}, u32[]{:S(2)}) collective-permute-start(bf16[64,4096]{1,0:T(8,128)(2,1)} %get-tuple-element.51), channel_id=1, source_target_pairs={{0,3},{1,0},{2,1},{3,2},{4,5},{5,6},{6,7},{7,4},{8,11},{9,8},{10,9... | collective-permute-start | bytes 1572872 | tf_op jit(solution)/shard_map/ppermute | solution.py:29
  190.8 0.9 collective-permute-start.11
  191.7 0.9 collective-permute-start.9
  192.7 5.9 %load.1 = (bf16[4096,1024]{1,0:T(8,128)(2,1)S(1)}, bf16[3,1024,512]{2,1,0:T(8,128)(2,1)S(1)}, bf16[512,1024]{1,0:T(8,128)(2,1)S(1)}, bf16[1024,2048]{1,0:T(8,128)(2,1)S(1)}) custom-call(bf16[4096,1024]{1,0:T(8,128)(2,1)} %refs_0_, bf16[3,1024,512]{2,1,0:T(8,128)(2,1)} %bitcast.71, bf16[512,1024]{1,0:T(8,128)(2,1)} %refs_2_, bf16[1024,2048]{1,0:T(8,128)(2,1)} %refs_3_), custom_call_target="tpu_custom_call" | custom-call | bytes 16777216 | tf_op jit(solution)/shard_map/load/pallas_call | solution.py:110
  198.6 15.0 %collective-permute-done.10.c_ref = bf16[64,4096]{1,0:T(8,128)(2,1)S(1)} collective-permute-done((bf16[64,4096]{1,0:T(8,128)(2,1)}, bf16[64,4096]{1,0:T(8,128)(2,1)S(1)}, u32[]{:S(2)}, u32[]{:S(2)}) %collective-permute-start.10) | collective-permute-done | bytes 524320 | tf_op jit(solution)/shard_map/ppermute | solution.py:29
  213.6 1.4 collective-permute-done.9.b_ref
  215.0 10.1 %depth.1 = f32[384,1]{1,0:T(8,128)S(1)} custom-call(bf16[64,4096]{1,0:T(8,128)(2,1)S(1)} %copy-done.1, bf16[64,4096]{1,0:T(8,128)(2,1)} %get-tuple-element.49.a_ref, bf16[64,4096]{1,0:T(8,128)(2,1)} %collective-permute-done.9.b_ref, bf16[64,4096]{1,0:T(8,128)(2,1)} %copy-done.4, bf16[64,4096]{1,0:T(8,128)(2,1)} %copy-done.7, ...), custom_call_target="tpu_custom_call" | custom-call | flops 4026531840 | bytes 4194304 | tf_op jit(solution)/shard_map/depth/pallas_call | solution.py:276
  225.6 1.8 collective-permute-start.12
  227.4 3.3 %collective-permute-done.12 = f32[64,6]{0,1:T(8,128)S(1)} collective-permute-done((f32[64,6]{0,1:T(8,128)S(1)}, f32[64,6]{0,1:T(8,128)S(1)}, u32[]{:S(2)}, u32[]{:S(2)}) %collective-permute-start.12) | collective-permute-done | bytes 1568 | tf_op jit(solution)/shard_map/ppermute | solution.py:21
  230.7 0.7 select_n.201
  (85 shorter events, 4.0 us)
Async XLA Ops:
  6.5 94.1 %all-gather.5.cloned.1.call-start = ((), (), s32[]{:S(2)}) async-start(), calls=%async_computation | async-start | bytes 17301504 | tf_op jit(solution)/shard_map/all_gather | solution.py:345
  7.7 17.8 %copy-start = (bf16[1,128,4096]{2,1,0:T(8,128)(2,1)S(1)}, bf16[1,128,4096]{2,1,0:T(8,128)(2,1)}, u32[]{:S(2)}) copy-start(bf16[1,128,4096]{2,1,0:T(8,128)(2,1)} %param.10) | copy-start | bytes 3145732
  9.1 18.4 %copy-start.10 = (s32[1,128,6]{1,0,2:T(1,128)S(1)}, s32[1,128,6]{1,0,2:T(1,128)}, u32[]{:S(2)}) copy-start(s32[1,128,6]{1,0,2:T(1,128)} %param.18) | copy-start | bytes 9220
  9.2 34.0 %copy-start.11 = (s32[6]{0:T(128)S(1)}, s32[6]{0:T(128)}, u32[]{:S(2)}) copy-start(s32[6]{0:T(128)} %param.19) | copy-start | bytes 76
  9.4 14.8 %collective-permute-start = (bf16[128,2048]{1,0:T(8,128)(2,1)S(1)}, bf16[128,2048]{1,0:T(8,128)(2,1)S(1)}, u32[]{:S(2)}, u32[]{:S(2)}) collective-permute-start(bf16[128,2048]{1,0:T(8,128)(2,1)S(1)} %fusion.3), channel_id=1, source_target_pairs={{0,3},{3,0},{1,2},{2,1},{4,7},{7,4},{5,6},{6,5},{8,11},{11,8},{9,1... | collective-permute-start | bytes 1572872 | tf_op jit(solution)/shard_map/ppermute | solution.py:21
  25.5 149.5 %all-gather.7.cloned.1.call-start = ((), (), s32[]{:S(2)}) async-start(), calls=%async_computation.1 | async-start | bytes 17301504 | tf_op jit(solution)/shard_map/all_gather | solution.py:380
  27.0 16.2 %collective-permute-start.1 = (bf16[128,4096]{1,0:T(8,128)(2,1)}, bf16[128,4096]{1,0:T(8,128)(2,1)S(1)}, u32[]{:S(2)}, u32[]{:S(2)}) collective-permute-start(bf16[128,4096]{1,0:T(8,128)(2,1)} %norm_rows.1.refs_0_), channel_id=1, source_target_pairs={{0,1},{1,2},{2,3},{3,0},{4,7},{5,4},{6,5},{7,6},{8,9},{9,10},{10,1... | collective-permute-start | bytes 3145736 | tf_op jit(solution)/shard_map/ppermute | solution.py:29
  27.6 15.9 %collective-permute-start.2 = (s32[2,6]{1,0:T(2,128)S(1)}, s32[2,6]{1,0:T(2,128)S(1)}, u32[]{:S(2)}, u32[]{:S(2)}) collective-permute-start(s32[2,6]{1,0:T(2,128)S(1)} %bitcast.85), channel_id=1, source_target_pairs={{0,1},{2,3},{4,5},{6,7},{8,9},{10,11},{12,13},{14,15},{16,17},{18,... | collective-permute-start | bytes 152 | tf_op jit(solution)/shard_map/ppermute | solution.py:350
  43.2 1.0 copy-start.2
  114.1 14.5 %collective-permute-start.3 = (bf16[64,4096]{1,0:T(8,128)(2,1)}, bf16[64,4096]{1,0:T(8,128)(2,1)S(1)}, u32[]{:S(2)}, u32[]{:S(2)}) collective-permute-start(bf16[64,4096]{1,0:T(8,128)(2,1)} %get-tuple-element.43), channel_id=1, source_target_pairs={{0,1},{1,2},{2,3},{3,0},{4,7},{5,4},{6,5},{7,6},{8,9},{9,10},{10,1... | collective-permute-start | bytes 1572872 | tf_op jit(solution)/shard_map/ppermute | solution.py:29
  115.7 24.4 %collective-permute-start.4 = (bf16[64,4096]{1,0:T(8,128)(2,1)}, bf16[64,4096]{1,0:T(8,128)(2,1)S(1)}, u32[]{:S(2)}, u32[]{:S(2)}) collective-permute-start(bf16[64,4096]{1,0:T(8,128)(2,1)} %get-tuple-element.44), channel_id=1, source_target_pairs={{0,3},{1,0},{2,1},{3,2},{4,5},{5,6},{6,7},{7,4},{8,11},{9,8},{10,9... | collective-permute-start | bytes 1572872 | tf_op jit(solution)/shard_map/ppermute | solution.py:29
  117.4 25.1 %collective-permute-start.5 = (bf16[64,4096]{1,0:T(8,128)(2,1)}, bf16[64,4096]{1,0:T(8,128)(2,1)}, u32[]{:S(2)}, u32[]{:S(2)}) collective-permute-start(bf16[64,4096]{1,0:T(8,128)(2,1)} %get-tuple-element.45), channel_id=1, source_target_pairs={{0,2},{1,3},{2,0},{3,1},{4,6},{5,7},{6,4},{7,5},{8,10},{9,11},{10,... | collective-permute-start | bytes 1572872 | tf_op jit(solution)/shard_map/ppermute | solution.py:21
  128.7 13.9 %copy-start.5 = (bf16[64,4096]{1,0:T(8,128)(2,1)}, bf16[64,4096]{1,0:T(8,128)(2,1)S(1)}, u32[]{:S(2)}) copy-start(bf16[64,4096]{1,0:T(8,128)(2,1)S(1)} %collective-permute-done.3.b_ref) | copy-start | bytes 1572868
  140.1 2.5 %copy-start.8 = (bf16[64,4096]{1,0:T(8,128)(2,1)}, bf16[64,4096]{1,0:T(8,128)(2,1)S(1)}, u32[]{:S(2)}) copy-start(bf16[64,4096]{1,0:T(8,128)(2,1)S(1)} %collective-permute-done.4.c_ref) | copy-start | bytes 1572868
  145.7 26.3 %collective-permute-start.6 = (bf16[64,4096]{1,0:T(8,128)(2,1)}, bf16[64,4096]{1,0:T(8,128)(2,1)S(1)}, u32[]{:S(2)}, u32[]{:S(2)}) collective-permute-start(bf16[64,4096]{1,0:T(8,128)(2,1)} %get-tuple-element.47.refs_0_), channel_id=1, source_target_pairs={{0,1},{1,2},{2,3},{3,0},{4,7},{5,4},{6,5},{7,6},{8,9},{9,10},{10,1... | collective-permute-start | bytes 1572872 | tf_op jit(solution)/shard_map/ppermute | solution.py:29
  145.7 26.3 %collective-permute-start.7 = (bf16[64,4096]{1,0:T(8,128)(2,1)}, bf16[64,4096]{1,0:T(8,128)(2,1)S(1)}, u32[]{:S(2)}, u32[]{:S(2)}) collective-permute-start(bf16[64,4096]{1,0:T(8,128)(2,1)} %get-tuple-element.47.refs_0_), channel_id=1, source_target_pairs={{0,3},{1,0},{2,1},{3,2},{4,5},{5,6},{6,7},{7,4},{8,11},{9,8},{10,9... | collective-permute-start | bytes 1572872 | tf_op jit(solution)/shard_map/ppermute | solution.py:29
  148.9 23.1 %collective-permute-start.8 = (bf16[64,4096]{1,0:T(8,128)(2,1)}, bf16[64,4096]{1,0:T(8,128)(2,1)S(1)}, u32[]{:S(2)}, u32[]{:S(2)}) collective-permute-start(bf16[64,4096]{1,0:T(8,128)(2,1)} %get-tuple-element.47.refs_0_), channel_id=1, source_target_pairs={{0,2},{1,3},{2,0},{3,1},{4,6},{5,7},{6,4},{7,5},{8,10},{9,11},{10,... | collective-permute-start | bytes 1572872 | tf_op jit(solution)/shard_map/ppermute | solution.py:21
  172.0 3.0 %copy-start.3 = (bf16[64,4096]{1,0:T(8,128)(2,1)}, bf16[64,4096]{1,0:T(8,128)(2,1)S(1)}, u32[]{:S(2)}) copy-start(bf16[64,4096]{1,0:T(8,128)(2,1)S(1)} %collective-permute-done.6.refs_1_) | copy-start | bytes 1572868
  172.0 3.0 %copy-start.6 = (bf16[64,4096]{1,0:T(8,128)(2,1)}, bf16[64,4096]{1,0:T(8,128)(2,1)S(1)}, u32[]{:S(2)}) copy-start(bf16[64,4096]{1,0:T(8,128)(2,1)S(1)} %collective-permute-done.7.refs_2_) | copy-start | bytes 1572868
  172.0 3.0 %copy-start.9 = (bf16[64,4096]{1,0:T(8,128)(2,1)}, bf16[64,4096]{1,0:T(8,128)(2,1)S(1)}, u32[]{:S(2)}) copy-start(bf16[64,4096]{1,0:T(8,128)(2,1)S(1)} %collective-permute-done.8.refs_3_) | copy-start | bytes 1572868
  188.1 25.5 %collective-permute-start.10 = (bf16[64,4096]{1,0:T(8,128)(2,1)}, bf16[64,4096]{1,0:T(8,128)(2,1)S(1)}, u32[]{:S(2)}, u32[]{:S(2)}) collective-permute-start(bf16[64,4096]{1,0:T(8,128)(2,1)} %get-tuple-element.51), channel_id=1, source_target_pairs={{0,3},{1,0},{2,1},{3,2},{4,5},{5,6},{6,7},{7,4},{8,11},{9,8},{10,9... | collective-permute-start | bytes 1572872 | tf_op jit(solution)/shard_map/ppermute | solution.py:29
  190.8 22.8 %collective-permute-start.11 = (bf16[64,4096]{1,0:T(8,128)(2,1)}, bf16[64,4096]{1,0:T(8,128)(2,1)S(1)}, u32[]{:S(2)}, u32[]{:S(2)}) collective-permute-start(bf16[64,4096]{1,0:T(8,128)(2,1)} %get-tuple-element.52), channel_id=1, source_target_pairs={{0,2},{1,3},{2,0},{3,1},{4,6},{5,7},{6,4},{7,5},{8,10},{9,11},{10,... | collective-permute-start | bytes 1572872 | tf_op jit(solution)/shard_map/ppermute | solution.py:21
  191.7 23.3 %collective-permute-start.9 = (bf16[64,4096]{1,0:T(8,128)(2,1)}, bf16[64,4096]{1,0:T(8,128)(2,1)}, u32[]{:S(2)}, u32[]{:S(2)}) collective-permute-start(bf16[64,4096]{1,0:T(8,128)(2,1)} %get-tuple-element.50), channel_id=1, source_target_pairs={{0,1},{1,2},{2,3},{3,0},{4,7},{5,4},{6,5},{7,6},{8,9},{9,10},{10,1... | collective-permute-start | bytes 1572872 | tf_op jit(solution)/shard_map/ppermute | solution.py:29
  192.7 22.3 %copy-start.1 = (bf16[64,4096]{1,0:T(8,128)(2,1)S(1)}, bf16[64,4096]{1,0:T(8,128)(2,1)}, u32[]{:S(2)}) copy-start(bf16[64,4096]{1,0:T(8,128)(2,1)} %get-tuple-element.46.x_ref) | copy-start | bytes 1572868
  213.6 1.4 copy-start.4
  213.6 1.4 copy-start.7
  225.6 5.1 %collective-permute-start.12 = (f32[64,6]{0,1:T(8,128)S(1)}, f32[64,6]{0,1:T(8,128)S(1)}, u32[]{:S(2)}, u32[]{:S(2)}) collective-permute-start(f32[64,6]{0,1:T(8,128)S(1)} %broadcast_select_fusion.3), channel_id=1, source_target_pairs={{0,2},{1,3},{2,0},{3,1},{4,6},{5,7},{6,4},{7,5},{8,10},{9,11},{10,... | collective-permute-start | bytes 4616 | tf_op jit(solution)/shard_map/ppermute | solution.py:21
Sparse Core Ops, SparseCore 0:
  25.6 75.0 all-gather.4
  102.9 71.9 all-gather.6

commit v3 on v2

--- a/solution.py
+++ b/solution.py
@@ -76,8 +76,8 @@
     return total.astype(BF)
 
 
-def merge_kernel(x_ref, a_ref, b_ref, c_ref, d_ref, x_out, n_out):
-    new = summed(x_ref, a_ref, b_ref, c_ref, d_ref)
+def merge_kernel(x_ref, a_ref, b_ref, c_ref, x_out, n_out):
+    new = summed(x_ref, a_ref, b_ref, c_ref)
     x_out[...] = new
     n_out[...] = rms(new.astype(F32))
 
@@ -86,11 +86,11 @@
     return pl.pallas_call(
         merge_kernel,
         out_shape=[pltpu.HBM(x.shape, BF)] * 2,
-        in_specs=[vmem()] * 5,
+        in_specs=[vmem()] * 4,
         out_specs=[vmem()] * 2,
         compiler_params=pltpu.CompilerParams(vmem_limit_bytes=8 * 2**20),
         name="merge_rows",
-    )(x, *in_hbm(parts))
+    )(x, *parts)
 
 
 def in_hbm(arrays):
@@ -132,36 +132,44 @@
 
 PAIR = 768
 HEADS = 4
+STEPS = 4
 
 
 def layer_kernel(place, cos_ref, sin_ref, *refs):
     *x_refs, w_ref = refs[: -SIDE - 6]
     outs = refs[-SIDE - 6 : -6]
     x_s, ctx_s, out_s, w_s, w_sem, o_sem = refs[-6:]
-    groups = (pl.ds(0, PAIR), pl.ds(PAIR, PAIR), pl.ds(2 * PAIR, HEADS * HD))
+    rows, width = x_s.shape
+    count = w_s.shape[0] // STEPS
     fetch = [
-        pltpu.make_async_copy(w_ref.at[:, :, cut], w_s.at[:, :, cut], w_sem.at[i])
-        for i, cut in enumerate(groups)
+        pltpu.make_async_copy(
+            w_ref.at[pl.ds(i * count, count)], w_s.at[pl.ds(i * count, count)], w_sem.at[i]
+        )
+        for i in range(STEPS)
     ]
     for copy in fetch:
         copy.start()
     for i, ref in enumerate(x_refs):
         start = pl.multiple_of(place[i], 64)
         x_s[pl.ds(start, ref.shape[0])] = ref[...]
-    rows, width = x_s.shape
-
-    projected = []
-    for half in range(2):
-        fetch[half].wait()
-        starts = [half * PAIR + 256 * i for i in range(3)]
-        projected.append([
-            jnp.dot(
-                x_s[...], w_s[:, :, start : start + 256].reshape(width, 256),
-                preferred_element_type=F32,
-            )
-            for start in starts
-        ])
-    fetch[2].wait()
+
+    def product(step, start):
+        some = slice(step * count, (step + 1) * count)
+        return jnp.dot(
+            x_s[:, step * count * 128 : (step + 1) * count * 128],
+            w_s[some, :, start : start + 256].reshape(count * 128, 256),
+            preferred_element_type=F32,
+        )
+
+    projected = None
+    for step, copy in enumerate(fetch):
+        copy.wait()
+        part = [
+            [product(step, half * PAIR + 256 * i) for i in range(3)] for half in range(2)
+        ]
+        projected = part if step == 0 else [
+            [a + b for a, b in zip(old, new)] for old, new in zip(projected, part)
+        ]
     lower = lax.broadcasted_iota(jnp.int32, (rows, rows), 0) >= lax.broadcasted_iota(
         jnp.int32, (rows, rows), 1
     )
@@ -210,7 +218,7 @@
             pltpu.VMEM((rows, HEADS * HD), BF),
             pltpu.VMEM((rows, width), BF),
             pltpu.VMEM(weight.shape, BF),
-            pltpu.SemaphoreType.DMA((3,)),
+            pltpu.SemaphoreType.DMA((STEPS,)),
             pltpu.SemaphoreType.DMA((SIDE,)),
         ],
         compiler_params=pltpu.CompilerParams(vmem_limit_bytes=36 * 2**20),
@@ -218,15 +226,15 @@
             flops=2 * rows * width * 2048, bytes_accessed=2**24, transcendentals=0
         ),
         name="layer",
-    )(place, *tables, *in_hbm([*blocks, weight]))
+    )(place, *tables, *blocks, *in_hbm([weight]))
 
 
 TF = 16
 
 
-def depth_kernel(x_ref, a_ref, b_ref, c_ref, d_ref, proj, dqkv, dout, logit, emb, target,
+def depth_kernel(x_ref, a_ref, b_ref, c_ref, proj, dqkv, dout, logit, emb, target,
                  o_ref, u_s, qkv_s, ctx_s):
-    new = summed(x_ref, a_ref, b_ref, c_ref, d_ref)
+    new = summed(x_ref, a_ref, b_ref, c_ref)
     normed = rms(new.astype(F32))
     depth_in = jnp.dot(normed, proj[...], preferred_element_type=F32).astype(BF)
     depth_in = depth_in.astype(F32)
@@ -276,7 +284,7 @@
     return pl.pallas_call(
         depth_kernel,
         out_shape=jax.ShapeDtypeStruct((count, 1), F32),
-        in_specs=[vmem()] * 11,
+        in_specs=[vmem()] * 10,
         out_specs=vmem(),
         scratch_shapes=[
             pltpu.VMEM((count, width), F32),
@@ -288,7 +296,7 @@
             flops=2 * count * width * 5120, bytes_accessed=2**22, transcendentals=0
         ),
         name="depth",
-    )(x, *in_hbm(parts), proj, dqkv, dout, logit, emb, target)
+    )(x, *parts, proj, dqkv, dout, logit, emb, target)
 
 
 def rope_tables(rows):
@@ -341,7 +349,6 @@
     given = lax.dynamic_index_in_dim(packed, 1 - s, 0, keepdims=False)
     got = xswap(given, [(0, 3), (3, 0), (1, 2), (2, 1)])
     first = jnp.where(s == 0, kept, got)
-    second = jnp.where(s == 0, got, kept)
     w0 = lax.all_gather(first, "dp")
     frames = frames_in[0]
     normed = norm_rows(frames)
@@ -374,10 +381,10 @@
         return emb, tiled(targets)[:, None], is_valid, rope_tables(2 * row_count)
 
     emb, target, is_valid, tables = prepare(far)
-    w0, far, emb, target, tables, second = lax.optimization_barrier(
-        (w0, far, emb, target, tables, second)
+    far, emb, target, tables, (kept, got) = lax.optimization_barrier(
+        (far, emb, target, tables, (kept, got))
     )
-    w1 = lax.all_gather(second, "dp")
+    w1 = lax.all_gather(jnp.where(s == 0, got, kept), "dp")
     place0 = place_of([f * row_count, (1 - f) * row_count])
     sent = layer(place0, tables, [normed, far], w0)
 
@@ -385,7 +392,9 @@
         return [block, xhop(block, 1), xhop(block, -1), xhop2(block)]
 
     def scattered(sent):
-        return [sent[0], xhop(sent[1], 1), xhop(sent[2], -1), xhop2(sent[3])]
+        relayed, back = xhop(sent[3], 1), xhop(sent[2], -1)
+        relayed = (sent[1].astype(F32) + relayed.astype(F32)).astype(BF)
+        return [sent[0], xhop(relayed, 1), back]
 
     mine = lax.dynamic_slice_in_dim(frames, s * part, part, 0)
     x1, n1 = merge_rows(mine, scattered(sent))

time: 239 us -> 235 us (0.983)
  Pallas kernels: 46.7 us -> 38.7 us
  waiting for transfers between devices: 143 us -> 135 us
  other arithmetic: 2.75 us -> 8.93 us
  local copies, waits for them, and re-layouts: 10.3 us -> 15.2 us
    ppermute x7 -> x9, waiting for transfers between devices: 71.6 us -> 37.3 us  [xhop(): return lax.ppermute(value, ('dp', 'segment', 'frame'), pairs)]
    all_gather x1, waiting for transfers between devices: 2.95 us -> 28.8 us  [local(): w1 = lax.all_gather(jnp.where(s == 0, got, kept), 'dp')]
    ppermute x1, waiting for transfers between devices: 0.01 us -> 8.31 us  [local(): lax.ppermute(given_codes[0, row_count - DMAX:], 'frame', [(0, 1)])]
    all_gather x1, waiting for transfers between devices: 50.8 us -> 45.7 us  [local(): w0 = lax.all_gather(first, 'dp')]
    pallas_call x2, Pallas kernels: 26.2 us -> 21.6 us  [layer(): pl.pallas_call(layer_kernel, out_shape=[pltpu.HBM((64, width), BF)] * SID...]
    unnamed x33 -> x31, local copies, waits for them, and re-layouts: 0.43 us -> 4.62 us
    convert_element_type x0 -> x2, other arithmetic: none -> 3.16 us  [scattered(): relayed = (sent[1].astype(F32) + relayed.astype(F32)).astype(BF)]
    ppermute x5 -> x3, waiting for transfers between devices: 17.7 us -> 15.1 us  [xswap(): return lax.ppermute(value, ('segment', 'frame'), pairs)]
  transfers between devices with their start and end apart: 15 -> 15, of which waited for: 11 -> 10; matrix products, arithmetic and copies ran while one was open for 3% -> 6% of each run, Pallas kernels for 10% -> 8%
where the time goes in v3:
time: 235 us
  waiting for transfers between devices  135 us (57%)
  Pallas kernels  38.7 us (16%)
  starting transfers between devices  22.7 us (10%)
  local copies, waits for them, and re-layouts  15.2 us (6%)
  between operations  14 us (6%)
  other arithmetic  8.93 us (4%)
    all_gather x1, waiting for transfers between devices, local(): w0 = lax.all_gather(first, 'dp')  45.7 us
    ppermute x9, waiting for transfers between devices, xhop(): return lax.ppermute(value, ('dp', 'segment', 'frame'), pairs)  37.3 us
    all_gather x1, waiting for transfers between devices, local(): w1 = lax.all_gather(jnp.where(s == 0, got, kept), 'dp')  28.8 us
    pallas_call x2, Pallas kernels, layer(): pl.pallas_call(layer_kernel, out_shape=[pltpu.HBM((64, width), BF)] * SID...  21.6 us
    ppermute x3, waiting for transfers between devices, xswap(): return lax.ppermute(value, ('segment', 'frame'), pairs)  15.1 us
    ppermute x9, starting transfers between devices, xhop(): return lax.ppermute(value, ('dp', 'segment', 'frame'), pairs)  12.6 us
    pallas_call x1, Pallas kernels, depth(): pl.pallas_call(depth_kernel, out_shape=jax.ShapeDtypeStruct((count, 1), F...  8.49 us
    ppermute x1, waiting for transfers between devices, local(): lax.ppermute(given_codes[0, row_count - DMAX:], 'frame', [(0, 1)])  8.31 us
  transfers between devices with their start and end apart: 15, of which 10 were waited for; matrix products, arithmetic and copies ran while one was open for 6% of the time, Pallas kernels for 8%

profile of v3, /device:TPU:0, one launch (start us, length us, event | category | flops | bytes accessed | tf_op | source)
XLA Modules:
  0.0 234.7 jit_solution(8436664945137734419)
XLA Ops:
  7.8 1.2 slice_bitcast_fusion
  9.4 2.9 %collective-permute-start = (bf16[128,2048]{1,0:T(8,128)(2,1)S(1)}, bf16[128,2048]{1,0:T(8,128)(2,1)S(1)}, u32[]{:S(2)}, u32[]{:S(2)}) collective-permute-start(bf16[128,2048]{1,0:T(8,128)(2,1)S(1)} %fusion.3), channel_id=1, source_target_pairs={{0,3},{3,0},{1,2},{2,1},{4,7},{7,4},{5,6},{6,5},{8,11},{11,8},{9,1... | collective-permute-start | bytes 1572872 | tf_op jit(solution)/shard_map/ppermute | solution.py:21
  12.3 11.9 %collective-permute-done = bf16[128,2048]{1,0:T(8,128)(2,1)S(1)} collective-permute-done((bf16[128,2048]{1,0:T(8,128)(2,1)S(1)}, bf16[128,2048]{1,0:T(8,128)(2,1)S(1)}, u32[]{:S(2)}, u32[]{:S(2)}) %collective-permute-start) | collective-permute-done | bytes 524320 | tf_op jit(solution)/shard_map/ppermute | solution.py:21
  25.6 1.4 norm_rows.1.refs_0_
  27.6 3.4 %collective-permute-start.2 = (s32[2,6]{1,0:T(2,128)S(1)}, s32[2,6]{1,0:T(2,128)S(1)}, u32[]{:S(2)}, u32[]{:S(2)}) collective-permute-start(s32[2,6]{1,0:T(2,128)S(1)} %bitcast.82), channel_id=1, source_target_pairs={{0,1},{2,3},{4,5},{6,7},{8,9},{10,11},{12,13},{14,15},{16,17},{18,... | collective-permute-start | bytes 152 | tf_op jit(solution)/shard_map/ppermute | solution.py:357
  31.8 8.3 %collective-permute-done.2 = s32[2,6]{1,0:T(2,128)S(1)} collective-permute-done((s32[2,6]{1,0:T(2,128)S(1)}, s32[2,6]{1,0:T(2,128)S(1)}, u32[]{:S(2)}, u32[]{:S(2)}) %collective-permute-start.2) | collective-permute-done | bytes 80 | tf_op jit(solution)/shard_map/ppermute | solution.py:357
  40.1 3.1 %collective-permute-done.1.refs_1_ = bf16[128,4096]{1,0:T(8,128)(2,1)S(1)} collective-permute-done((bf16[128,4096]{1,0:T(8,128)(2,1)}, bf16[128,4096]{1,0:T(8,128)(2,1)S(1)}, u32[]{:S(2)}, u32[]{:S(2)}) %collective-permute-start.1) | collective-permute-done | bytes 1048608 | tf_op jit(solution)/shard_map/ppermute | solution.py:29
  45.1 6.3 %gather_fusion = bf16[384,1024]{1,0:T(8,128)(2,1)} fusion(bf16[2048,1024]{1,0:T(8,128)(2,1)} %param.16, s32[1024]{0:T(1024)S(1)} %pad_clamp_fusion), kind=kCustom, calls=%fused_computation | custom fusion | bytes 1574400 | tf_op jit(solution)/shard_map/jit(_take)/gather | solution.py:379
  51.4 1.3 broadcast_select_fusion.emb
  52.7 1.9 broadcast_select_fusion.1
  54.9 45.7 %all-gather.5.cloned.1.call-done = bf16[4096,2048]{1,0:T(8,128)(2,1)} async-done(((bf16[128,2048]{1,0:T(8,128)(2,1)}), bf16[4096,2048]{1,0:T(8,128)(2,1)}) %all-gather.5.cloned.1.call-update) | async-done | bytes 16777232 | tf_op jit(solution)/shard_map/all_gather | solution.py:352
  100.6 1.2 copy-done.3
  101.8 10.8 %layer.2 = (bf16[64,4096]{1,0:T(8,128)(2,1)}, bf16[64,4096]{1,0:T(8,128)(2,1)}, bf16[64,4096]{1,0:T(8,128)(2,1)}, bf16[64,4096]{1,0:T(8,128)(2,1)}) custom-call(s32[8]{0:T(128)S(1)} %stack.62.place, f32[256,128]{1,0:T(8,128)S(1)} %get-tuple-element.38.cos_ref, f32[256,128]{1,0:T(8,128)S(1)} %get-tuple-element.39.sin_ref, bf16[128,4096]{1,0:T(8,128)(2,1)S(1)} %copy-done, ...), custom_call_target="tpu_custom_call" | custom-call | flops 4294967296 | bytes 16777216 | tf_op jit(solution)/shard_map/layer/pallas_call | solution.py:211
  112.7 1.5 collective-permute-start.3
  114.2 1.8 collective-permute-start.5
  116.0 11.2 %collective-permute-done.3 = bf16[64,4096]{1,0:T(8,128)(2,1)S(1)} collective-permute-done((bf16[64,4096]{1,0:T(8,128)(2,1)}, bf16[64,4096]{1,0:T(8,128)(2,1)S(1)}, u32[]{:S(2)}, u32[]{:S(2)}) %collective-permute-start.3) | collective-permute-done | bytes 524320 | tf_op jit(solution)/shard_map/ppermute | solution.py:29
  127.2 2.0 add_convert_fusion.1
  129.2 1.6 collective-permute-start.4
  130.8 9.0 %collective-permute-done.4.b_ref = bf16[64,4096]{1,0:T(8,128)(2,1)S(1)} collective-permute-done((bf16[64,4096]{1,0:T(8,128)(2,1)}, bf16[64,4096]{1,0:T(8,128)(2,1)S(1)}, u32[]{:S(2)}, u32[]{:S(2)}) %collective-permute-start.4) | collective-permute-done | bytes 524320 | tf_op jit(solution)/shard_map/ppermute | solution.py:29
  140.8 1.3 merge_rows.1
  142.1 1.9 collective-permute-start.8
  146.1 28.8 %all-gather.7.cloned.1.call-done = bf16[4096,2048]{1,0:T(8,128)(2,1)} async-done(((bf16[128,2048]{1,0:T(8,128)(2,1)}), bf16[4096,2048]{1,0:T(8,128)(2,1)}) %all-gather.7.cloned.1.call-update) | async-done | bytes 16777232 | tf_op jit(solution)/shard_map/all_gather | solution.py:387
  175.9 10.8 %layer.3 = (bf16[64,4096]{1,0:T(8,128)(2,1)}, bf16[64,4096]{1,0:T(8,128)(2,1)}, bf16[64,4096]{1,0:T(8,128)(2,1)}, bf16[64,4096]{1,0:T(8,128)(2,1)}) custom-call(s32[8]{0:T(128)S(1)} %stack.63.place, f32[256,128]{1,0:T(8,128)S(1)} %get-tuple-element.38.cos_ref, f32[256,128]{1,0:T(8,128)S(1)} %get-tuple-element.39.sin_ref, bf16[64,4096]{1,0:T(8,128)(2,1)S(1)} %copy-done.6, ...), custom_call_target="tpu_custom_call" | custom-call | flops 4294967296 | bytes 16777216 | tf_op jit(solution)/shard_map/layer/pallas_call | solution.py:211
  186.7 1.5 collective-permute-start.9
  188.3 1.8 collective-permute-start.11
  190.0 11.2 %collective-permute-done.9 = bf16[64,4096]{1,0:T(8,128)(2,1)S(1)} collective-permute-done((bf16[64,4096]{1,0:T(8,128)(2,1)}, bf16[64,4096]{1,0:T(8,128)(2,1)S(1)}, u32[]{:S(2)}, u32[]{:S(2)}) %collective-permute-start.9) | collective-permute-done | bytes 524320 | tf_op jit(solution)/shard_map/ppermute | solution.py:29
  202.4 1.9 collective-permute-start.10
  204.5 5.9 %load.1 = (bf16[4096,1024]{1,0:T(8,128)(2,1)S(1)}, bf16[3,1024,512]{2,1,0:T(8,128)(2,1)S(1)}, bf16[512,1024]{1,0:T(8,128)(2,1)S(1)}, bf16[1024,2048]{1,0:T(8,128)(2,1)S(1)}) custom-call(bf16[4096,1024]{1,0:T(8,128)(2,1)} %refs_0_, bf16[3,1024,512]{2,1,0:T(8,128)(2,1)} %bitcast.68, bf16[512,1024]{1,0:T(8,128)(2,1)} %refs_2_, bf16[1024,2048]{1,0:T(8,128)(2,1)} %refs_3_), custom_call_target="tpu_custom_call" | custom-call | bytes 16777216 | tf_op jit(solution)/shard_map/load/pallas_call | solution.py:110
  210.4 2.7 %collective-permute-done.10.b_ref = bf16[64,4096]{1,0:T(8,128)(2,1)S(1)} collective-permute-done((bf16[64,4096]{1,0:T(8,128)(2,1)S(1)}, bf16[64,4096]{1,0:T(8,128)(2,1)S(1)}, u32[]{:S(2)}, u32[]{:S(2)}) %collective-permute-start.10) | collective-permute-done | bytes 524320 | tf_op jit(solution)/shard_map/ppermute | solution.py:29
  213.1 8.5 %depth.1 = f32[384,1]{1,0:T(8,128)S(1)} custom-call(bf16[64,4096]{1,0:T(8,128)(2,1)S(1)} %copy-done.4, bf16[64,4096]{1,0:T(8,128)(2,1)S(1)} %copy-done.5, bf16[64,4096]{1,0:T(8,128)(2,1)S(1)} %collective-permute-done.10.b_ref, bf16[64,4096]{1,0:T(8,128)(2,1)S(1)} %collective-permute-done.11.c_ref, bf16[4096,1024]{1,0:T(8,128)(2,1)S(1)} %get-tuple-element.57.proj, ...), custom_call_target="tpu_custom_call" | custom-call | flops 4026531840 | bytes 4194304 | tf_op jit(solution)/shard_map/depth/pallas_call | solution.py:284
  222.1 1.9 collective-permute-start.12
  224.0 3.2 %collective-permute-done.12 = f32[64,6]{0,1:T(8,128)S(1)} collective-permute-done((f32[64,6]{0,1:T(8,128)S(1)}, f32[64,6]{0,1:T(8,128)S(1)}, u32[]{:S(2)}, u32[]{:S(2)}) %collective-permute-start.12) | collective-permute-done | bytes 1568 | tf_op jit(solution)/shard_map/ppermute | solution.py:21
  (86 shorter events, 12.9 us)
Async XLA Ops:
  6.5 94.0 %all-gather.5.cloned.1.call-start = ((), (), s32[]{:S(2)}) async-start(), calls=%async_computation | async-start | bytes 17301504 | tf_op jit(solution)/shard_map/all_gather | solution.py:352
  7.8 17.8 %copy-start.1 = (bf16[1,128,4096]{2,1,0:T(8,128)(2,1)S(1)}, bf16[1,128,4096]{2,1,0:T(8,128)(2,1)}, u32[]{:S(2)}) copy-start(bf16[1,128,4096]{2,1,0:T(8,128)(2,1)} %param.10) | copy-start | bytes 3145732
  9.1 18.4 %copy-start.9 = (s32[1,128,6]{1,0,2:T(1,128)S(1)}, s32[1,128,6]{1,0,2:T(1,128)}, u32[]{:S(2)}) copy-start(s32[1,128,6]{1,0,2:T(1,128)} %param.18) | copy-start | bytes 9220
  9.2 35.0 %copy-start.10 = (s32[6]{0:T(128)S(1)}, s32[6]{0:T(128)}, u32[]{:S(2)}) copy-start(s32[6]{0:T(128)} %param.19) | copy-start | bytes 76
  9.4 14.8 %collective-permute-start = (bf16[128,2048]{1,0:T(8,128)(2,1)S(1)}, bf16[128,2048]{1,0:T(8,128)(2,1)S(1)}, u32[]{:S(2)}, u32[]{:S(2)}) collective-permute-start(bf16[128,2048]{1,0:T(8,128)(2,1)S(1)} %fusion.3), channel_id=1, source_target_pairs={{0,3},{3,0},{1,2},{2,1},{4,7},{7,4},{5,6},{6,5},{8,11},{11,8},{9,1... | collective-permute-start | bytes 1572872 | tf_op jit(solution)/shard_map/ppermute | solution.py:21
  24.3 1.3 copy-start.8
  25.5 149.4 %all-gather.7.cloned.1.call-start = ((), (), s32[]{:S(2)}) async-start(), calls=%async_computation.1 | async-start | bytes 17301504 | tf_op jit(solution)/shard_map/all_gather | solution.py:387
  27.0 16.2 %collective-permute-start.1 = (bf16[128,4096]{1,0:T(8,128)(2,1)}, bf16[128,4096]{1,0:T(8,128)(2,1)S(1)}, u32[]{:S(2)}, u32[]{:S(2)}) collective-permute-start(bf16[128,4096]{1,0:T(8,128)(2,1)} %norm_rows.1.refs_0_), channel_id=1, source_target_pairs={{0,1},{1,2},{2,3},{3,0},{4,7},{5,4},{6,5},{7,6},{8,9},{9,10},{10,1... | collective-permute-start | bytes 3145736 | tf_op jit(solution)/shard_map/ppermute | solution.py:29
  27.6 12.5 %collective-permute-start.2 = (s32[2,6]{1,0:T(2,128)S(1)}, s32[2,6]{1,0:T(2,128)S(1)}, u32[]{:S(2)}, u32[]{:S(2)}) collective-permute-start(s32[2,6]{1,0:T(2,128)S(1)} %bitcast.82), channel_id=1, source_target_pairs={{0,1},{2,3},{4,5},{6,7},{8,9},{10,11},{12,13},{14,15},{16,17},{18,... | collective-permute-start | bytes 152 | tf_op jit(solution)/shard_map/ppermute | solution.py:357
  43.2 1.0 copy-start.2
  45.1 55.5 %copy-start = (bf16[128,4096]{1,0:T(8,128)(2,1)S(1)}, bf16[128,4096]{1,0:T(8,128)(2,1)}, u32[]{:S(2)}) copy-start(bf16[128,4096]{1,0:T(8,128)(2,1)} %norm_rows.1.refs_0_) | copy-start | bytes 3145732
  100.6 1.2 copy-start.3
  112.7 14.5 %collective-permute-start.3 = (bf16[64,4096]{1,0:T(8,128)(2,1)}, bf16[64,4096]{1,0:T(8,128)(2,1)S(1)}, u32[]{:S(2)}, u32[]{:S(2)}) collective-permute-start(bf16[64,4096]{1,0:T(8,128)(2,1)} %get-tuple-element.43), channel_id=1, source_target_pairs={{0,1},{1,2},{2,3},{3,0},{4,7},{5,4},{6,5},{7,6},{8,9},{9,10},{10,1... | collective-permute-start | bytes 1572872 | tf_op jit(solution)/shard_map/ppermute | solution.py:29
  114.2 16.6 %collective-permute-start.5 = (bf16[64,4096]{1,0:T(8,128)(2,1)}, bf16[64,4096]{1,0:T(8,128)(2,1)S(1)}, u32[]{:S(2)}, u32[]{:S(2)}) collective-permute-start(bf16[64,4096]{1,0:T(8,128)(2,1)} %get-tuple-element.44), channel_id=1, source_target_pairs={{0,3},{1,0},{2,1},{3,2},{4,5},{5,6},{6,7},{7,4},{8,11},{9,8},{10,9... | collective-permute-start | bytes 1572872 | tf_op jit(solution)/shard_map/ppermute | solution.py:29
  129.2 10.6 %collective-permute-start.4 = (bf16[64,4096]{1,0:T(8,128)(2,1)}, bf16[64,4096]{1,0:T(8,128)(2,1)S(1)}, u32[]{:S(2)}, u32[]{:S(2)}) collective-permute-start(bf16[64,4096]{1,0:T(8,128)(2,1)} %add_convert_fusion.1), channel_id=1, source_target_pairs={{0,1},{1,2},{2,3},{3,0},{4,7},{5,4},{6,5},{7,6},{8,9},{9,10},{10,1... | collective-permute-start | bytes 1572872 | tf_op jit(solution)/shard_map/ppermute | solution.py:29
  139.8 1.0 copy-start.7
  142.1 32.8 %collective-permute-start.8 = (bf16[64,4096]{1,0:T(8,128)(2,1)}, bf16[64,4096]{1,0:T(8,128)(2,1)S(1)}, u32[]{:S(2)}, u32[]{:S(2)}) collective-permute-start(bf16[64,4096]{1,0:T(8,128)(2,1)} %get-tuple-element.46.refs_0_), channel_id=1, source_target_pairs={{0,2},{1,3},{2,0},{3,1},{4,6},{5,7},{6,4},{7,5},{8,10},{9,11},{10,... | collective-permute-start | bytes 1572872 | tf_op jit(solution)/shard_map/ppermute | solution.py:21
  144.0 30.9 %collective-permute-start.7 = (bf16[64,4096]{1,0:T(8,128)(2,1)}, bf16[64,4096]{1,0:T(8,128)(2,1)S(1)}, u32[]{:S(2)}, u32[]{:S(2)}) collective-permute-start(bf16[64,4096]{1,0:T(8,128)(2,1)} %get-tuple-element.46.refs_0_), channel_id=1, source_target_pairs={{0,3},{1,0},{2,1},{3,2},{4,5},{5,6},{6,7},{7,4},{8,11},{9,8},{10,9... | collective-permute-start | bytes 1572872 | tf_op jit(solution)/shard_map/ppermute | solution.py:29
  145.2 29.7 %collective-permute-start.6 = (bf16[64,4096]{1,0:T(8,128)(2,1)}, bf16[64,4096]{1,0:T(8,128)(2,1)S(1)}, u32[]{:S(2)}, u32[]{:S(2)}) collective-permute-start(bf16[64,4096]{1,0:T(8,128)(2,1)} %get-tuple-element.46.refs_0_), channel_id=1, source_target_pairs={{0,1},{1,2},{2,3},{3,0},{4,7},{5,4},{6,5},{7,6},{8,9},{9,10},{10,1... | collective-permute-start | bytes 1572872 | tf_op jit(solution)/shard_map/ppermute | solution.py:29
  174.9 1.0 copy-start.6
  186.7 14.5 %collective-permute-start.9 = (bf16[64,4096]{1,0:T(8,128)(2,1)}, bf16[64,4096]{1,0:T(8,128)(2,1)S(1)}, u32[]{:S(2)}, u32[]{:S(2)}) collective-permute-start(bf16[64,4096]{1,0:T(8,128)(2,1)} %get-tuple-element.51), channel_id=1, source_target_pairs={{0,1},{1,2},{2,3},{3,0},{4,7},{5,4},{6,5},{7,6},{8,9},{9,10},{10,1... | collective-permute-start | bytes 1572872 | tf_op jit(solution)/shard_map/ppermute | solution.py:29
  188.3 22.1 %collective-permute-start.11 = (bf16[64,4096]{1,0:T(8,128)(2,1)}, bf16[64,4096]{1,0:T(8,128)(2,1)S(1)}, u32[]{:S(2)}, u32[]{:S(2)}) collective-permute-start(bf16[64,4096]{1,0:T(8,128)(2,1)} %get-tuple-element.52), channel_id=1, source_target_pairs={{0,3},{1,0},{2,1},{3,2},{4,5},{5,6},{6,7},{7,4},{8,11},{9,8},{10,9... | collective-permute-start | bytes 1572872 | tf_op jit(solution)/shard_map/ppermute | solution.py:29
  202.4 10.7 %collective-permute-start.10 = (bf16[64,4096]{1,0:T(8,128)(2,1)S(1)}, bf16[64,4096]{1,0:T(8,128)(2,1)S(1)}, u32[]{:S(2)}, u32[]{:S(2)}) collective-permute-start(bf16[64,4096]{1,0:T(8,128)(2,1)S(1)} %add_convert_fusion), channel_id=1, source_target_pairs={{0,1},{1,2},{2,3},{3,0},{4,7},{5,4},{6,5},{7,6},{8,9},{9,10},{10,1... | collective-permute-start | bytes 1572872 | tf_op jit(solution)/shard_map/ppermute | solution.py:29
  204.4 8.7 %copy-start.4 = (bf16[64,4096]{1,0:T(8,128)(2,1)S(1)}, bf16[64,4096]{1,0:T(8,128)(2,1)}, u32[]{:S(2)}) copy-start(bf16[64,4096]{1,0:T(8,128)(2,1)} %get-tuple-element.45.x_ref) | copy-start | bytes 1572868
  204.4 8.7 %copy-start.5 = (bf16[64,4096]{1,0:T(8,128)(2,1)S(1)}, bf16[64,4096]{1,0:T(8,128)(2,1)}, u32[]{:S(2)}) copy-start(bf16[64,4096]{1,0:T(8,128)(2,1)} %get-tuple-element.49.a_ref) | copy-start | bytes 1572868
  222.1 5.1 %collective-permute-start.12 = (f32[64,6]{0,1:T(8,128)S(1)}, f32[64,6]{0,1:T(8,128)S(1)}, u32[]{:S(2)}, u32[]{:S(2)}) collective-permute-start(f32[64,6]{0,1:T(8,128)S(1)} %broadcast_select_fusion.3), channel_id=1, source_target_pairs={{0,2},{1,3},{2,0},{3,1},{4,6},{5,7},{6,4},{7,5},{8,10},{9,11},{10,... | collective-permute-start | bytes 4616 | tf_op jit(solution)/shard_map/ppermute | solution.py:21
Sparse Core Ops, SparseCore 0:
  25.6 74.9 all-gather.4
  102.8 71.9 all-gather.6

commit v4 on v3

--- a/solution.py
+++ b/solution.py
@@ -85,7 +85,7 @@
 def merge_rows(x, parts):
     return pl.pallas_call(
         merge_kernel,
-        out_shape=[pltpu.HBM(x.shape, BF)] * 2,
+        out_shape=[pltpu.HBM(x.shape, BF), pltpu.VMEM(x.shape, BF)],
         in_specs=[vmem()] * 4,
         out_specs=[vmem()] * 2,
         compiler_params=pltpu.CompilerParams(vmem_limit_bytes=8 * 2**20),
@@ -132,7 +132,7 @@
 
 PAIR = 768
 HEADS = 4
-STEPS = 4
+STEPS = 8
 
 
 def layer_kernel(place, cos_ref, sin_ref, *refs):
@@ -310,15 +310,18 @@
     )
 
 
-def packed_weights(qkv_weight, out_weight):
+def packed_qkv(qkv_weight):
     w = jnp.transpose(qkv_weight[0], (1, 0, 2))
-    o = out_weight[0]
     halves = []
     for i in range(2):
         cuts = [slice(512 * i + 256 * j, 512 * i + 256 * j + 256) for j in range(2)]
-        parts = [w[k][:, cut] for cut in cuts for k in range(3)]
-        halves.append(jnp.concatenate([*parts, o[512 * i : 512 * i + 512].T], axis=1))
+        halves.append(jnp.concatenate([w[k][:, cut] for cut in cuts for k in range(3)], axis=1))
     return jnp.stack(halves)
+
+
+def packed_out(out_weight):
+    o = out_weight[0]
+    return jnp.stack([o[512 * i : 512 * i + 512].T for i in range(2)])
 
 
 def local(
@@ -344,10 +347,12 @@
         targets = [rows_of(me + k * sign + 4) for k in (0, 1, -1, 2)]
         return jnp.stack([*starts, *targets]).astype(jnp.int32)
 
-    packed = packed_weights(qkv_weight, out_weight)
-    kept = lax.dynamic_index_in_dim(packed, s, 0, keepdims=False)
-    given = lax.dynamic_index_in_dim(packed, 1 - s, 0, keepdims=False)
-    got = xswap(given, [(0, 3), (3, 0), (1, 2), (2, 1)])
+    kept, got = [], []
+    for packed in (packed_qkv(qkv_weight), packed_out(out_weight)):
+        kept.append(lax.dynamic_index_in_dim(packed, s, 0, keepdims=False))
+        given = lax.dynamic_index_in_dim(packed, 1 - s, 0, keepdims=False)
+        got.append(xswap(given, [(0, 3), (3, 0), (1, 2), (2, 1)]))
+    kept, got = (jnp.concatenate(parts, axis=1) for parts in (kept, got))
     first = jnp.where(s == 0, kept, got)
     w0 = lax.all_gather(first, "dp")
     frames = frames_in[0]

time: 235 us -> 234 us (level)
  waiting for transfers between devices: 135 us -> 129 us
  local copies, waits for them, and re-layouts: 15.2 us -> 18.4 us
    unnamed x31 -> x37, local copies, waits for them, and re-layouts: 4.62 us -> 8.19 us
    all_gather x1, waiting for transfers between devices: 28.8 us -> 26.4 us  [local(): w1 = lax.all_gather(jnp.where(s == 0, got, kept), 'dp')]
    ppermute x3 -> x4, waiting for transfers between devices: 15.1 us -> 14.4 us  [xswap(): return lax.ppermute(value, ('segment', 'frame'), pairs)]
    ppermute x3 -> x4, starting transfers between devices: 6.71 us -> 6.96 us  [xswap(): return lax.ppermute(value, ('segment', 'frame'), pairs)]
  transfers between devices with their start and end apart: 15 -> 16, of which waited for: 10 -> 10; matrix products, arithmetic and copies ran while one was open for 6% -> 7% of each run, Pallas kernels for 8% -> 8%
where the time goes in v4:
time: 234 us; the launch traced here: 233 us
  waiting for transfers between devices  129 us (55%)
  Pallas kernels  38 us (16%)
  starting transfers between devices  22.9 us (10%)
  local copies, waits for them, and re-layouts  18.4 us (8%)
  between operations  13.9 us (6%)
  other arithmetic  10.5 us (4%)
    all_gather x1, waiting for transfers between devices, local(): w0 = lax.all_gather(first, 'dp')  44.5 us
    ppermute x9, waiting for transfers between devices, xhop(): return lax.ppermute(value, ('dp', 'segment', 'frame'), pairs)  36.4 us
    all_gather x1, waiting for transfers between devices, local(): w1 = lax.all_gather(jnp.where(s == 0, got, kept), 'dp')  26.4 us
    pallas_call x2, Pallas kernels, layer(): pl.pallas_call(layer_kernel, out_shape=[pltpu.HBM((64, width), BF)] * SID...  21.2 us
    ppermute x4, waiting for transfers between devices, xswap(): return lax.ppermute(value, ('segment', 'frame'), pairs)  14.4 us
    ppermute x9, starting transfers between devices, xhop(): return lax.ppermute(value, ('dp', 'segment', 'frame'), pairs)  12.6 us
    pallas_call x1, Pallas kernels, depth(): pl.pallas_call(depth_kernel, out_shape=jax.ShapeDtypeStruct((count, 1), F...  8.48 us
    unnamed x37, local copies, waits for them, and re-layouts  8.19 us
  transfers between devices with their start and end apart: 16, of which 10 were waited for; matrix products, arithmetic and copies ran while one was open for 7% of the time, Pallas kernels for 8%

profile of v4, /device:TPU:0, one launch (start us, length us, event | category | flops | bytes accessed | tf_op | source)
XLA Modules:
  0.0 233.1 jit_solution(12314571983907690114)
XLA Ops:
  6.5 1.3 slice_bitcast_fusion
  9.0 2.8 %collective-permute-start = (bf16[128,1536]{1,0:T(8,128)(2,1)}, bf16[128,1536]{1,0:T(8,128)(2,1)S(1)}, u32[]{:S(2)}, u32[]{:S(2)}) collective-permute-start(bf16[128,1536]{1,0:T(8,128)(2,1)} %get-tuple-element.64), channel_id=1, source_target_pairs={{0,3},{3,0},{1,2},{2,1},{4,7},{7,4},{5,6},{6,5},{8,11},{11,8},{9,1... | collective-permute-start | bytes 1179656 | tf_op jit(solution)/shard_map/ppermute | solution.py:21
  12.7 11.3 %collective-permute-done.1 = bf16[128,512]{1,0:T(8,128)(2,1)S(1)} collective-permute-done((bf16[128,512]{1,0:T(8,128)(2,1)S(1)}, bf16[128,512]{1,0:T(8,128)(2,1)S(1)}, u32[]{:S(2)}, u32[]{:S(2)}) %collective-permute-start.1) | collective-permute-done | bytes 131104 | tf_op jit(solution)/shard_map/ppermute | solution.py:21
  25.0 1.4 norm_rows.1.refs_0_
  28.5 3.4 %collective-permute-start.3 = (s32[2,6]{1,0:T(2,128)S(1)}, s32[2,6]{1,0:T(2,128)S(1)}, u32[]{:S(2)}, u32[]{:S(2)}) collective-permute-start(s32[2,6]{1,0:T(2,128)S(1)} %bitcast.89), channel_id=1, source_target_pairs={{0,1},{2,3},{4,5},{6,7},{8,9},{10,11},{12,13},{14,15},{16,17},{18,... | collective-permute-start | bytes 152 | tf_op jit(solution)/shard_map/ppermute | solution.py:362
  33.5 7.4 %collective-permute-done.3 = s32[2,6]{1,0:T(2,128)S(1)} collective-permute-done((s32[2,6]{1,0:T(2,128)S(1)}, s32[2,6]{1,0:T(2,128)S(1)}, u32[]{:S(2)}, u32[]{:S(2)}) %collective-permute-start.3) | collective-permute-done | bytes 80 | tf_op jit(solution)/shard_map/ppermute | solution.py:362
  40.9 3.1 %collective-permute-done.2.refs_1_ = bf16[128,4096]{1,0:T(8,128)(2,1)S(1)} collective-permute-done((bf16[128,4096]{1,0:T(8,128)(2,1)}, bf16[128,4096]{1,0:T(8,128)(2,1)S(1)}, u32[]{:S(2)}, u32[]{:S(2)}) %collective-permute-start.2) | collective-permute-done | bytes 1048608 | tf_op jit(solution)/shard_map/ppermute | solution.py:29
  45.9 6.2 %gather_fusion = bf16[384,1024]{1,0:T(8,128)(2,1)} fusion(bf16[2048,1024]{1,0:T(8,128)(2,1)} %param.16, s32[1024]{0:T(1024)S(1)} %pad_clamp_fusion), kind=kCustom, calls=%fused_computation | custom fusion | bytes 1574400 | tf_op jit(solution)/shard_map/jit(_take)/gather | solution.py:384
  52.2 1.3 broadcast_select_fusion.emb
  53.4 1.9 broadcast_select_fusion.1
  55.7 44.5 %all-gather.4.cloned.1.call-done.refs_2_ = bf16[32,128,2048]{2,1,0:T(8,128)(2,1)} async-done(((bf16[1,128,2048]{2,1,0:T(8,128)(2,1)}), bf16[32,128,2048]{2,1,0:T(8,128)(2,1)}) %all-gather.4.cloned.1.call-update) | async-done | bytes 16777232 | tf_op jit(solution)/shard_map/all_gather | solution.py:357
  100.2 1.2 copy-done.3
  101.4 10.6 %layer.2 = (bf16[64,4096]{1,0:T(8,128)(2,1)}, bf16[64,4096]{1,0:T(8,128)(2,1)}, bf16[64,4096]{1,0:T(8,128)(2,1)}, bf16[64,4096]{1,0:T(8,128)(2,1)}) custom-call(s32[8]{0:T(128)S(1)} %stack.74.place, f32[256,128]{1,0:T(8,128)S(1)} %get-tuple-element.38.cos_ref, f32[256,128]{1,0:T(8,128)S(1)} %get-tuple-element.39.sin_ref, bf16[128,4096]{1,0:T(8,128)(2,1)S(1)} %copy-done, ...), custom_call_target="tpu_custom_call" | custom-call | flops 4294967296 | bytes 16777216 | tf_op jit(solution)/shard_map/layer/pallas_call | solution.py:211
  112.0 1.5 collective-permute-start.4
  113.5 1.8 collective-permute-start.6
  115.3 11.2 %collective-permute-done.4 = bf16[64,4096]{1,0:T(8,128)(2,1)S(1)} collective-permute-done((bf16[64,4096]{1,0:T(8,128)(2,1)}, bf16[64,4096]{1,0:T(8,128)(2,1)S(1)}, u32[]{:S(2)}, u32[]{:S(2)}) %collective-permute-start.4) | collective-permute-done | bytes 524320 | tf_op jit(solution)/shard_map/ppermute | solution.py:29
  126.5 2.0 add_convert_fusion.1
  128.5 1.6 collective-permute-start.5
  130.9 8.1 %collective-permute-done.5.b_ref = bf16[64,4096]{1,0:T(8,128)(2,1)S(1)} collective-permute-done((bf16[64,4096]{1,0:T(8,128)(2,1)}, bf16[64,4096]{1,0:T(8,128)(2,1)S(1)}, u32[]{:S(2)}, u32[]{:S(2)}) %collective-permute-start.5) | collective-permute-done | bytes 524320 | tf_op jit(solution)/shard_map/ppermute | solution.py:29
  142.0 1.2 copy-done.10
  144.3 1.7 collective-permute-start.9
  148.1 26.4 %all-gather.6.cloned.1.call-done = bf16[4096,2048]{1,0:T(8,128)(2,1)} async-done(((bf16[128,2048]{1,0:T(8,128)(2,1)}), bf16[4096,2048]{1,0:T(8,128)(2,1)}) %all-gather.6.cloned.1.call-update) | async-done | bytes 16777232 | tf_op jit(solution)/shard_map/all_gather | solution.py:392
  174.5 10.6 %layer.3 = (bf16[64,4096]{1,0:T(8,128)(2,1)}, bf16[64,4096]{1,0:T(8,128)(2,1)}, bf16[64,4096]{1,0:T(8,128)(2,1)}, bf16[64,4096]{1,0:T(8,128)(2,1)}) custom-call(s32[8]{0:T(128)S(1)} %stack.75.place, f32[256,128]{1,0:T(8,128)S(1)} %get-tuple-element.38.cos_ref, f32[256,128]{1,0:T(8,128)S(1)} %get-tuple-element.39.sin_ref, ...), custom_call_target="tpu_custom_call" | custom-call | flops 4294967296 | bytes 16777216 | tf_op jit(solution)/shard_map/layer/pallas_call | solution.py:211
  185.1 1.5 collective-permute-start.10
  186.6 1.8 collective-permute-start.12
  188.4 11.2 %collective-permute-done.10 = bf16[64,4096]{1,0:T(8,128)(2,1)S(1)} collective-permute-done((bf16[64,4096]{1,0:T(8,128)(2,1)}, bf16[64,4096]{1,0:T(8,128)(2,1)S(1)}, u32[]{:S(2)}, u32[]{:S(2)}) %collective-permute-start.10) | collective-permute-done | bytes 524320 | tf_op jit(solution)/shard_map/ppermute | solution.py:29
  200.8 1.9 collective-permute-start.11
  202.8 5.9 %load.1 = (bf16[4096,1024]{1,0:T(8,128)(2,1)S(1)}, bf16[3,1024,512]{2,1,0:T(8,128)(2,1)S(1)}, bf16[512,1024]{1,0:T(8,128)(2,1)S(1)}, bf16[1024,2048]{1,0:T(8,128)(2,1)S(1)}) custom-call(bf16[4096,1024]{1,0:T(8,128)(2,1)} %refs_0_, bf16[3,1024,512]{2,1,0:T(8,128)(2,1)} %bitcast.72, bf16[512,1024]{1,0:T(8,128)(2,1)} %refs_2_, bf16[1024,2048]{1,0:T(8,128)(2,1)} %refs_3_), custom_call_target="tpu_custom_call" | custom-call | bytes 16777216 | tf_op jit(solution)/shard_map/load/pallas_call | solution.py:110
  208.7 2.7 %collective-permute-done.11.b_ref = bf16[64,4096]{1,0:T(8,128)(2,1)S(1)} collective-permute-done((bf16[64,4096]{1,0:T(8,128)(2,1)S(1)}, bf16[64,4096]{1,0:T(8,128)(2,1)S(1)}, u32[]{:S(2)}, u32[]{:S(2)}) %collective-permute-start.11) | collective-permute-done | bytes 524320 | tf_op jit(solution)/shard_map/ppermute | solution.py:29
  211.5 8.5 %depth.1 = f32[384,1]{1,0:T(8,128)S(1)} custom-call(bf16[64,4096]{1,0:T(8,128)(2,1)S(1)} %copy-done.4, bf16[64,4096]{1,0:T(8,128)(2,1)S(1)} %copy-done.5, bf16[64,4096]{1,0:T(8,128)(2,1)S(1)} %collective-permute-done.11.b_ref, bf16[64,4096]{1,0:T(8,128)(2,1)S(1)} %collective-permute-done.12.c_ref, bf16[4096,1024]{1,0:T(8,128)(2,1)S(1)} %get-tuple-element.57.proj, ...), custom_call_target="tpu_custom_call" | custom-call | flops 4026531840 | bytes 4194304 | tf_op jit(solution)/shard_map/depth/pallas_call | solution.py:284
  220.4 1.9 collective-permute-start.13
  222.4 3.1 %collective-permute-done.13 = f32[64,6]{0,1:T(8,128)S(1)} collective-permute-done((f32[64,6]{0,1:T(8,128)S(1)}, f32[64,6]{0,1:T(8,128)S(1)}, u32[]{:S(2)}, u32[]{:S(2)}) %collective-permute-start.13) | collective-permute-done | bytes 1568 | tf_op jit(solution)/shard_map/ppermute | solution.py:21
  (97 shorter events, 18.0 us)
Async XLA Ops:
  6.5 5.3 %copy-start.11 = (bf16[1,1024,128]{2,1,0:T(8,128)(2,1)S(1)}, bf16[1,1024,128]{2,1,0:T(8,128)(2,1)}, u32[]{:S(2)}) copy-start(bf16[1,1024,128]{2,1,0:T(8,128)(2,1)} %param.12) | copy-start | bytes 786436
  6.5 93.6 %all-gather.4.cloned.1.call-start = ((), (), s32[]{:S(2)}) async-start(), calls=%async_computation | async-start | bytes 17301504 | tf_op jit(solution)/shard_map/all_gather | solution.py:357
  6.5 18.4 %copy-start.1 = (bf16[1,128,4096]{2,1,0:T(8,128)(2,1)S(1)}, bf16[1,128,4096]{2,1,0:T(8,128)(2,1)}, u32[]{:S(2)}) copy-start(bf16[1,128,4096]{2,1,0:T(8,128)(2,1)} %param.10) | copy-start | bytes 3145732
  7.9 20.4 %copy-start.12 = (s32[1,128,6]{1,0,2:T(1,128)S(1)}, s32[1,128,6]{1,0,2:T(1,128)}, u32[]{:S(2)}) copy-start(s32[1,128,6]{1,0,2:T(1,128)} %param.18) | copy-start | bytes 9220
  9.0 15.0 %collective-permute-start = (bf16[128,1536]{1,0:T(8,128)(2,1)}, bf16[128,1536]{1,0:T(8,128)(2,1)S(1)}, u32[]{:S(2)}, u32[]{:S(2)}) collective-permute-start(bf16[128,1536]{1,0:T(8,128)(2,1)} %get-tuple-element.64), channel_id=1, source_target_pairs={{0,3},{3,0},{1,2},{2,1},{4,7},{7,4},{5,6},{6,5},{8,11},{11,8},{9,1... | collective-permute-start | bytes 1179656 | tf_op jit(solution)/shard_map/ppermute | solution.py:21
  12.0 33.1 %copy-start.13 = (s32[6]{0:T(128)S(1)}, s32[6]{0:T(128)}, u32[]{:S(2)}) copy-start(s32[6]{0:T(128)} %param.19) | copy-start | bytes 76
  12.2 11.7 %collective-permute-start.1 = (bf16[128,512]{1,0:T(8,128)(2,1)S(1)}, bf16[128,512]{1,0:T(8,128)(2,1)S(1)}, u32[]{:S(2)}, u32[]{:S(2)}) collective-permute-start(bf16[128,512]{1,0:T(8,128)(2,1)S(1)} %get-tuple-element.69), channel_id=1, source_target_pairs={{0,3},{3,0},{1,2},{2,1},{4,7},{7,4},{5,6},{6,5},{8,11},{11,8},{9,1... | collective-permute-start | bytes 393224 | tf_op jit(solution)/shard_map/ppermute | solution.py:21
  24.9 149.6 %all-gather.6.cloned.1.call-start = ((), (), s32[]{:S(2)}) async-start(), calls=%async_computation.1 | async-start | bytes 17301504 | tf_op jit(solution)/shard_map/all_gather | solution.py:392
  27.8 16.2 %collective-permute-start.2 = (bf16[128,4096]{1,0:T(8,128)(2,1)}, bf16[128,4096]{1,0:T(8,128)(2,1)S(1)}, u32[]{:S(2)}, u32[]{:S(2)}) collective-permute-start(bf16[128,4096]{1,0:T(8,128)(2,1)} %norm_rows.1.refs_0_), channel_id=1, source_target_pairs={{0,1},{1,2},{2,3},{3,0},{4,7},{5,4},{6,5},{7,6},{8,9},{9,10},{10,1... | collective-permute-start | bytes 3145736 | tf_op jit(solution)/shard_map/ppermute | solution.py:29
  28.5 12.5 %collective-permute-start.3 = (s32[2,6]{1,0:T(2,128)S(1)}, s32[2,6]{1,0:T(2,128)S(1)}, u32[]{:S(2)}, u32[]{:S(2)}) collective-permute-start(s32[2,6]{1,0:T(2,128)S(1)} %bitcast.89), channel_id=1, source_target_pairs={{0,1},{2,3},{4,5},{6,7},{8,9},{10,11},{12,13},{14,15},{16,17},{18,... | collective-permute-start | bytes 152 | tf_op jit(solution)/shard_map/ppermute | solution.py:362
  44.0 1.0 copy-start.2
  45.9 54.3 %copy-start = (bf16[128,4096]{1,0:T(8,128)(2,1)S(1)}, bf16[128,4096]{1,0:T(8,128)(2,1)}, u32[]{:S(2)}) copy-start(bf16[128,4096]{1,0:T(8,128)(2,1)} %norm_rows.1.refs_0_) | copy-start | bytes 3145732
  100.2 1.2 copy-start.3
  112.0 14.5 %collective-permute-start.4 = (bf16[64,4096]{1,0:T(8,128)(2,1)}, bf16[64,4096]{1,0:T(8,128)(2,1)S(1)}, u32[]{:S(2)}, u32[]{:S(2)}) collective-permute-start(bf16[64,4096]{1,0:T(8,128)(2,1)} %get-tuple-element.43), channel_id=1, source_target_pairs={{0,1},{1,2},{2,3},{3,0},{4,7},{5,4},{6,5},{7,6},{8,9},{9,10},{10,1... | collective-permute-start | bytes 1572872 | tf_op jit(solution)/shard_map/ppermute | solution.py:29
  113.5 16.6 %collective-permute-start.6 = (bf16[64,4096]{1,0:T(8,128)(2,1)}, bf16[64,4096]{1,0:T(8,128)(2,1)S(1)}, u32[]{:S(2)}, u32[]{:S(2)}) collective-permute-start(bf16[64,4096]{1,0:T(8,128)(2,1)} %get-tuple-element.44), channel_id=1, source_target_pairs={{0,3},{1,0},{2,1},{3,2},{4,5},{5,6},{6,7},{7,4},{8,11},{9,8},{10,9... | collective-permute-start | bytes 1572872 | tf_op jit(solution)/shard_map/ppermute | solution.py:29
  128.5 10.6 %collective-permute-start.5 = (bf16[64,4096]{1,0:T(8,128)(2,1)}, bf16[64,4096]{1,0:T(8,128)(2,1)S(1)}, u32[]{:S(2)}, u32[]{:S(2)}) collective-permute-start(bf16[64,4096]{1,0:T(8,128)(2,1)} %add_convert_fusion.1), channel_id=1, source_target_pairs={{0,1},{1,2},{2,3},{3,0},{4,7},{5,4},{6,5},{7,6},{8,9},{9,10},{10,1... | collective-permute-start | bytes 1572872 | tf_op jit(solution)/shard_map/ppermute | solution.py:29
  130.1 0.8 copy-start.7
  139.1 0.8 copy-start.9
  139.9 1.0 copy-start.6
  140.9 1.0 copy-start.8
  142.0 1.2 copy-start.10
  144.3 30.2 %collective-permute-start.9 = (bf16[64,4096]{1,0:T(8,128)(2,1)S(1)}, bf16[64,4096]{1,0:T(8,128)(2,1)S(1)}, u32[]{:S(2)}, u32[]{:S(2)}) collective-permute-start(bf16[64,4096]{1,0:T(8,128)(2,1)S(1)} %get-tuple-element.46.refs_0_), channel_id=1, source_target_pairs={{0,2},{1,3},{2,0},{3,1},{4,6},{5,7},{6,4},{7,5},{8,10},{9,11},{10,... | collective-permute-start | bytes 1572872 | tf_op jit(solution)/shard_map/ppermute | solution.py:21
  146.0 28.5 %collective-permute-start.8 = (bf16[64,4096]{1,0:T(8,128)(2,1)S(1)}, bf16[64,4096]{1,0:T(8,128)(2,1)S(1)}, u32[]{:S(2)}, u32[]{:S(2)}) collective-permute-start(bf16[64,4096]{1,0:T(8,128)(2,1)S(1)} %get-tuple-element.46.refs_0_), channel_id=1, source_target_pairs={{0,3},{1,0},{2,1},{3,2},{4,5},{5,6},{6,7},{7,4},{8,11},{9,8},{10,9... | collective-permute-start | bytes 1572872 | tf_op jit(solution)/shard_map/ppermute | solution.py:29
  147.2 27.3 %collective-permute-start.7 = (bf16[64,4096]{1,0:T(8,128)(2,1)S(1)}, bf16[64,4096]{1,0:T(8,128)(2,1)S(1)}, u32[]{:S(2)}, u32[]{:S(2)}) collective-permute-start(bf16[64,4096]{1,0:T(8,128)(2,1)S(1)} %get-tuple-element.46.refs_0_), channel_id=1, source_target_pairs={{0,1},{1,2},{2,3},{3,0},{4,7},{5,4},{6,5},{7,6},{8,9},{9,10},{10,1... | collective-permute-start | bytes 1572872 | tf_op jit(solution)/shard_map/ppermute | solution.py:29
  185.1 14.5 %collective-permute-start.10 = (bf16[64,4096]{1,0:T(8,128)(2,1)}, bf16[64,4096]{1,0:T(8,128)(2,1)S(1)}, u32[]{:S(2)}, u32[]{:S(2)}) collective-permute-start(bf16[64,4096]{1,0:T(8,128)(2,1)} %get-tuple-element.51), channel_id=1, source_target_pairs={{0,1},{1,2},{2,3},{3,0},{4,7},{5,4},{6,5},{7,6},{8,9},{9,10},{10,1... | collective-permute-start | bytes 1572872 | tf_op jit(solution)/shard_map/ppermute | solution.py:29
  186.6 22.1 %collective-permute-start.12 = (bf16[64,4096]{1,0:T(8,128)(2,1)}, bf16[64,4096]{1,0:T(8,128)(2,1)S(1)}, u32[]{:S(2)}, u32[]{:S(2)}) collective-permute-start(bf16[64,4096]{1,0:T(8,128)(2,1)} %get-tuple-element.52), channel_id=1, source_target_pairs={{0,3},{1,0},{2,1},{3,2},{4,5},{5,6},{6,7},{7,4},{8,11},{9,8},{10,9... | collective-permute-start | bytes 1572872 | tf_op jit(solution)/shard_map/ppermute | solution.py:29
  200.8 10.7 %collective-permute-start.11 = (bf16[64,4096]{1,0:T(8,128)(2,1)S(1)}, bf16[64,4096]{1,0:T(8,128)(2,1)S(1)}, u32[]{:S(2)}, u32[]{:S(2)}) collective-permute-start(bf16[64,4096]{1,0:T(8,128)(2,1)S(1)} %add_convert_fusion), channel_id=1, source_target_pairs={{0,1},{1,2},{2,3},{3,0},{4,7},{5,4},{6,5},{7,6},{8,9},{9,10},{10,1... | collective-permute-start | bytes 1572872 | tf_op jit(solution)/shard_map/ppermute | solution.py:29
  202.8 8.7 %copy-start.4 = (bf16[64,4096]{1,0:T(8,128)(2,1)S(1)}, bf16[64,4096]{1,0:T(8,128)(2,1)}, u32[]{:S(2)}) copy-start(bf16[64,4096]{1,0:T(8,128)(2,1)} %get-tuple-element.45.x_ref) | copy-start | bytes 1572868
  202.8 8.7 %copy-start.5 = (bf16[64,4096]{1,0:T(8,128)(2,1)S(1)}, bf16[64,4096]{1,0:T(8,128)(2,1)}, u32[]{:S(2)}) copy-start(bf16[64,4096]{1,0:T(8,128)(2,1)} %get-tuple-element.49.a_ref) | copy-start | bytes 1572868
  220.4 5.1 %collective-permute-start.13 = (f32[64,6]{0,1:T(8,128)S(1)}, f32[64,6]{0,1:T(8,128)S(1)}, u32[]{:S(2)}, u32[]{:S(2)}) collective-permute-start(f32[64,6]{0,1:T(8,128)S(1)} %broadcast_select_fusion.2), channel_id=1, source_target_pairs={{0,2},{1,3},{2,0},{3,1},{4,6},{5,7},{6,4},{7,5},{8,10},{9,11},{10,... | collective-permute-start | bytes 4616 | tf_op jit(solution)/shard_map/ppermute | solution.py:21
Sparse Core Ops, SparseCore 0:
  25.0 75.1 all-gather.3
  102.4 71.9 all-gather.5

commit v5 on v4

--- a/solution.py
+++ b/solution.py
@@ -210,9 +210,9 @@
     rows, width = sum(b.shape[0] for b in blocks), blocks[0].shape[1]
     return pl.pallas_call(
         layer_kernel,
-        out_shape=[pltpu.HBM((64, width), BF)] * SIDE,
+        out_shape=[pltpu.VMEM((64, width), BF)] * SIDE,
         in_specs=[smem()] + [vmem()] * (2 + len(blocks)) + [anywhere()],
-        out_specs=[anywhere()] * SIDE,
+        out_specs=[vmem()] * SIDE,
         scratch_shapes=[
             pltpu.VMEM((rows, width), BF),
             pltpu.VMEM((rows, HEADS * HD), BF),
@@ -221,7 +221,7 @@
             pltpu.SemaphoreType.DMA((STEPS,)),
             pltpu.SemaphoreType.DMA((SIDE,)),
         ],
-        compiler_params=pltpu.CompilerParams(vmem_limit_bytes=36 * 2**20),
+        compiler_params=pltpu.CompilerParams(vmem_limit_bytes=28 * 2**20),
         cost_estimate=pl.CostEstimate(
             flops=2 * rows * width * 2048, bytes_accessed=2**24, transcendentals=0
         ),

time: 234 us -> 236 us (level)
  waiting for transfers between devices: 129 us -> 134 us
    all_gather x1, waiting for transfers between devices: 26.4 us -> 30.6 us  [local(): w1 = lax.all_gather(jnp.where(s == 0, got, kept), 'dp')]
where the time goes in v5:
time: 236 us; the launch traced here: 235 us
  waiting for transfers between devices  134 us (57%)
  Pallas kernels  37.3 us (16%)
  starting transfers between devices  23.6 us (10%)
  local copies, waits for them, and re-layouts  18.3 us (8%)
  between operations  13.9 us (6%)
  other arithmetic  8.43 us (4%)
    all_gather x1, waiting for transfers between devices, local(): w0 = lax.all_gather(first, 'dp')  44.5 us
    ppermute x9, waiting for transfers between devices, xhop(): return lax.ppermute(value, ('dp', 'segment', 'frame'), pairs)  36.8 us
    all_gather x1, waiting for transfers between devices, local(): w1 = lax.all_gather(jnp.where(s == 0, got, kept), 'dp')  30.6 us
    pallas_call x2, Pallas kernels, layer(): pl.pallas_call(layer_kernel, out_shape=[pltpu.VMEM((64, width), BF)] * SI...  20.5 us
    ppermute x4, waiting for transfers between devices, xswap(): return lax.ppermute(value, ('segment', 'frame'), pairs)  14.1 us
    ppermute x9, starting transfers between devices, xhop(): return lax.ppermute(value, ('dp', 'segment', 'frame'), pairs)  12.5 us
    pallas_call x1, Pallas kernels, depth(): pl.pallas_call(depth_kernel, out_shape=jax.ShapeDtypeStruct((count, 1), F...  8.48 us
    unnamed x37, local copies, waits for them, and re-layouts  8.06 us
  transfers between devices with their start and end apart: 16, of which 10 were waited for; matrix products, arithmetic and copies ran while one was open for 7% of the time, Pallas kernels for 8%

profile of v5, /device:TPU:0, one launch (start us, length us, event | category | flops | bytes accessed | tf_op | source)
XLA Modules:
  0.0 235.1 jit_solution(10509764555105181375)
XLA Ops:
  6.5 1.3 slice_bitcast_fusion
  9.0 2.8 %collective-permute-start = (bf16[128,1536]{1,0:T(8,128)(2,1)}, bf16[128,1536]{1,0:T(8,128)(2,1)S(1)}, u32[]{:S(2)}, u32[]{:S(2)}) collective-permute-start(bf16[128,1536]{1,0:T(8,128)(2,1)} %get-tuple-element.64), channel_id=1, source_target_pairs={{0,3},{3,0},{1,2},{2,1},{4,7},{7,4},{5,6},{6,5},{8,11},{11,8},{9,1... | collective-permute-start | bytes 1179656 | tf_op jit(solution)/shard_map/ppermute | solution.py:21
  12.7 11.3 %collective-permute-done.1 = bf16[128,512]{1,0:T(8,128)(2,1)S(1)} collective-permute-done((bf16[128,512]{1,0:T(8,128)(2,1)S(1)}, bf16[128,512]{1,0:T(8,128)(2,1)S(1)}, u32[]{:S(2)}, u32[]{:S(2)}) %collective-permute-start.1) | collective-permute-done | bytes 131104 | tf_op jit(solution)/shard_map/ppermute | solution.py:21
  25.0 1.4 norm_rows.1.refs_0_
  28.5 3.4 %collective-permute-start.3 = (s32[2,6]{1,0:T(2,128)S(1)}, s32[2,6]{1,0:T(2,128)S(1)}, u32[]{:S(2)}, u32[]{:S(2)}) collective-permute-start(s32[2,6]{1,0:T(2,128)S(1)} %bitcast.89), channel_id=1, source_target_pairs={{0,1},{2,3},{4,5},{6,7},{8,9},{10,11},{12,13},{14,15},{16,17},{18,... | collective-permute-start | bytes 152 | tf_op jit(solution)/shard_map/ppermute | solution.py:362
  33.5 7.4 %collective-permute-done.3 = s32[2,6]{1,0:T(2,128)S(1)} collective-permute-done((s32[2,6]{1,0:T(2,128)S(1)}, s32[2,6]{1,0:T(2,128)S(1)}, u32[]{:S(2)}, u32[]{:S(2)}) %collective-permute-start.3) | collective-permute-done | bytes 80 | tf_op jit(solution)/shard_map/ppermute | solution.py:362
  40.9 3.1 %collective-permute-done.2.refs_1_ = bf16[128,4096]{1,0:T(8,128)(2,1)S(1)} collective-permute-done((bf16[128,4096]{1,0:T(8,128)(2,1)}, bf16[128,4096]{1,0:T(8,128)(2,1)S(1)}, u32[]{:S(2)}, u32[]{:S(2)}) %collective-permute-start.2) | collective-permute-done | bytes 1048608 | tf_op jit(solution)/shard_map/ppermute | solution.py:29
  45.9 6.2 %gather_fusion = bf16[384,1024]{1,0:T(8,128)(2,1)} fusion(bf16[2048,1024]{1,0:T(8,128)(2,1)} %param.16, s32[1024]{0:T(1024)S(1)} %pad_clamp_fusion), kind=kCustom, calls=%fused_computation | custom fusion | bytes 1574400 | tf_op jit(solution)/shard_map/jit(_take)/gather | solution.py:384
  52.2 1.3 broadcast_select_fusion.emb
  53.4 1.9 broadcast_select_fusion.1
  55.7 44.5 %all-gather.4.cloned.1.call-done.refs_2_ = bf16[32,128,2048]{2,1,0:T(8,128)(2,1)} async-done(((bf16[1,128,2048]{2,1,0:T(8,128)(2,1)}), bf16[32,128,2048]{2,1,0:T(8,128)(2,1)}) %all-gather.4.cloned.1.call-update) | async-done | bytes 16777232 | tf_op jit(solution)/shard_map/all_gather | solution.py:357
  100.2 1.2 copy-done.3
  101.4 10.2 %layer.2 = (bf16[64,4096]{1,0:T(8,128)(2,1)S(1)}, bf16[64,4096]{1,0:T(8,128)(2,1)S(1)}, bf16[64,4096]{1,0:T(8,128)(2,1)}, bf16[64,4096]{1,0:T(8,128)(2,1)S(1)}) custom-call(s32[8]{0:T(128)S(1)} %stack.74.place, f32[256,128]{1,0:T(8,128)S(1)} %get-tuple-element.38.cos_ref, f32[256,128]{1,0:T(8,128)S(1)} %get-tuple-element.39.sin_ref, ...), custom_call_target="tpu_custom_call" | custom-call | flops 4294967296 | bytes 16777216 | tf_op jit(solution)/shard_map/layer/pallas_call | solution.py:211
  111.7 1.5 collective-permute-start.4
  113.2 1.8 collective-permute-start.6
  115.0 10.8 %collective-permute-done.4 = bf16[64,4096]{1,0:T(8,128)(2,1)S(1)} collective-permute-done((bf16[64,4096]{1,0:T(8,128)(2,1)S(1)}, bf16[64,4096]{1,0:T(8,128)(2,1)S(1)}, u32[]{:S(2)}, u32[]{:S(2)}) %collective-permute-start.4) | collective-permute-done | bytes 524320 | tf_op jit(solution)/shard_map/ppermute | solution.py:29
  126.7 1.6 collective-permute-start.5
  128.3 9.1 %collective-permute-done.5.b_ref = bf16[64,4096]{1,0:T(8,128)(2,1)S(1)} collective-permute-done((bf16[64,4096]{1,0:T(8,128)(2,1)}, bf16[64,4096]{1,0:T(8,128)(2,1)S(1)}, u32[]{:S(2)}, u32[]{:S(2)}) %collective-permute-start.5) | collective-permute-done | bytes 524320 | tf_op jit(solution)/shard_map/ppermute | solution.py:29
  138.5 1.1 merge_rows.1
  139.6 2.2 collective-permute-start.9
  142.5 1.3 collective-permute-start.7
  143.9 30.6 %all-gather.6.cloned.1.call-done = bf16[4096,2048]{1,0:T(8,128)(2,1)} async-done(((bf16[128,2048]{1,0:T(8,128)(2,1)}), bf16[4096,2048]{1,0:T(8,128)(2,1)}) %all-gather.6.cloned.1.call-update) | async-done | bytes 16777232 | tf_op jit(solution)/shard_map/all_gather | solution.py:392
  178.2 10.2 %layer.3 = (bf16[64,4096]{1,0:T(8,128)(2,1)S(1)}, bf16[64,4096]{1,0:T(8,128)(2,1)S(1)}, bf16[64,4096]{1,0:T(8,128)(2,1)}, bf16[64,4096]{1,0:T(8,128)(2,1)S(1)}) custom-call(s32[8]{0:T(128)S(1)} %stack.75.place, f32[256,128]{1,0:T(8,128)S(1)} %get-tuple-element.38.cos_ref, f32[256,128]{1,0:T(8,128)S(1)} %get-tuple-element.39.sin_ref, ...), custom_call_target="tpu_custom_call" | custom-call | flops 4294967296 | bytes 16777216 | tf_op jit(solution)/shard_map/layer/pallas_call | solution.py:211
  188.5 1.5 collective-permute-start.10
  190.0 1.8 collective-permute-start.12
  191.8 10.8 %collective-permute-done.10 = bf16[64,4096]{1,0:T(8,128)(2,1)S(1)} collective-permute-done((bf16[64,4096]{1,0:T(8,128)(2,1)S(1)}, bf16[64,4096]{1,0:T(8,128)(2,1)S(1)}, u32[]{:S(2)}, u32[]{:S(2)}) %collective-permute-start.10) | collective-permute-done | bytes 524320 | tf_op jit(solution)/shard_map/ppermute | solution.py:29
  202.7 1.8 collective-permute-start.11
  204.7 5.9 %load.1 = (bf16[4096,1024]{1,0:T(8,128)(2,1)S(1)}, bf16[3,1024,512]{2,1,0:T(8,128)(2,1)S(1)}, bf16[512,1024]{1,0:T(8,128)(2,1)S(1)}, bf16[1024,2048]{1,0:T(8,128)(2,1)S(1)}) custom-call(bf16[4096,1024]{1,0:T(8,128)(2,1)} %refs_0_, bf16[3,1024,512]{2,1,0:T(8,128)(2,1)} %bitcast.72, bf16[512,1024]{1,0:T(8,128)(2,1)} %refs_2_, bf16[1024,2048]{1,0:T(8,128)(2,1)} %refs_3_), custom_call_target="tpu_custom_call" | custom-call | bytes 16777216 | tf_op jit(solution)/shard_map/load/pallas_call | solution.py:110
  210.6 3.0 %collective-permute-done.11.b_ref = bf16[64,4096]{1,0:T(8,128)(2,1)S(1)} collective-permute-done((bf16[64,4096]{1,0:T(8,128)(2,1)S(1)}, bf16[64,4096]{1,0:T(8,128)(2,1)S(1)}, u32[]{:S(2)}, u32[]{:S(2)}) %collective-permute-start.11) | collective-permute-done | bytes 524320 | tf_op jit(solution)/shard_map/ppermute | solution.py:29
  213.5 8.5 %depth.1 = f32[384,1]{1,0:T(8,128)S(1)} custom-call(bf16[64,4096]{1,0:T(8,128)(2,1)S(1)} %copy-done.4, bf16[64,4096]{1,0:T(8,128)(2,1)S(1)} %get-tuple-element.49.a_ref, bf16[64,4096]{1,0:T(8,128)(2,1)S(1)} %collective-permute-done.11.b_ref, bf16[64,4096]{1,0:T(8,128)(2,1)S(1)} %collective-permute-done.12.c_ref, ...), custom_call_target="tpu_custom_call" | custom-call | flops 4026531840 | bytes 4194304 | tf_op jit(solution)/shard_map/depth/pallas_call | solution.py:284
  222.5 2.2 collective-permute-start.13
  224.7 2.9 %collective-permute-done.13 = f32[64,6]{0,1:T(8,128)S(1)} collective-permute-done((f32[64,6]{0,1:T(8,128)S(1)}, f32[64,6]{0,1:T(8,128)S(1)}, u32[]{:S(2)}, u32[]{:S(2)}) %collective-permute-start.13) | collective-permute-done | bytes 1568 | tf_op jit(solution)/shard_map/ppermute | solution.py:21
  (97 shorter events, 16.6 us)
Async XLA Ops:
  6.5 5.3 %copy-start.11 = (bf16[1,1024,128]{2,1,0:T(8,128)(2,1)S(1)}, bf16[1,1024,128]{2,1,0:T(8,128)(2,1)}, u32[]{:S(2)}) copy-start(bf16[1,1024,128]{2,1,0:T(8,128)(2,1)} %param.12) | copy-start | bytes 786436
  6.5 93.6 %all-gather.4.cloned.1.call-start = ((), (), s32[]{:S(2)}) async-start(), calls=%async_computation | async-start | bytes 17301504 | tf_op jit(solution)/shard_map/all_gather | solution.py:357
  6.5 18.4 %copy-start.1 = (bf16[1,128,4096]{2,1,0:T(8,128)(2,1)S(1)}, bf16[1,128,4096]{2,1,0:T(8,128)(2,1)}, u32[]{:S(2)}) copy-start(bf16[1,128,4096]{2,1,0:T(8,128)(2,1)} %param.10) | copy-start | bytes 3145732
  7.9 20.4 %copy-start.12 = (s32[1,128,6]{1,0,2:T(1,128)S(1)}, s32[1,128,6]{1,0,2:T(1,128)}, u32[]{:S(2)}) copy-start(s32[1,128,6]{1,0,2:T(1,128)} %param.18) | copy-start | bytes 9220
  9.0 15.0 %collective-permute-start = (bf16[128,1536]{1,0:T(8,128)(2,1)}, bf16[128,1536]{1,0:T(8,128)(2,1)S(1)}, u32[]{:S(2)}, u32[]{:S(2)}) collective-permute-start(bf16[128,1536]{1,0:T(8,128)(2,1)} %get-tuple-element.64), channel_id=1, source_target_pairs={{0,3},{3,0},{1,2},{2,1},{4,7},{7,4},{5,6},{6,5},{8,11},{11,8},{9,1... | collective-permute-start | bytes 1179656 | tf_op jit(solution)/shard_map/ppermute | solution.py:21
  12.0 33.1 %copy-start.13 = (s32[6]{0:T(128)S(1)}, s32[6]{0:T(128)}, u32[]{:S(2)}) copy-start(s32[6]{0:T(128)} %param.19) | copy-start | bytes 76
  12.2 11.7 %collective-permute-start.1 = (bf16[128,512]{1,0:T(8,128)(2,1)S(1)}, bf16[128,512]{1,0:T(8,128)(2,1)S(1)}, u32[]{:S(2)}, u32[]{:S(2)}) collective-permute-start(bf16[128,512]{1,0:T(8,128)(2,1)S(1)} %get-tuple-element.69), channel_id=1, source_target_pairs={{0,3},{3,0},{1,2},{2,1},{4,7},{7,4},{5,6},{6,5},{8,11},{11,8},{9,1... | collective-permute-start | bytes 393224 | tf_op jit(solution)/shard_map/ppermute | solution.py:21
  24.9 149.6 %all-gather.6.cloned.1.call-start = ((), (), s32[]{:S(2)}) async-start(), calls=%async_computation.1 | async-start | bytes 17301504 | tf_op jit(solution)/shard_map/all_gather | solution.py:392
  27.8 16.2 %collective-permute-start.2 = (bf16[128,4096]{1,0:T(8,128)(2,1)}, bf16[128,4096]{1,0:T(8,128)(2,1)S(1)}, u32[]{:S(2)}, u32[]{:S(2)}) collective-permute-start(bf16[128,4096]{1,0:T(8,128)(2,1)} %norm_rows.1.refs_0_), channel_id=1, source_target_pairs={{0,1},{1,2},{2,3},{3,0},{4,7},{5,4},{6,5},{7,6},{8,9},{9,10},{10,1... | collective-permute-start | bytes 3145736 | tf_op jit(solution)/shard_map/ppermute | solution.py:29
  28.5 12.5 %collective-permute-start.3 = (s32[2,6]{1,0:T(2,128)S(1)}, s32[2,6]{1,0:T(2,128)S(1)}, u32[]{:S(2)}, u32[]{:S(2)}) collective-permute-start(s32[2,6]{1,0:T(2,128)S(1)} %bitcast.89), channel_id=1, source_target_pairs={{0,1},{2,3},{4,5},{6,7},{8,9},{10,11},{12,13},{14,15},{16,17},{18,... | collective-permute-start | bytes 152 | tf_op jit(solution)/shard_map/ppermute | solution.py:362
  44.0 1.0 copy-start.2
  45.9 54.3 %copy-start = (bf16[128,4096]{1,0:T(8,128)(2,1)S(1)}, bf16[128,4096]{1,0:T(8,128)(2,1)}, u32[]{:S(2)}) copy-start(bf16[128,4096]{1,0:T(8,128)(2,1)} %norm_rows.1.refs_0_) | copy-start | bytes 3145732
  100.2 1.2 copy-start.3
  111.7 15.0 %copy-start.9 = (bf16[64,4096]{1,0:T(8,128)(2,1)}, bf16[64,4096]{1,0:T(8,128)(2,1)S(1)}, u32[]{:S(2)}) copy-start(bf16[64,4096]{1,0:T(8,128)(2,1)S(1)} %get-tuple-element.41.a_ref) | copy-start | bytes 1572868
  111.7 14.1 %collective-permute-start.4 = (bf16[64,4096]{1,0:T(8,128)(2,1)S(1)}, bf16[64,4096]{1,0:T(8,128)(2,1)S(1)}, u32[]{:S(2)}, u32[]{:S(2)}) collective-permute-start(bf16[64,4096]{1,0:T(8,128)(2,1)S(1)} %get-tuple-element.43), channel_id=1, source_target_pairs={{0,1},{1,2},{2,3},{3,0},{4,7},{5,4},{6,5},{7,6},{8,9},{9,10},{10,1... | collective-permute-start | bytes 1572872 | tf_op jit(solution)/shard_map/ppermute | solution.py:29
  113.2 15.1 %collective-permute-start.6 = (bf16[64,4096]{1,0:T(8,128)(2,1)}, bf16[64,4096]{1,0:T(8,128)(2,1)S(1)}, u32[]{:S(2)}, u32[]{:S(2)}) collective-permute-start(bf16[64,4096]{1,0:T(8,128)(2,1)} %get-tuple-element.44), channel_id=1, source_target_pairs={{0,3},{1,0},{2,1},{3,2},{4,5},{5,6},{6,7},{7,4},{8,11},{9,8},{10,9... | collective-permute-start | bytes 1572872 | tf_op jit(solution)/shard_map/ppermute | solution.py:29
  126.7 10.8 %collective-permute-start.5 = (bf16[64,4096]{1,0:T(8,128)(2,1)}, bf16[64,4096]{1,0:T(8,128)(2,1)S(1)}, u32[]{:S(2)}, u32[]{:S(2)}) collective-permute-start(bf16[64,4096]{1,0:T(8,128)(2,1)} %add_convert_fusion.1), channel_id=1, source_target_pairs={{0,1},{1,2},{2,3},{3,0},{4,7},{5,4},{6,5},{7,6},{8,9},{9,10},{10,1... | collective-permute-start | bytes 1572872 | tf_op jit(solution)/shard_map/ppermute | solution.py:29
  137.4 1.0 copy-start.10
  139.6 34.9 %collective-permute-start.9 = (bf16[64,4096]{1,0:T(8,128)(2,1)S(1)}, bf16[64,4096]{1,0:T(8,128)(2,1)S(1)}, u32[]{:S(2)}, u32[]{:S(2)}) collective-permute-start(bf16[64,4096]{1,0:T(8,128)(2,1)S(1)} %get-tuple-element.46.refs_0_), channel_id=1, source_target_pairs={{0,2},{1,3},{2,0},{3,1},{4,6},{5,7},{6,4},{7,5},{8,10},{9,11},{10,... | collective-permute-start | bytes 1572872 | tf_op jit(solution)/shard_map/ppermute | solution.py:21
  141.8 32.7 %collective-permute-start.8 = (bf16[64,4096]{1,0:T(8,128)(2,1)S(1)}, bf16[64,4096]{1,0:T(8,128)(2,1)S(1)}, u32[]{:S(2)}, u32[]{:S(2)}) collective-permute-start(bf16[64,4096]{1,0:T(8,128)(2,1)S(1)} %get-tuple-element.46.refs_0_), channel_id=1, source_target_pairs={{0,3},{1,0},{2,1},{3,2},{4,5},{5,6},{6,7},{7,4},{8,11},{9,8},{10,9... | collective-permute-start | bytes 1572872 | tf_op jit(solution)/shard_map/ppermute | solution.py:29
  142.5 32.9 %collective-permute-start.7 = (bf16[64,4096]{1,0:T(8,128)(2,1)S(1)}, bf16[64,4096]{1,0:T(8,128)(2,1)S(1)}, u32[]{:S(2)}, u32[]{:S(2)}) collective-permute-start(bf16[64,4096]{1,0:T(8,128)(2,1)S(1)} %get-tuple-element.46.refs_0_), channel_id=1, source_target_pairs={{0,1},{1,2},{2,3},{3,0},{4,7},{5,4},{6,5},{7,6},{8,9},{9,10},{10,1... | collective-permute-start | bytes 1572872 | tf_op jit(solution)/shard_map/ppermute | solution.py:29
  174.5 0.8 copy-start.5
  175.3 0.8 copy-start.7
  176.1 1.0 copy-start.6
  177.2 1.0 copy-start.8
  188.5 14.1 %collective-permute-start.10 = (bf16[64,4096]{1,0:T(8,128)(2,1)S(1)}, bf16[64,4096]{1,0:T(8,128)(2,1)S(1)}, u32[]{:S(2)}, u32[]{:S(2)}) collective-permute-start(bf16[64,4096]{1,0:T(8,128)(2,1)S(1)} %get-tuple-element.51), channel_id=1, source_target_pairs={{0,1},{1,2},{2,3},{3,0},{4,7},{5,4},{6,5},{7,6},{8,9},{9,10},{10,1... | collective-permute-start | bytes 1572872 | tf_op jit(solution)/shard_map/ppermute | solution.py:29
  190.0 20.6 %collective-permute-start.12 = (bf16[64,4096]{1,0:T(8,128)(2,1)}, bf16[64,4096]{1,0:T(8,128)(2,1)S(1)}, u32[]{:S(2)}, u32[]{:S(2)}) collective-permute-start(bf16[64,4096]{1,0:T(8,128)(2,1)} %get-tuple-element.52), channel_id=1, source_target_pairs={{0,3},{1,0},{2,1},{3,2},{4,5},{5,6},{6,7},{7,4},{8,11},{9,8},{10,9... | collective-permute-start | bytes 1572872 | tf_op jit(solution)/shard_map/ppermute | solution.py:29
  202.7 10.8 %collective-permute-start.11 = (bf16[64,4096]{1,0:T(8,128)(2,1)S(1)}, bf16[64,4096]{1,0:T(8,128)(2,1)S(1)}, u32[]{:S(2)}, u32[]{:S(2)}) collective-permute-start(bf16[64,4096]{1,0:T(8,128)(2,1)S(1)} %add_convert_fusion), channel_id=1, source_target_pairs={{0,1},{1,2},{2,3},{3,0},{4,7},{5,4},{6,5},{7,6},{8,9},{9,10},{10,1... | collective-permute-start | bytes 1572872 | tf_op jit(solution)/shard_map/ppermute | solution.py:29
  204.7 8.9 %copy-start.4 = (bf16[64,4096]{1,0:T(8,128)(2,1)S(1)}, bf16[64,4096]{1,0:T(8,128)(2,1)}, u32[]{:S(2)}) copy-start(bf16[64,4096]{1,0:T(8,128)(2,1)} %get-tuple-element.45.x_ref) | copy-start | bytes 1572868
  222.5 5.1 %collective-permute-start.13 = (f32[64,6]{0,1:T(8,128)S(1)}, f32[64,6]{0,1:T(8,128)S(1)}, u32[]{:S(2)}, u32[]{:S(2)}) collective-permute-start(f32[64,6]{0,1:T(8,128)S(1)} %broadcast_select_fusion.2), channel_id=1, source_target_pairs={{0,2},{1,3},{2,0},{3,1},{4,6},{5,7},{6,4},{7,5},{8,10},{9,11},{10,... | collective-permute-start | bytes 4616 | tf_op jit(solution)/shard_map/ppermute | solution.py:21
Sparse Core Ops, SparseCore 0:
  25.0 75.1 all-gather.3
  102.4 71.9 all-gather.5
